TPU v7x, 256 devices: a whole 4x4x8 slice. The times are simulated.
256 devices in a mesh: dp: 2 (over core), row: 32 (over x, z), dim: 4 (over y).
Axes of the slice: x: 4, y: 4, z: 8, core: 2. Of those that a mesh axis runs over, the one named last changes fastest.
Arguments:
- tokens: bfloat16 [8192, 2048], P(('dp', 'row'), 'dim'), may hold values from -6 to 6
- query_weight: bfloat16 [2048, 512], P('dim'), may hold values from -0.125 to 0.125
- keys_first: bfloat16 [64, 256], replicated, may hold values from -0.375 to 0.375
- keys_second: bfloat16 [1024, 256], replicated, may hold values from -0.375 to 0.375
- values: bfloat16 [65536, 1024], P('row', 'dim'), may hold values from -6 to 6
- picks: int32 [8192, 32], P(('dp', 'row')), may hold values from 0 to 65535, as said below
- out_grad: bfloat16 [8192, 1024], P(('dp', 'row'), 'dim'), may hold values from -6 to 6
Outputs:
- mixed: bfloat16 [8192, 1024], P(('dp', 'row'), 'dim')
- token_grad: bfloat16 [8192, 2048], P(('dp', 'row'), 'dim')
- query_weight_grad: float32 [2048, 512], P('dim')
- first_key_grad: float32 [64, 256], replicated
- second_key_grad: float32 [1024, 256], replicated
- value_grad: float32 [65536, 1024], P(('row', 'dp'), 'dim')
Inputs may be any that keep to these rules, and one draw needn't show every extreme that they name: Call rows k * 2048 to (k + 1) * 2048 - 1 owner k's rows. Of the picks of one device's 128 tokens (aligned blocks of 128 token rows), at most 256 fall on one owner's rows; one owner, the same for every block, receives exactly 256 picks from every block.
All inputs are finite; a program needn't handle non-finite values.
Results may differ from a plain program's by a relative error of at most 0.0065.
Values may be sent and summed in bfloat16 or wider, within the bound.
No kernel may reach another device: no remote copies, remote signals or barrier semaphores. Data moves between devices by JAX's collectives and lax.ppermute only.
A program may use at most 64 MiB of HBM per device.

v0:
```python
import jax
import jax.numpy as jnp
from jax import lax
from jax.sharding import PartitionSpec as P


def body(tokens, query_weight, keys_first, keys_second, values, picks, out_grad):
    tok_count, topk = picks.shape
    row_dev, value_cols = values.shape
    half = keys_first.shape[1]
    first_count = keys_first.shape[0]
    second_count = keys_second.shape[0]
    n_row = lax.axis_size("row")
    capacity = 2 * tok_count * topk // n_row
    total = tok_count * topk
    partial_query = jnp.dot(tokens, query_weight, preferred_element_type=jnp.float32)
    query = lax.psum(partial_query, "dim").astype(jnp.bfloat16)
    query_a = query[:, :half]
    query_b = query[:, half:]
    first_scores = jnp.dot(query_a, keys_first.T, preferred_element_type=jnp.float32)
    second_scores = jnp.dot(query_b, keys_second.T, preferred_element_type=jnp.float32)
    first_index = picks // second_count
    second_index = picks % second_count
    score = jnp.take_along_axis(first_scores, first_index, 1) + jnp.take_along_axis(
        second_scores, second_index, 1
    )
    expo = jnp.exp(score)
    weight = expo / jnp.sum(expo, axis=1, keepdims=True)
    weight_b = weight.astype(jnp.bfloat16)
    owner = (picks // row_dev).reshape(-1)
    local_row = (picks % row_dev).reshape(-1)
    owner_onehot = (owner[:, None] == jnp.arange(n_row, dtype=jnp.int32)[None, :]).astype(jnp.int32)
    earlier = jnp.cumsum(owner_onehot, axis=0) - owner_onehot
    rank = jnp.sum(earlier * owner_onehot, axis=1)
    slot = owner * capacity + rank
    request_rows = (
        jnp.zeros((n_row * capacity,), jnp.int32).at[slot].set(local_row).reshape(n_row, capacity)
    )
    recv_rows = lax.all_to_all(request_rows, "row", split_axis=0, concat_axis=0, tiled=True)
    flat_rows = recv_rows.reshape(-1)
    own_rows = jnp.take(values, flat_rows, axis=0).reshape(n_row, capacity, value_cols)
    returned = lax.all_to_all(own_rows, "row", split_axis=0, concat_axis=0, tiled=True)
    picked = jnp.take(returned.reshape(n_row * capacity, value_cols), slot, axis=0).reshape(
        tok_count, topk, value_cols
    )
    mixed = jnp.einsum("tk,tkv->tv", weight_b, picked, preferred_element_type=jnp.float32).astype(
        jnp.bfloat16
    )
    partial_pick = jnp.einsum("tv,tkv->tk", out_grad, picked, preferred_element_type=jnp.float32)
    pick_grad = lax.psum(partial_pick, "dim")
    score_grad = weight * (pick_grad - jnp.sum(weight * pick_grad, axis=1, keepdims=True))
    row_ids = jnp.broadcast_to(jnp.arange(tok_count, dtype=jnp.int32)[:, None], (tok_count, topk))
    grad_a = (
        jnp.zeros((tok_count, first_count), jnp.float32)
        .at[row_ids, first_index]
        .add(score_grad)
        .astype(jnp.bfloat16)
    )
    grad_b = (
        jnp.zeros((tok_count, second_count), jnp.float32)
        .at[row_ids, second_index]
        .add(score_grad)
        .astype(jnp.bfloat16)
    )
    query_grad = jnp.concatenate(
        [
            jnp.dot(grad_a, keys_first, preferred_element_type=jnp.float32),
            jnp.dot(grad_b, keys_second, preferred_element_type=jnp.float32),
        ],
        axis=1,
    ).astype(jnp.bfloat16)
    token_grad = jnp.dot(query_grad, query_weight.T, preferred_element_type=jnp.float32).astype(
        jnp.bfloat16
    )
    weight_part = jnp.dot(tokens.T, query_grad, preferred_element_type=jnp.float32)
    first_part = jnp.dot(grad_a.T, query_a, preferred_element_type=jnp.float32)
    second_part = jnp.dot(grad_b.T, query_b, preferred_element_type=jnp.float32)
    weight_sum, first_sum, second_sum = lax.psum(
        (weight_part, first_part, second_part), ("dp", "row")
    )
    token_of = jnp.arange(total, dtype=jnp.int32) // topk
    send_grad = (
        jnp.zeros((n_row * capacity, value_cols), jnp.bfloat16)
        .at[slot]
        .set(jnp.take(out_grad, token_of, axis=0))
        .reshape(n_row, capacity, value_cols)
    )
    send_weight = (
        jnp.zeros((n_row * capacity,), jnp.bfloat16)
        .at[slot]
        .set(weight_b.reshape(-1))
        .reshape(n_row, capacity)
    )
    recv_grad, recv_weight = (
        lax.all_to_all(send_grad, "row", split_axis=0, concat_axis=0, tiled=True),
        lax.all_to_all(send_weight, "row", split_axis=0, concat_axis=0, tiled=True),
    )
    contrib = recv_weight.reshape(-1, 1).astype(jnp.float32) * recv_grad.reshape(
        -1, value_cols
    ).astype(jnp.float32)
    value_part = jnp.zeros((row_dev, value_cols), jnp.float32).at[flat_rows].add(contrib)
    value_grad = lax.psum_scatter(value_part, "dp", scatter_dimension=0, tiled=True)
    return (mixed, token_grad, weight_sum, first_sum, second_sum, value_grad)


def solution(mesh):
    return jax.shard_map(
        body,
        mesh=mesh,
        in_specs=(
            P(("dp", "row"), "dim"),
            P("dim", None),
            P(),
            P(),
            P("row", "dim"),
            P(("dp", "row"), None),
            P(("dp", "row"), "dim"),
        ),
        out_specs=(
            P(("dp", "row"), "dim"),
            P(("dp", "row"), "dim"),
            P("dim", None),
            P(),
            P(),
            P(("row", "dp"), "dim"),
        ),
        check_vma=False,
    )
```

profile of v0, /device:TPU:8, one launch (start us, length us, event | category | flops | bytes accessed | tf_op | source)
XLA Modules:
  0.0 643.9 jit_solution(13563676538009704904)
XLA Ops:
  8.0 0.8 broadcast_multiply_fusion
  9.4 9.2 %reduce-window.6 = s32[32,32,128]{2,1,0:T(8,128)S(1)} reduce-window(s32[32,32,128]{2,1,0:T(8,128)S(1)} %fusion.15, s32[]{:T(128)} %constant.136.clone.1), window={size=1x1x128 pad=0_0x0_0x127_0}, to_apply=%region_2.3 | reduce-window | flops 16646144 | bytes 1048580 | tf_op jit(solution)/shard_map/reduce-window
  18.6 0.8 slice_reduce_fusion
  19.4 0.2 reduce-window.9
  19.6 0.2 broadcast_add_fusion
  20.0 0.4 fusion.14
  20.4 15.5 %scatter_custom_fusion = s32[8192]{0:T(1024)S(1)} fusion(s32[4096]{0:T(1024)S(1)} %bitcast.85, s32[4096]{0:T(1024)S(1)} %reshape.310, s32[]{:T(128)} %constant.136.clone.1), kind=kCustom, calls=%fused_computation.98 | custom fusion | bytes 32772 | tf_op jit(solution)/shard_map/scatter | solution.py:37
  36.0 21.0 %all_to_all.29 = s32[32,1,256]{2,1,0:T(1,128)S(1)} all-to-all(s32[32,1,256]{2,1,0:T(1,128)S(1)} %bitcast.79), channel_id=1, replica_groups=mesh['dp'=2,'row'=32,'dim'=4] {'row'}, dimensions={0} | all-to-all | bytes 65536 | tf_op jit(solution)/shard_map/all_to_all | solution.py:39
  57.1 32.9 %gather_fusion = bf16[8192,256]{1,0:T(8,128)(2,1)} fusion(bf16[2048,256]{1,0:T(8,128)(2,1)S(1)} %copy-done, s32[8192]{0:T(1024)S(1)} %broadcast_clamp_fusion), kind=kCustom, calls=%fused_computation | custom fusion | bytes 8421376 | tf_op jit(solution)/shard_map/jit(_take)/gather | solution.py:41
  90.0 5.2 broadcast_select_fusion
  95.2 5.0 all-to-all-start.1
  100.3 0.2 fusion.54
  100.6 0.1 copy.36
  101.2 95.0 %all-to-all-done.1 = bf16[32,256,256]{2,1,0:T(8,128)(2,1)} async-done(((bf16[32,256,256]{2,1,0:T(8,128)(2,1)}), bf16[32,256,256]{2,1,0:T(8,128)(2,1)}, u32[]{:S(2)}, u32[]{:S(2)}) %all-to-all-start.1) | async-done | bytes 4194336 | tf_op jit(solution)/shard_map/all_to_all | solution.py:42
  196.2 18.6 %gather_fusion.1 = bf16[4096,256]{1,0:T(8,128)(2,1)} fusion(bf16[8192,256]{1,0:T(8,128)(2,1)} %bitcast.10, s32[4096]{0:T(1024)S(1)} %broadcast_clamp_fusion.2), kind=kCustom, calls=%fused_computation.1 | custom fusion | bytes 4210688 | tf_op jit(solution)/shard_map/jit(_take)/gather | solution.py:43
  214.8 2.4 fusion.6
  217.2 17.5 %all-reduce.6 = (bf16[128,512]{1,0:T(8,128)(2,1)S(1)}, f32[128,32]{0,1:T(8,128)S(1)}) all-reduce(f32[128,512]{1,0:T(8,128)S(1)} %fusion.54, f32[128,32]{0,1:T(8,128)S(1)} %bitcast.84), channel_id=1, replica_groups=mesh['dp'=2,'row'=32,'dim'=4] {'dim'}, use_global_device_ids=true, to_apply=%region_0.0 | all-reduce | flops 69632 | bytes 425984 | tf_op jit(solution)/shard_map/psum | solution.py:17
  234.7 0.3 fusion.21
  235.0 32.8 %gather_fusion.3 = f32[4096]{0:T(1024)S(1)} fusion(f32[128,1024]{1,0:T(8,128)S(1)} %fusion.21, s32[4096]{0:T(1024)S(1)} %reshape.300), kind=kCustom, calls=%fused_computation.4 | custom fusion | bytes 65536 | tf_op jit(solution)/shard_map/jit(take_along_axis)/gather | solution.py:24
  268.0 0.1 fusion.25
  268.1 26.6 %gather_fusion.2 = f32[4096]{0:T(1024)S(1)} fusion(f32[128,64]{0,1:T(8,128)S(1)} %fusion.25, s32[4096]{0:T(1024)S(1)} %reshape.294), kind=kCustom, calls=%fused_computation.3 | custom fusion | bytes 65536 | tf_op jit(solution)/shard_map/jit(take_along_axis)/gather | solution.py:24
  294.9 0.1 copy.42
  295.1 28.6 %scatter_custom_fusion.1 = bf16[8192]{0:T(1024)(128)(2,1)S(1)} fusion(s32[4096]{0:T(1024)S(1)} %bitcast.87, bf16[4096]{0:T(1024)(128)(2,1)S(1)} %reshape.318, bf16[]{:T(256)} %constant.152.clone.1), kind=kCustom, calls=%fused_computation.111 | custom fusion | bytes 16386 | tf_op jit(solution)/shard_map/scatter | solution.py:91
  323.7 0.5 broadcast.339
  324.3 0.7 reduce.10
  325.0 0.6 reshape.375
  325.6 5.5 all-to-all-start.2
  331.2 35.5 %scatter_custom_fusion.2 = bf16[8192,256]{1,0:T(8,128)(2,1)} fusion(s32[4096]{0:T(1024)S(1)} %bitcast.88, bf16[]{:T(256)} %constant.152.clone.1, pred[4096]{0:T(1024)(128)(4,1)S(1)} %fusion.37, bf16[]{:T(256)} %constant.151.clone.1, bf16[128,256]{1,0:T(8,128)(2,1)S(1)} %copy-done.7, s32[4096]{0:T(1024)S(1)} %broadcast_clamp_fusion.1), kind=kCustom, calls=%fused_computation.15 | custom fusion | flops 1048576 | bytes 4280324 | tf_op jit(solution)/shard_map/scatter | solution.py:85
  366.7 10.1 %all-to-all-start.3 = ((bf16[32,256,256]{2,1,0:T(8,128)(2,1)}), bf16[32,256,256]{2,1,0:T(8,128)(2,1)}, u32[]{:S(2)}, u32[]{:S(2)}) async-start(bf16[32,256,256]{2,1,0:T(8,128)(2,1)} %bitcast.69), calls=%async_computation.3 | async-start | bytes 8388608 | tf_op jit(solution)/shard_map/all_to_all | solution.py:95
  377.4 0.1 copy.40
  377.6 28.4 %scatter_custom_fusion.5 = f32[131072]{0:T(1024)S(1)} fusion(s32[4096]{0:T(1024)S(1)} %reshape.344, f32[4096]{0:T(1024)S(1)} %reshape.340, f32[]{:T(128)} %constant.144.clone.1), kind=kCustom, calls=%fused_computation.38 | custom fusion | flops 4096 | bytes 524292
  406.1 0.1 reshape.266
  406.2 21.9 %scatter_custom_fusion.4 = f32[8192]{0:T(1024)S(1)} fusion(s32[4096]{0:T(1024)S(1)} %reshape.338, f32[4096]{0:T(1024)S(1)} %reshape.340, f32[]{:T(128)} %constant.144.clone.1), kind=kCustom, calls=%fused_computation.94 | custom fusion | flops 4096 | bytes 32772
  428.1 0.2 convolution_convert_fusion.2
  428.3 0.8 fusion.23
  429.1 0.2 convolution_convert_fusion.1
  429.3 1.3 convolution_bitcast_fusion
  430.6 1.3 fusion.19
  432.1 37.1 %all-to-all-done.3 = bf16[32,256,256]{2,1,0:T(8,128)(2,1)} async-done(((bf16[32,256,256]{2,1,0:T(8,128)(2,1)}), bf16[32,256,256]{2,1,0:T(8,128)(2,1)}, u32[]{:S(2)}, u32[]{:S(2)}) %all-to-all-start.3) | async-done | bytes 4194336 | tf_op jit(solution)/shard_map/all_to_all | solution.py:95
  469.1 56.2 %scatter_custom_fusion.3 = f32[2048,256]{1,0:T(8,128)} fusion(s32[8192]{0:T(1024)S(1)} %bitcast.78, bf16[8192,256]{1,0:T(8,128)(2,1)} %bitcast.21, f32[8192]{0:T(1024)S(1)} %bitcast.76, f32[]{:T(128)} %constant.144.clone.1), kind=kCustom, calls=%fused_computation.12 | custom fusion | flops 6291456 | bytes 6324228 | tf_op jit(solution)/shard_map/scatter-add | solution.py:101
  525.4 0.1 copy.45
  525.5 2.3 fusion.7
  527.8 0.6 copy.58
  528.5 1.0 convolution_convert_fusion
  529.4 102.8 %all-reduce.5.cloned.1.call-done = (f32[512,512]{0,1:T(8,128)}, f32[64,256]{1,0:T(8,128)}, f32[1024,256]{1,0:T(8,128)}) async-done(((f32[512,512]{0,1:T(8,128)}, f32[64,256]{1,0:T(8,128)}, f32[1024,256]{1,0:T(8,128)}), (f32[512,512]{0,1:T(8,128)}, f32[64,256]{1,0:T(8,128)}, f32[1024,256]{1,0:T(8,128)})) %all-reduce.5.cloned.1.call-update) | async-done | bytes 2162704 | tf_op jit(solution)/shard_map/psum | solution.py:78
  632.3 2.6 copy.44
  634.9 0.6 copy.65
  635.5 1.0 copy.66
  (78 shorter events, 2.8 us)
Async XLA Ops:
  8.0 49.0 %copy-start = (bf16[2048,256]{1,0:T(8,128)(2,1)S(1)}, bf16[2048,256]{1,0:T(8,128)(2,1)}, u32[]{:S(2)}) copy-start(bf16[2048,256]{1,0:T(8,128)(2,1)} %param.11) | copy-start | bytes 3145732
  95.2 5.1 copy-start.1
  95.2 5.1 copy-start.4
  95.2 5.5 copy-start.5
  95.2 101.0 %all-to-all-start.1 = ((bf16[32,256,256]{2,1,0:T(8,128)(2,1)}), bf16[32,256,256]{2,1,0:T(8,128)(2,1)}, u32[]{:S(2)}, u32[]{:S(2)}) async-start(bf16[32,256,256]{2,1,0:T(8,128)(2,1)} %broadcast_select_fusion), calls=%async_computation.1 | async-start | bytes 8388608 | tf_op jit(solution)/shard_map/all_to_all | solution.py:42
  196.2 18.6 %copy-start.7 = (bf16[128,256]{1,0:T(8,128)(2,1)S(1)}, bf16[128,256]{1,0:T(8,128)(2,1)}, u32[]{:S(2)}) copy-start(bf16[128,256]{1,0:T(8,128)(2,1)} %param.13) | copy-start | bytes 196612
  214.8 19.9 %copy-start.2 = (bf16[1024,256]{1,0:T(8,128)(2,1)S(1)}, bf16[1024,256]{1,0:T(8,128)(2,1)}, u32[]{:S(2)}) copy-start(bf16[1024,256]{1,0:T(8,128)(2,1)} %param.10) | copy-start | bytes 1572868
  235.0 32.9 %copy-start.6 = (bf16[64,256]{1,0:T(8,128)(2,1)S(1)}, bf16[64,256]{1,0:T(8,128)(2,1)}, u32[]{:S(2)}) copy-start(bf16[64,256]{1,0:T(8,128)(2,1)} %param.9) | copy-start | bytes 98308
  325.6 41.1 %all-to-all-start.2 = ((bf16[32,2,128]{2,1,0:T(2,128)(2,1)}), bf16[32,2,128]{2,1,0:T(2,128)(2,1)S(1)}, u32[]{:S(2)}, u32[]{:S(2)}) async-start(bf16[32,2,128]{2,1,0:T(2,128)(2,1)} %reshape.375), calls=%async_computation.2 | async-start | bytes 32768 | tf_op jit(solution)/shard_map/all_to_all | solution.py:96
  366.7 10.2 %copy-start.11 = (s32[2]{0:T(128)S(1)}, s32[2]{0:T(128)}, u32[]{:S(2)}) copy-start(s32[2]{0:T(128)} %constant.157) | copy-start | bytes 28
  366.7 10.2 %copy-start.12 = (s32[2]{0:T(128)S(1)}, s32[2]{0:T(128)}, u32[]{:S(2)}) copy-start(s32[2]{0:T(128)} %constant.163) | copy-start | bytes 28
  366.7 10.2 %copy-start.9 = (s32[2]{0:T(128)S(1)}, s32[2]{0:T(128)}, u32[]{:S(2)}) copy-start(s32[2]{0:T(128)} %constant.160) | copy-start | bytes 28
  366.7 10.2 %copy-start.10 = (s32[2]{0:T(128)S(1)}, s32[2]{0:T(128)}, u32[]{:S(2)}) copy-start(s32[2]{0:T(128)} %constant.166) | copy-start | bytes 28
  366.7 102.4 %all-to-all-start.3 = ((bf16[32,256,256]{2,1,0:T(8,128)(2,1)}), bf16[32,256,256]{2,1,0:T(8,128)(2,1)}, u32[]{:S(2)}, u32[]{:S(2)}) async-start(bf16[32,256,256]{2,1,0:T(8,128)(2,1)} %bitcast.69), calls=%async_computation.3 | async-start | bytes 8388608 | tf_op jit(solution)/shard_map/all_to_all | solution.py:95
  376.8 255.5 %all-reduce.5.cloned.1.call-start = ((), (), s32[]{:S(2)}) async-start(), calls=%async_computation.6 | async-start | bytes 4325376 | tf_op jit(solution)/shard_map/psum | solution.py:78
  431.9 202.9 %reduce-scatter.2.cloned.1.call-start = ((), (), s32[]{:S(2)}) async-start(), calls=%async_computation.5 | async-start | bytes 3145728 | tf_op jit(solution)/shard_map/reduce_scatter | solution.py:102
  632.3 2.6 copy-start.8
  632.3 3.3 copy-start.3
Sparse Core Ops, SparseCore 0:
  432.1 200.1 all-reduce.4
Sparse Core Ops, SparseCore 1:
  525.5 13.0 reduce-scatter.1
where the time goes:
time: 644 us
  waiting for transfers between devices  235 us (36%)
  local copies, waits for them, and re-layouts  164 us (25%)
  other arithmetic  159 us (25%)
  blocking collectives  38.5 us (6%)
  starting transfers between devices  20.7 us (3%)
  between operations  15.9 us (2%)
  matrix products  10.1 us (2%)
    psum x1, waiting for transfers between devices, body(): lax.psum((weight_part, first_part, second_part), ('dp', 'row'))  103 us
    all_to_all x1, waiting for transfers between devices, body(): lax.all_to_all(own_rows, 'row', split_axis=0, concat_axis=0, tiled=True)  95 us
    scatter-add x1, other arithmetic, body(): jnp.zeros((row_dev, value_cols), jnp.float32).at[flat_rows].add(contrib)  56.2 us
    unnamed x5, other arithmetic  50.5 us
    all_to_all x1, waiting for transfers between devices, body(): lax.all_to_all(send_grad, 'row', split_axis=0, concat_axis=0, tiled=True)  37.1 us
    scatter x1, other arithmetic, body(): send_grad = jnp.zeros((n_row * capacity, value_cols), jnp.bfloat16).at[sl...  35.5 us
    gather x5, local copies, waits for them, and re-layouts, body(): jnp.take_along_axis(second_scores, second_index, 1)  33.1 us
    gather x1, local copies, waits for them, and re-layouts, body(): jnp.take(values, flat_rows, axis=0).reshape(n_row, capacity, value_cols)  32.9 us
  transfers between devices with their start and end apart: 5, of which 3 were waited for; matrix products, arithmetic and copies ran while one was open for 24% of the time, Pallas kernels for 0%

commit v1 on v0

v1 whole, which is shorter than its diff:
```python
import functools

import jax
import jax.numpy as jnp
from jax import lax
from jax.experimental import pallas as pl
from jax.experimental.pallas import tpu as pltpu
from jax.sharding import PartitionSpec as P

BF = jnp.bfloat16
F32 = jnp.float32
I32 = jnp.int32
NT = (((1,), (1,)), ((), ()))
TN = (((0,), (0,)), ((), ()))
MIB = 1 << 20


def dot(x, y, dims=(((1,), (0,)), ((), ()))):
    return lax.dot_general(x, y, dims, preferred_element_type=F32)


def iota(shape, dim):
    return lax.broadcasted_iota(I32, shape, dim)


def whole(shape):
    return pl.BlockSpec(shape, lambda *_: (0,) * len(shape))


def route_kernel(
    row_dev, query_ref, first_ref, second_ref, picks_ref,
    lists_ref, rank_ref, weight_ref, score_b, score, lhs, slots,
):
    topk, tok = picks_ref.shape
    half = first_ref.shape[1]
    na, nb = first_ref.shape[0], second_ref.shape[0]
    n_row = lists_ref.shape[0]
    cap = slots.shape[0]
    query = query_ref[...]
    score_a = dot(first_ref[...], query[:, :half], NT)
    score_b[...] = dot(second_ref[...], query[:, half:], NT)

    def look_up(k, carry):
        pick = picks_ref[pl.ds(k, 1), :]
        in_a = iota((na, tok), 0) == pick // nb
        in_b = iota((nb, tok), 0) == pick % nb
        part_a = jnp.sum(jnp.where(in_a, score_a, 0.0), axis=0, keepdims=True)
        part_b = jnp.sum(jnp.where(in_b, score_b[...], 0.0), axis=0, keepdims=True)
        score[pl.ds(k, 1), :] = part_a + part_b
        return carry

    lax.fori_loop(0, topk, look_up, 0)
    expo = jnp.exp(score[...])
    weight = expo / jnp.sum(expo, axis=0, keepdims=True)
    weight_ref[...] = weight

    picks = picks_ref[...]
    owner = picks // row_dev
    local = picks % row_dev
    at_owner = iota((n_row, tok), 0)
    onehots = [(at_owner == owner[k : k + 1, :]) for k in range(topk)]
    stacked = jnp.concatenate([jnp.where(hot, 1.0, 0.0) for hot in onehots], axis=0).astype(BF)
    upto = jnp.where(iota((tok, tok), 0) <= iota((tok, tok), 1), 1.0, 0.0).astype(BF)
    running = dot(stacked, upto)
    totals = dot(stacked, jnp.ones((tok, tok), BF))
    base = jnp.full((n_row, tok), -1.0, F32)
    token = iota((n_row, tok), 1).astype(F32)
    for k in range(topk):
        hot = onehots[k]
        part = slice(k * n_row, (k + 1) * n_row)
        rank = jnp.sum(jnp.where(hot, running[part] + base, 0.0), axis=0, keepdims=True).astype(I32)
        base = base + totals[part]
        rank_ref[k : k + 1, :] = rank
        lanes = slice(k * tok, (k + 1) * tok)
        slots[:, lanes] = jnp.where(iota((cap, tok), 0) == rank, 1.0, 0.0).astype(BF)
        high = (local[k : k + 1, :] // 256).astype(F32)
        low = (local[k : k + 1, :] % 256).astype(F32)
        sent = [weight[k : k + 1, :], high, low, token]
        lhs[:, lanes] = jnp.concatenate([jnp.where(hot, v, 0.0) for v in sent], axis=0).astype(BF)
    listed = dot(lhs[...], slots[...], NT)
    weights = listed[:n_row]
    rows = listed[n_row : 2 * n_row] * 256.0 + listed[2 * n_row : 3 * n_row]
    tokens = listed[3 * n_row :]
    for at, part in enumerate((weights, rows, tokens)):
        lists_ref[:, 2 * at, :] = part[:, :128]
        lists_ref[:, 2 * at + 1, :] = part[:, 128:]
    lists_ref[:, 6, :] = jnp.zeros((n_row, 128), F32)
    lists_ref[:, 7, :] = jnp.zeros((n_row, 128), F32)


def route(query, keys_first, keys_second, picks_t, row_dev, n_row, cap):
    topk, tok = picks_t.shape
    return pl.pallas_call(
        functools.partial(route_kernel, row_dev),
        out_shape=(
            jax.ShapeDtypeStruct((n_row, 8, 128), F32),
            jax.ShapeDtypeStruct((topk, tok), I32),
            jax.ShapeDtypeStruct((topk, tok), F32),
        ),
        scratch_shapes=[
            pltpu.VMEM((keys_second.shape[0], tok), F32),
            pltpu.VMEM((topk, tok), F32),
            pltpu.VMEM((4 * n_row, topk * tok), BF),
            pltpu.VMEM((cap, topk * tok), BF),
        ],
        compiler_params=pltpu.CompilerParams(vmem_limit_bytes=32 * MIB),
        name="route",
    )(query, keys_first, keys_second, picks_t)


def listed(lists, at):
    return jnp.concatenate([lists[2 * at : 2 * at + 1, :], lists[2 * at + 1 : 2 * at + 2, :]], axis=1)


def owner_kernel(order_ref, lists_ref, grad_ref, values_ref, mixed_ref, pick_ref, spread_ref):
    cap = pick_ref.shape[2]
    rows = values_ref.shape[1]
    tok = grad_ref.shape[0]
    lists = lists_ref[0]
    weight = listed(lists, 0)
    row = listed(lists, 1).astype(I32)
    token = listed(lists, 2).astype(I32)
    hot = jnp.where(iota((rows, cap), 0) == row, 1.0, 0.0).astype(BF)
    picked = dot(values_ref[...], hot)
    at_token = iota((tok, cap), 0) == token
    spread = dot(grad_ref[...], jnp.where(at_token, 1.0, 0.0).astype(BF), TN)
    pick_ref[0] = jnp.sum(picked * spread, axis=0, keepdims=True)
    spread_ref[...] = spread.astype(BF)
    mixed_ref[...] = dot(
        jnp.where(at_token, weight, 0.0).astype(BF), picked.astype(BF), NT
    ).astype(BF)


def owner_side(order, lists, grads, values_t, cap):
    blocks = lists.shape[0]
    tok = grads.shape[0] // blocks
    cols, rows = values_t.shape
    return pl.pallas_call(
        owner_kernel,
        grid_spec=pltpu.PrefetchScalarGridSpec(
            num_scalar_prefetch=1,
            grid=(blocks,),
            in_specs=[
                pl.BlockSpec((1, 8, 128), lambda b, order: (order[b], 0, 0)),
                pl.BlockSpec((tok, cols), lambda b, order: (b, 0)),
                whole((cols, rows)),
            ],
            out_specs=[
                pl.BlockSpec((tok, cols), lambda b, order: (order[b], 0)),
                pl.BlockSpec((1, 1, cap), lambda b, order: (order[b], 0, 0)),
                pl.BlockSpec((cols, cap), lambda b, order: (0, order[b])),
            ],
        ),
        out_shape=(
            jax.ShapeDtypeStruct((blocks * tok, cols), BF),
            jax.ShapeDtypeStruct((blocks, 1, cap), F32),
            jax.ShapeDtypeStruct((cols, blocks * cap), BF),
        ),
        compiler_params=pltpu.CompilerParams(vmem_limit_bytes=32 * MIB),
        name="owner_side",
    )(order, lists, grads, values_t)


def scatter_kernel(lists_ref, spread_ref, out_ref):
    blocks = lists_ref.shape[0]
    tile = out_ref.shape[0]
    cap = spread_ref.shape[1] // blocks
    at_row = iota((tile, cap), 0) + pl.program_id(0) * tile
    total = jnp.zeros(out_ref.shape, F32)
    for b in range(blocks):
        lists = lists_ref[b]
        hot = jnp.where(at_row == listed(lists, 1).astype(I32), listed(lists, 0), 0.0).astype(BF)
        total = total + dot(hot, spread_ref[:, b * cap : (b + 1) * cap], NT)
    out_ref[...] = total


def scatter(lists, spread, rows, tile):
    cols, total = spread.shape
    return pl.pallas_call(
        scatter_kernel,
        grid=(rows // tile,),
        in_specs=[whole(lists.shape), whole(spread.shape)],
        out_specs=pl.BlockSpec((tile, cols), lambda r: (r, 0)),
        out_shape=jax.ShapeDtypeStruct((rows, cols), F32),
        compiler_params=pltpu.CompilerParams(vmem_limit_bytes=32 * MIB),
        name="scatter",
    )(lists, spread)


def grads_kernel(
    row_dev, parts_ref, rank_ref, picks_ref, weight_ref, query_ref, first_ref, second_ref,
    qw_ref, tokens_ref, token_grad_ref, qw_part_ref, first_part_ref, second_part_ref,
    slots, sums, grad_b,
):
    topk, tok = picks_ref.shape
    half = first_ref.shape[1]
    na, nb = first_ref.shape[0], second_ref.shape[0]
    cap = parts_ref.shape[2]
    n_row = parts_ref.shape[0]
    parts = parts_ref[...]
    by_slot = parts[:, 0, :]
    for m in range(1, parts_ref.shape[1]):
        by_slot = by_slot + parts[:, m, :]
    one = by_slot.astype(BF)
    rest = by_slot - one.astype(F32)
    two = rest.astype(BF)
    three = (rest - two.astype(F32)).astype(BF)
    for k in range(topk):
        slots[:, k * tok : (k + 1) * tok] = jnp.where(
            iota((cap, tok), 0) == rank_ref[k : k + 1, :], 1.0, 0.0
        ).astype(BF)
    sums[...] = dot(jnp.concatenate([one, two, three], axis=0), slots[...])
    picks = picks_ref[...]
    owner = picks // row_dev
    at_owner = iota((n_row, tok), 0)
    rows = []
    for k in range(topk):
        got = sums[:, k * tok : (k + 1) * tok]
        got = got[:n_row] + got[n_row : 2 * n_row] + got[2 * n_row :]
        rows.append(jnp.sum(jnp.where(at_owner == owner[k : k + 1, :], got, 0.0), axis=0, keepdims=True))
    pick_grad = jnp.concatenate(rows, axis=0)
    weight = weight_ref[...]
    score_grad = weight * (pick_grad - jnp.sum(weight * pick_grad, axis=0, keepdims=True))
    first_index = picks // nb
    second_index = picks % nb
    grad_a = jnp.zeros((na, tok), F32)
    for k in range(topk):
        grad_a = grad_a + jnp.where(
            iota((na, tok), 0) == first_index[k : k + 1, :], score_grad[k : k + 1, :], 0.0
        )
    grad_a = grad_a.astype(BF)
    tile = 128

    def one_tile(i, carry):
        at_b = iota((tile, tok), 0) + i * tile
        total = jnp.zeros((tile, tok), F32)
        for k in range(topk):
            total = total + jnp.where(
                at_b == second_index[k : k + 1, :], score_grad[k : k + 1, :], 0.0
            )
        grad_b[pl.ds(pl.multiple_of(i * tile, tile), tile), :] = total.astype(BF)
        return carry

    lax.fori_loop(0, nb // tile, one_tile, 0)
    query = query_ref[...]
    query_grad = jnp.concatenate(
        [dot(grad_a, first_ref[...], TN), dot(grad_b[...], second_ref[...], TN)], axis=1
    ).astype(BF)
    token_grad_ref[...] = dot(query_grad, qw_ref[...], NT).astype(BF)
    qw_part_ref[...] = dot(tokens_ref[...], query_grad, TN).astype(BF)
    first_part_ref[...] = dot(grad_a, query[:, :half]).astype(BF)
    second_part_ref[...] = dot(grad_b[...], query[:, half:]).astype(BF)


def grads(parts, rank, picks_t, weight, query, keys_first, keys_second, qw, tokens, row_dev):
    topk, tok = picks_t.shape
    cap = parts.shape[2]
    return pl.pallas_call(
        functools.partial(grads_kernel, row_dev),
        out_shape=(
            jax.ShapeDtypeStruct(tokens.shape, BF),
            jax.ShapeDtypeStruct(qw.shape, BF),
            jax.ShapeDtypeStruct(keys_first.shape, BF),
            jax.ShapeDtypeStruct(keys_second.shape, BF),
        ),
        scratch_shapes=[
            pltpu.VMEM((cap, topk * tok), BF),
            pltpu.VMEM((3 * parts.shape[0], topk * tok), F32),
            pltpu.VMEM((keys_second.shape[0], tok), BF),
        ],
        compiler_params=pltpu.CompilerParams(vmem_limit_bytes=32 * MIB),
        name="grads",
    )(parts, rank, picks_t, weight, query, keys_first, keys_second, qw, tokens)


def gather_blocks(block, n_x, n_z):
    def shift(sx, sz):
        return [
            (x * n_z + z, (x + sx) % n_x * n_z + (z + sz) % n_z)
            for x in range(n_x)
            for z in range(n_z)
        ]

    column = jnp.stack([block] + [lax.ppermute(block, "row", shift(s, 0)) for s in range(1, n_x)])
    held = {0: column}
    up = down = column
    for step in range(1, n_z // 2 + 1):
        up = lax.ppermute(up, "row", shift(0, 1))
        held[-step % n_z] = up
        if step < n_z // 2:
            down = lax.ppermute(down, "row", shift(0, -1))
            held[step] = down
    return held


def body(tokens, query_weight, keys_first, keys_second, values, picks, out_grad):
    tok, topk = picks.shape
    row_dev, cols = values.shape
    n_row, n_dim = lax.axis_size("row"), lax.axis_size("dim")
    cap = 2 * tok * topk // n_row
    n_x, n_z = 4, n_row // 4
    row_at = lax.axis_index("row")

    held = gather_blocks(out_grad, n_x, n_z)
    by_shift = jnp.stack([held[d] for d in range(n_z)])

    partial = dot(tokens, query_weight)
    pieces = lax.all_to_all(partial, "dim", 0, 0, tiled=True)
    quarter = jnp.sum(pieces.reshape(n_dim, tok // n_dim, -1), axis=0).astype(BF)
    query = lax.all_gather(quarter, "dim", tiled=True)
    picks_t = picks.T
    lists, rank, weight = route(query, keys_first, keys_second, picks_t, row_dev, n_row, cap)
    own_lists = lax.all_to_all(lists, "row", 0, 0, tiled=True)

    x_at, z_at = row_at // n_z, row_at % n_z
    order_d = jnp.arange(n_row, dtype=I32) // n_x
    order_s = jnp.arange(n_row, dtype=I32) % n_x
    order = (x_at - order_s) % n_x * n_z + (z_at + order_d) % n_z
    mixed_part, pick_part, spread = owner_side(
        order, own_lists, by_shift.reshape(n_row * tok, cols), values.T, cap
    )
    pick_sent = jnp.broadcast_to(pick_part, (n_row, n_dim, cap)).reshape(n_row * n_dim, cap)
    pick_parts = lax.all_to_all(pick_sent, ("row", "dim"), 0, 0, tiled=True).reshape(n_row, n_dim, cap)

    mixed_got = lax.all_to_all(mixed_part.reshape(n_row, tok, cols), "row", 0, 0, tiled=True)

    token_grad, qw_part, first_part, second_part = grads(
        pick_parts, rank, picks_t, weight, query, keys_first, keys_second, query_weight, tokens, row_dev
    )
    sums = jnp.concatenate([qw_part.reshape(-1, keys_first.shape[1]), first_part, second_part], axis=0)
    share = sums.shape[0] // n_row
    sums_got = lax.all_to_all(sums.reshape(n_row, share, -1), "row", 0, 0, tiled=True)
    summed = jnp.sum(sums_got.astype(F32), axis=0)
    summed = summed + lax.ppermute(summed, "dp", [(0, 1), (1, 0)])
    summed = jnp.broadcast_to(summed.astype(BF)[None], (n_row,) + summed.shape)
    sums_all = lax.all_to_all(summed, "row", 0, 0, tiled=True).reshape(sums.shape).astype(F32)
    n_qw = qw_part.size // keys_first.shape[1]
    qw_grad = sums_all[:n_qw].reshape(qw_part.shape)
    first_grad = sums_all[n_qw : n_qw + keys_first.shape[0]]
    second_grad = sums_all[n_qw + keys_first.shape[0] :]

    value_part = scatter(own_lists, spread, row_dev, 256)
    dp_at = lax.axis_index("dp")
    own = row_dev // 2
    theirs = lax.dynamic_slice_in_dim(value_part, (1 - dp_at) * own, own, 0)
    mine = lax.dynamic_slice_in_dim(value_part, dp_at * own, own, 0)
    value_grad = mine + lax.ppermute(theirs, "dp", [(0, 1), (1, 0)])
    mixed = jnp.sum(mixed_got.astype(F32), axis=0).astype(BF)
    return (mixed, token_grad, qw_grad, first_grad, second_grad, value_grad)


def solution(mesh):
    return jax.shard_map(
        body,
        mesh=mesh,
        in_specs=(
            P(("dp", "row"), "dim"),
            P("dim", None),
            P(),
            P(),
            P("row", "dim"),
            P(("dp", "row"), None),
            P(("dp", "row"), "dim"),
        ),
        out_specs=(
            P(("dp", "row"), "dim"),
            P(("dp", "row"), "dim"),
            P("dim", None),
            P(),
            P(),
            P(("row", "dp"), "dim"),
        ),
        check_vma=False,
    )
```

time: 644 us -> 249 us (0.39)
  waiting for transfers between devices: 235 us -> 58.6 us
  other arithmetic: 159 us -> 9.63 us
  local copies, waits for them, and re-layouts: 164 us -> 24.1 us
  Pallas kernels: 0 us -> 47.5 us
  blocking collectives: 38.5 us -> 61.4 us
  starting transfers between devices: 20.7 us -> 41 us
  between operations: 15.9 us -> 0.95 us
  matrix products: 10.1 us -> 2.05 us
    gather x13 -> x0, local copies, waits for them, and re-layouts: 111 us -> none  [the longest x5 33.1 us: body(): jnp.take_along_axis(second_scores, second_index, 1)]
    psum x1 -> x0, waiting for transfers between devices: 103 us -> none  [body(): lax.psum((weight_part, first_part, second_part), ('dp', 'row'))]
    all_to_all x3 -> x4, waiting for transfers between devices: 132 us -> 39.3 us  [the longest x1 39.1 us: body(): lax.all_to_all(mixed_part.reshape(n_row, tok, cols), 'row', 0, 0, tiled=T...]
    scatter-add x1 -> x0, other arithmetic: 56.2 us -> none  [body(): jnp.zeros((row_dev, value_cols), jnp.float32).at[flat_rows].add(contrib)]
    unnamed x5 -> x1, other arithmetic: 50.5 us -> 0.86 us
    pallas_call x0 -> x4, Pallas kernels: none -> 47.5 us  [the longest x1 23.5 us: owner_side(): pl.pallas_call(owner_kernel, grid_spec=pltpu.PrefetchScalarGridSpec(num_s...]
    scatter x2 -> x0, local copies, waits for them, and re-layouts: 44.1 us -> none  [the longest x1 28.6 us: body(): send_weight = jnp.zeros((n_row * capacity,), jnp.bfloat16).at[slot].set(w...]
    scatter x1 -> x0, other arithmetic: 35.5 us -> none  [body(): send_grad = jnp.zeros((n_row * capacity, value_cols), jnp.bfloat16).at[sl...]
  transfers between devices with their start and end apart: 5 -> 16, of which waited for: 3 -> 10; matrix products, arithmetic and copies ran while one was open for 24% -> 7% of each run, Pallas kernels for 0% -> 8%
where the time goes in v1:
time: 249 us; the launch traced here: 245 us
  blocking collectives  61.4 us (25%)
  waiting for transfers between devices  58.6 us (24%)
  Pallas kernels  47.5 us (19%)
  starting transfers between devices  41 us (16%)
  local copies, waits for them, and re-layouts  24.1 us (10%)
  other arithmetic  9.63 us (4%)
    all_to_all x1, waiting for transfers between devices, body(): lax.all_to_all(mixed_part.reshape(n_row, tok, cols), 'row', 0, 0, tiled=T...  39.1 us
    all_to_all x1, blocking collectives, body(): lax.all_to_all(sums.reshape(n_row, share, -1), 'row', 0, 0, tiled=True)  26.7 us
    pallas_call x1, Pallas kernels, owner_side(): pl.pallas_call(owner_kernel, grid_spec=pltpu.PrefetchScalarGridSpec(num_s...  23.5 us
    all_to_all x1, blocking collectives, body(): lax.all_to_all(pick_sent, ('row', 'dim'), 0, 0, tiled=True)  22.6 us
    unnamed x44, local copies, waits for them, and re-layouts  15.9 us
    all_gather x1, blocking collectives, body(): query = lax.all_gather(quarter, 'dim', tiled=True)  12 us
    ppermute x3, starting transfers between devices, gather_blocks(): down = lax.ppermute(down, 'row', shift(0, -1))  10.4 us
    pallas_call x1, Pallas kernels, scatter(): pl.pallas_call(scatter_kernel, grid=(rows // tile,), in_specs=[whole(list...  10.2 us
  transfers between devices with their start and end apart: 16, of which 10 were waited for; matrix products, arithmetic and copies ran while one was open for 7% of the time, Pallas kernels for 8%

profile of v1, /device:TPU:8, one launch (start us, length us, event | category | flops | bytes accessed | tf_op | source)
XLA Modules:
  0.0 245.2 jit_solution(14681048141614392426)
XLA Ops:
  0.7 1.6 collective-permute-start
  2.2 2.7 %collective-permute-start.1 = (bf16[128,256]{1,0:T(8,128)(2,1)}, bf16[128,256]{1,0:T(8,128)(2,1)S(1)}, u32[]{:S(2)}, u32[]{:S(2)}) collective-permute-start(bf16[128,256]{1,0:T(8,128)(2,1)} %param.13), channel_id=1, source_target_pairs={{0,64},{4,68},{8,72},{12,76},{16,80},{20,84},{24,88},{28,92},{32,9... | collective-permute-start | bytes 196616 | tf_op jit(solution)/shard_map/ppermute | solution.py:284
  5.0 1.4 collective-permute-start.2
  7.0 1.4 collective-permute-done.1
  8.4 1.1 collective-permute-done.2
  9.4 0.9 pad_maximum_fusion.1
  10.4 2.0 collective-permute-start.6
  12.3 4.0 %collective-permute-start.3 = (bf16[4,128,256]{2,1,0:T(8,128)(2,1)S(1)}, bf16[4,128,256]{2,1,0:T(8,128)(2,1)}, u32[]{:S(2)}, u32[]{:S(2)}) collective-permute-start(bf16[4,128,256]{2,1,0:T(8,128)(2,1)S(1)} %pad_maximum_fusion.1), channel_id=1, source_target_pairs={{0,28},{4,0},{8,4},{12,8},{16,12},{20,16},{24,20},{28,24},{32,60},... | collective-permute-start | bytes 786440 | tf_op jit(solution)/shard_map/ppermute | solution.py:291
  16.4 5.1 %collective-permute-done.6 = bf16[4,128,256]{2,1,0:T(8,128)(2,1)} collective-permute-done((bf16[4,128,256]{2,1,0:T(8,128)(2,1)S(1)}, bf16[4,128,256]{2,1,0:T(8,128)(2,1)}, u32[]{:S(2)}, u32[]{:S(2)}) %collective-permute-start.6) | collective-permute-done | bytes 262176 | tf_op jit(solution)/shard_map/ppermute | solution.py:288
  21.5 2.1 fusion.7
  23.6 4.9 %all-to-all-start = ((f32[4,32,512]{2,1,0:T(8,128)}), f32[4,32,512]{2,1,0:T(8,128)}, u32[]{:S(2)}, u32[]{:S(2)}) async-start(f32[4,32,512]{2,1,0:T(8,128)} %bitcast), calls=%async_computation | async-start | bytes 524288 | tf_op jit(solution)/shard_map/all_to_all | solution.py:308
  29.2 3.3 %collective-permute-start.4 = (bf16[4,128,256]{2,1,0:T(8,128)(2,1)}, bf16[4,128,256]{2,1,0:T(8,128)(2,1)}, u32[]{:S(2)}, u32[]{:S(2)}) collective-permute-start(bf16[4,128,256]{2,1,0:T(8,128)(2,1)} %collective-permute-done.3), channel_id=1, source_target_pairs={{0,28},{4,0},{8,4},{12,8},{16,12},{20,16},{24,20},{28,24},{32,60},... | collective-permute-start | bytes 786440 | tf_op jit(solution)/shard_map/ppermute | solution.py:291
  33.0 0.9 bitcast_dynamic-update-slice_fusion.7
  33.9 1.0 reduce_sum.30
  35.0 12.0 %all_gather.3.query_ref = bf16[128,512]{1,0:T(8,128)(2,1)S(1)} all-gather(bf16[32,512]{1,0:T(8,128)(2,1)S(1)} %reduce_sum.30), channel_id=1, replica_groups=mesh['dp'=2,'row'=32,'dim'=4] {'dim'}, dimensions={0}, use_global_device_ids=true | all-gather | bytes 163840 | tf_op jit(solution)/shard_map/all_gather | solution.py:310
  47.0 1.0 copy-done.3
  48.0 9.4 %route.1 = (f32[32,8,128]{2,1,0:T(8,128)}, s32[32,128]{1,0:T(8,128)S(1)}, f32[32,128]{1,0:T(8,128)S(1)}) custom-call(bf16[128,512]{1,0:T(8,128)(2,1)S(1)} %all_gather.3.query_ref, bf16[64,256]{1,0:T(8,128)(2,1)S(1)} %copy-done.6, bf16[1024,256]{1,0:T(8,128)(2,1)S(1)} %copy-done.3, s32[32,128]{1,0:T(8,128)S(1)} %bitcast.32), custom_call_target="tpu_custom_call" | custom-call | tf_op jit(solution)/shard_map/route/pallas_call | solution.py:93
  58.6 8.3 %all-to-all-start.1 = ((f32[32,8,128]{2,1,0:T(8,128)}), f32[32,8,128]{2,1,0:T(8,128)S(1)}, u32[]{:S(2)}, u32[]{:S(2)}) async-start(f32[32,8,128]{2,1,0:T(8,128)} %get-tuple-element.16), calls=%async_computation.1 | async-start | bytes 262144 | tf_op jit(solution)/shard_map/all_to_all | solution.py:313
  66.9 3.1 %collective-permute-start.5 = (bf16[4,128,256]{2,1,0:T(8,128)(2,1)}, bf16[4,128,256]{2,1,0:T(8,128)(2,1)S(1)}, u32[]{:S(2)}, u32[]{:S(2)}) collective-permute-start(bf16[4,128,256]{2,1,0:T(8,128)(2,1)} %collective-permute-done.4), channel_id=1, source_target_pairs={{0,28},{4,0},{8,4},{12,8},{16,12},{20,16},{24,20},{28,24},{32,60},... | collective-permute-start | bytes 786440 | tf_op jit(solution)/shard_map/ppermute | solution.py:291
  70.0 1.0 bitcast_dynamic-update-slice_fusion.6
  71.1 1.0 bitcast_dynamic-update-slice_fusion.5
  72.0 2.5 %collective-permute-done.5 = bf16[4,128,256]{2,1,0:T(8,128)(2,1)S(1)} collective-permute-done((bf16[4,128,256]{2,1,0:T(8,128)(2,1)}, bf16[4,128,256]{2,1,0:T(8,128)(2,1)S(1)}, u32[]{:S(2)}, u32[]{:S(2)}) %collective-permute-start.5) | collective-permute-done | bytes 262176 | tf_op jit(solution)/shard_map/ppermute | solution.py:291
  74.6 4.3 %collective-permute-done.9 = bf16[4,128,256]{2,1,0:T(8,128)(2,1)S(1)} collective-permute-done((bf16[4,128,256]{2,1,0:T(8,128)(2,1)}, bf16[4,128,256]{2,1,0:T(8,128)(2,1)S(1)}, u32[]{:S(2)}, u32[]{:S(2)}) %collective-permute-start.9) | collective-permute-done | bytes 262176 | tf_op jit(solution)/shard_map/ppermute | solution.py:288
  78.9 1.0 bitcast_dynamic-update-slice_fusion.2
  79.8 1.0 bitcast_dynamic-update-slice_fusion.1
  80.8 1.0 bitcast_dynamic-update-slice_fusion
  82.5 23.5 %owner_side.1 = (bf16[4096,256]{1,0:T(8,128)(2,1)}, f32[32,1,256]{2,1,0:T(1,128)S(1)}, bf16[256,8192]{1,0:T(8,128)(2,1)S(1)}) custom-call(s32[32]{0:T(128)S(1)} %copy-done.13, f32[32,8,128]{2,1,0:T(8,128)S(1)} %all-to-all-done.1.lists_ref, bf16[4096,256]{1,0:T(8,128)(2,1)S(1)} %bitcast.31, bf16[256,2048]{1,0:T(8,128)(2,1)S(1)} %bitcast.30), custom_call_target="tpu_custom_call" | custom-call | tf_op jit(solution)/shard_map/owner_side/pallas_call | solution.py:138
  105.9 2.0 copy-done
  108.1 22.6 %all_to_all.38 = f32[128,1,256]{2,1,0:T(1,128)S(1)} all-to-all(f32[128,1,256]{2,1,0:T(1,128)S(1)} %all_to_all.28), channel_id=1, replica_groups=mesh['dp'=2,'row'=32,'dim'=4] {'row','dim'}, dimensions={0} | all-to-all | bytes 262144 | tf_op jit(solution)/shard_map/all_to_all | solution.py:323
  131.1 1.0 copy-done.2
  132.1 1.0 copy-done.4
  135.4 4.4 %grads.1 = (bf16[128,512]{1,0:T(8,128)(2,1)}, bf16[512,512]{1,0:T(8,128)(2,1)S(1)}, bf16[64,256]{1,0:T(8,128)(2,1)S(1)}, bf16[1024,256]{1,0:T(8,128)(2,1)S(1)}) custom-call(f32[32,4,256]{2,1,0:T(4,128)S(1)} %reshape.45.parts_ref, s32[32,128]{1,0:T(8,128)S(1)} %copy-done.10, s32[32,128]{1,0:T(8,128)S(1)} %bitcast.33, f32[32,128]{1,0:T(8,128)S(1)} %copy-done.12, ...), custom_call_target="tpu_custom_call" | custom-call | tf_op jit(solution)/shard_map/grads/pallas_call | solution.py:258
  139.9 1.0 pad_maximum_fusion
  141.0 1.4 reshape.47
  142.3 26.7 %all_to_all.39 = bf16[32,66,256]{2,1,0:T(8,128)(2,1)S(1)} all-to-all(bf16[32,66,256]{2,1,0:T(8,128)(2,1)S(1)} %reshape.47), channel_id=1, replica_groups=mesh['dp'=2,'row'=32,'dim'=4] {'row'}, dimensions={0} | all-to-all | bytes 2162688 | tf_op jit(solution)/shard_map/all_to_all | solution.py:332
  169.1 4.0 %all-to-all-start.2 = ((bf16[32,128,256]{2,1,0:T(8,128)(2,1)}), bf16[32,128,256]{2,1,0:T(8,128)(2,1)S(1)}, u32[]{:S(2)}, u32[]{:S(2)}) async-start(bf16[32,128,256]{2,1,0:T(8,128)(2,1)} %bitcast.16), calls=%async_computation.2 | async-start | bytes 4194304 | tf_op jit(solution)/shard_map/all_to_all | solution.py:325
  173.4 1.3 collective-permute-done.10
  174.6 39.1 %all-to-all-done.2 = bf16[32,128,256]{2,1,0:T(8,128)(2,1)S(1)} async-done(((bf16[32,128,256]{2,1,0:T(8,128)(2,1)}), bf16[32,128,256]{2,1,0:T(8,128)(2,1)S(1)}, u32[]{:S(2)}, u32[]{:S(2)}) %all-to-all-start.2) | async-done | bytes 2097184 | tf_op jit(solution)/shard_map/all_to_all | solution.py:325
  213.8 1.2 broadcast_in_dim.15
  214.9 5.4 %all-to-all-start.5 = ((bf16[32,66,256]{2,1,0:T(8,128)(2,1)}), bf16[32,66,256]{2,1,0:T(8,128)(2,1)S(1)}, u32[]{:S(2)}, u32[]{:S(2)}) async-start(bf16[32,66,256]{2,1,0:T(8,128)(2,1)} %broadcast_in_dim.15), calls=%async_computation.5 | async-start | bytes 2359296 | tf_op jit(solution)/shard_map/all_to_all | solution.py:336
  220.3 2.2 copy-done.1
  222.5 10.2 %scatter.1 = f32[2048,256]{1,0:T(8,128)S(1)} custom-call(f32[32,8,128]{2,1,0:T(8,128)S(1)} %all-to-all-done.1.lists_ref, bf16[256,8192]{1,0:T(8,128)(2,1)S(1)} %copy-done.1), custom_call_target="tpu_custom_call" | custom-call | tf_op jit(solution)/shard_map/scatter/pallas_call | solution.py:179
  232.8 1.0 constant_dynamic-slice_fusion
  233.8 3.0 %collective-permute-done.11 = f32[1024,256]{1,0:T(8,128)} collective-permute-done((f32[1024,256]{1,0:T(8,128)}, f32[1024,256]{1,0:T(8,128)}, u32[]{:S(2)}, u32[]{:S(2)}) %collective-permute-start.11) | collective-permute-done | bytes 1048608 | tf_op jit(solution)/shard_map/ppermute | solution.py:347
  236.8 2.3 dynamic-slice_add_fusion
  239.1 2.5 %reduce_sum.31 = bf16[128,256]{1,0:T(8,128)(2,1)} reduce(bf16[32,128,256]{2,1,0:T(8,128)(2,1)} %copy-done.14, bf16[]{:T(256)} %constant.81.clone.1), dimensions={0}, to_apply=%region_1.2 | reduce | flops 1015808 | bytes 2162690 | tf_op jit(solution)/shard_map/reduce_sum | solution.py:348
  242.2 1.1 fusion.6
  243.9 1.3 reshape.48
  (58 shorter events, 8.2 us)
Async XLA Ops:
  0.6 32.4 %copy-start.16 = (bf16[128,256]{1,0:T(8,128)(2,1)S(1)}, bf16[128,256]{1,0:T(8,128)(2,1)}, u32[]{:S(2)}) copy-start(bf16[128,256]{1,0:T(8,128)(2,1)} %param.13) | copy-start | bytes 196612
  0.6 27.9 %copy-start.15 = (bf16[2048,256]{1,0:T(8,128)(2,1)S(1)}, bf16[2048,256]{1,0:T(8,128)(2,1)}, u32[]{:S(2)}) copy-start(bf16[2048,256]{1,0:T(8,128)(2,1)} %param.11) | copy-start | bytes 3145732
  0.7 6.4 %collective-permute-start = (bf16[128,256]{1,0:T(8,128)(2,1)}, bf16[128,256]{1,0:T(8,128)(2,1)S(1)}, u32[]{:S(2)}, u32[]{:S(2)}) collective-permute-start(bf16[128,256]{1,0:T(8,128)(2,1)} %param.13), channel_id=1, source_target_pairs={{0,32},{4,36},{8,40},{12,44},{16,48},{20,52},{24,56},{28,60},{32,6... | collective-permute-start | bytes 196616 | tf_op jit(solution)/shard_map/ppermute | solution.py:284
  2.2 6.2 %collective-permute-start.1 = (bf16[128,256]{1,0:T(8,128)(2,1)}, bf16[128,256]{1,0:T(8,128)(2,1)S(1)}, u32[]{:S(2)}, u32[]{:S(2)}) collective-permute-start(bf16[128,256]{1,0:T(8,128)(2,1)} %param.13), channel_id=1, source_target_pairs={{0,64},{4,68},{8,72},{12,76},{16,80},{20,84},{24,88},{28,92},{32,9... | collective-permute-start | bytes 196616 | tf_op jit(solution)/shard_map/ppermute | solution.py:284
  5.0 4.5 %collective-permute-start.2 = (bf16[128,256]{1,0:T(8,128)(2,1)}, bf16[128,256]{1,0:T(8,128)(2,1)S(1)}, u32[]{:S(2)}, u32[]{:S(2)}) collective-permute-start(bf16[128,256]{1,0:T(8,128)(2,1)} %param.13), channel_id=1, source_target_pairs={{0,96},{4,100},{8,104},{12,108},{16,112},{20,116},{24,120},{28,124... | collective-permute-start | bytes 196616 | tf_op jit(solution)/shard_map/ppermute | solution.py:284
  9.4 23.0 %copy-start.17 = (bf16[128,256]{1,0:T(8,128)(2,1)}, bf16[128,256]{1,0:T(8,128)(2,1)S(1)}, u32[]{:S(2)}) copy-start(bf16[128,256]{1,0:T(8,128)(2,1)S(1)} %collective-permute-done.2) | copy-start | bytes 196612
  10.3 36.6 %copy-start.6 = (bf16[64,256]{1,0:T(8,128)(2,1)S(1)}, bf16[64,256]{1,0:T(8,128)(2,1)}, u32[]{:S(2)}) copy-start(bf16[64,256]{1,0:T(8,128)(2,1)} %first_ref.3) | copy-start | bytes 98308
  10.3 36.6 %copy-start.8 = (s32[128,32]{0,1:T(8,128)S(1)}, s32[128,32]{0,1:T(8,128)}, u32[]{:S(2)}) copy-start(s32[128,32]{0,1:T(8,128)} %param.12) | copy-start | bytes 49156
  10.4 11.2 %collective-permute-start.6 = (bf16[4,128,256]{2,1,0:T(8,128)(2,1)S(1)}, bf16[4,128,256]{2,1,0:T(8,128)(2,1)}, u32[]{:S(2)}, u32[]{:S(2)}) collective-permute-start(bf16[4,128,256]{2,1,0:T(8,128)(2,1)S(1)} %pad_maximum_fusion.1), channel_id=1, source_target_pairs={{0,4},{4,8},{8,12},{12,16},{16,20},{20,24},{24,28},{28,0},{32,36},... | collective-permute-start | bytes 786440 | tf_op jit(solution)/shard_map/ppermute | solution.py:288
  12.3 16.8 %collective-permute-start.3 = (bf16[4,128,256]{2,1,0:T(8,128)(2,1)S(1)}, bf16[4,128,256]{2,1,0:T(8,128)(2,1)}, u32[]{:S(2)}, u32[]{:S(2)}) collective-permute-start(bf16[4,128,256]{2,1,0:T(8,128)(2,1)S(1)} %pad_maximum_fusion.1), channel_id=1, source_target_pairs={{0,28},{4,0},{8,4},{12,8},{16,12},{20,16},{24,20},{28,24},{32,60},... | collective-permute-start | bytes 786440 | tf_op jit(solution)/shard_map/ppermute | solution.py:291
  21.5 13.3 %collective-permute-start.7 = (bf16[4,128,256]{2,1,0:T(8,128)(2,1)}, bf16[4,128,256]{2,1,0:T(8,128)(2,1)}, u32[]{:S(2)}, u32[]{:S(2)}) collective-permute-start(bf16[4,128,256]{2,1,0:T(8,128)(2,1)} %collective-permute-done.6), channel_id=1, source_target_pairs={{0,4},{4,8},{8,12},{12,16},{16,20},{20,24},{24,28},{28,0},{32,36},... | collective-permute-start | bytes 786440 | tf_op jit(solution)/shard_map/ppermute | solution.py:288
  23.6 10.3 %all-to-all-start = ((f32[4,32,512]{2,1,0:T(8,128)}), f32[4,32,512]{2,1,0:T(8,128)}, u32[]{:S(2)}, u32[]{:S(2)}) async-start(f32[4,32,512]{2,1,0:T(8,128)} %bitcast), calls=%async_computation | async-start | bytes 524288 | tf_op jit(solution)/shard_map/all_to_all | solution.py:308
  29.2 37.7 %collective-permute-start.4 = (bf16[4,128,256]{2,1,0:T(8,128)(2,1)}, bf16[4,128,256]{2,1,0:T(8,128)(2,1)}, u32[]{:S(2)}, u32[]{:S(2)}) collective-permute-start(bf16[4,128,256]{2,1,0:T(8,128)(2,1)} %collective-permute-done.3), channel_id=1, source_target_pairs={{0,28},{4,0},{8,4},{12,8},{16,12},{20,16},{24,20},{28,24},{32,60},... | collective-permute-start | bytes 786440 | tf_op jit(solution)/shard_map/ppermute | solution.py:291
  34.9 36.1 %collective-permute-start.8 = (bf16[4,128,256]{2,1,0:T(8,128)(2,1)}, bf16[4,128,256]{2,1,0:T(8,128)(2,1)}, u32[]{:S(2)}, u32[]{:S(2)}) collective-permute-start(bf16[4,128,256]{2,1,0:T(8,128)(2,1)} %collective-permute-done.7), channel_id=1, source_target_pairs={{0,4},{4,8},{8,12},{12,16},{16,20},{20,24},{24,28},{28,0},{32,36},... | collective-permute-start | bytes 786440 | tf_op jit(solution)/shard_map/ppermute | solution.py:288
  47.0 1.0 copy-start.3
  57.4 0.6 copy-start.9
  58.0 0.6 copy-start.11
  58.6 23.2 %all-to-all-start.1 = ((f32[32,8,128]{2,1,0:T(8,128)}), f32[32,8,128]{2,1,0:T(8,128)S(1)}, u32[]{:S(2)}, u32[]{:S(2)}) async-start(f32[32,8,128]{2,1,0:T(8,128)} %get-tuple-element.16), calls=%async_computation.1 | async-start | bytes 262144 | tf_op jit(solution)/shard_map/all_to_all | solution.py:313
  66.9 7.6 %collective-permute-start.5 = (bf16[4,128,256]{2,1,0:T(8,128)(2,1)}, bf16[4,128,256]{2,1,0:T(8,128)(2,1)S(1)}, u32[]{:S(2)}, u32[]{:S(2)}) collective-permute-start(bf16[4,128,256]{2,1,0:T(8,128)(2,1)} %collective-permute-done.4), channel_id=1, source_target_pairs={{0,28},{4,0},{8,4},{12,8},{16,12},{20,16},{24,20},{28,24},{32,60},... | collective-permute-start | bytes 786440 | tf_op jit(solution)/shard_map/ppermute | solution.py:291
  71.0 7.9 %collective-permute-start.9 = (bf16[4,128,256]{2,1,0:T(8,128)(2,1)}, bf16[4,128,256]{2,1,0:T(8,128)(2,1)S(1)}, u32[]{:S(2)}, u32[]{:S(2)}) collective-permute-start(bf16[4,128,256]{2,1,0:T(8,128)(2,1)} %collective-permute-done.8), channel_id=1, source_target_pairs={{0,4},{4,8},{8,12},{12,16},{16,20},{20,24},{24,28},{28,0},{32,36},... | collective-permute-start | bytes 786440 | tf_op jit(solution)/shard_map/ppermute | solution.py:288
  81.8 0.7 copy-start.13
  82.5 48.6 %copy-start.5 = (bf16[128,512]{1,0:T(8,128)(2,1)S(1)}, bf16[128,512]{1,0:T(8,128)(2,1)}, u32[]{:S(2)}) copy-start(bf16[128,512]{1,0:T(8,128)(2,1)} %tokens_ref.1) | copy-start | bytes 393220
  105.9 2.0 copy-start
  131.1 1.0 copy-start.2
  132.1 1.0 copy-start.4
  133.2 0.8 copy-start.7
  133.9 0.7 copy-start.10
  134.7 0.7 copy-start.12
  169.1 44.7 %all-to-all-start.2 = ((bf16[32,128,256]{2,1,0:T(8,128)(2,1)}), bf16[32,128,256]{2,1,0:T(8,128)(2,1)S(1)}, u32[]{:S(2)}, u32[]{:S(2)}) async-start(bf16[32,128,256]{2,1,0:T(8,128)(2,1)} %bitcast.16), calls=%async_computation.2 | async-start | bytes 4194304 | tf_op jit(solution)/shard_map/all_to_all | solution.py:325
  173.3 1.4 collective-permute-start.10
  213.8 6.6 %copy-start.14 = (bf16[32,128,256]{2,1,0:T(8,128)(2,1)}, bf16[32,128,256]{2,1,0:T(8,128)(2,1)S(1)}, u32[]{:S(2)}) copy-start(bf16[32,128,256]{2,1,0:T(8,128)(2,1)S(1)} %all-to-all-done.2) | copy-start | bytes 6291460
  214.9 27.0 %all-to-all-start.5 = ((bf16[32,66,256]{2,1,0:T(8,128)(2,1)}), bf16[32,66,256]{2,1,0:T(8,128)(2,1)S(1)}, u32[]{:S(2)}, u32[]{:S(2)}) async-start(bf16[32,66,256]{2,1,0:T(8,128)(2,1)} %broadcast_in_dim.15), calls=%async_computation.5 | async-start | bytes 2359296 | tf_op jit(solution)/shard_map/all_to_all | solution.py:336
  220.3 2.2 copy-start.1
  233.8 3.0 %collective-permute-start.11 = (f32[1024,256]{1,0:T(8,128)}, f32[1024,256]{1,0:T(8,128)}, u32[]{:S(2)}, u32[]{:S(2)}) collective-permute-start(f32[1024,256]{1,0:T(8,128)} %constant_dynamic-slice_fusion), channel_id=1, source_target_pairs={{0,128},{128,0},{1,129},{129,1},{2,130},{130,2},{3,131},{131,3},{4... | collective-permute-start | bytes 3145736 | tf_op jit(solution)/shard_map/ppermute | solution.py:347

commit v2 on v1

v2 whole, which is shorter than its diff:
```python
import functools

import jax
import jax.numpy as jnp
from jax import lax
from jax.experimental import pallas as pl
from jax.experimental.pallas import tpu as pltpu
from jax.sharding import PartitionSpec as P

BF = jnp.bfloat16
F32 = jnp.float32
I32 = jnp.int32
NT = (((1,), (1,)), ((), ()))
TN = (((0,), (0,)), ((), ()))
MIB = 1 << 20


def dot(x, y, dims=(((1,), (0,)), ((), ()))):
    return lax.dot_general(x, y, dims, preferred_element_type=F32)


def iota(shape, dim):
    return lax.broadcasted_iota(I32, shape, dim)


def whole(shape):
    return pl.BlockSpec(shape, lambda *_: (0,) * len(shape))


def owner_order(picks, row_dev, n_z, n_x):
    owner = picks // row_dev
    return owner % n_z * n_x + owner // n_z


def small_iota(shape, dim):
    return iota(shape, dim).astype(F32).astype(BF)


def small(array):
    return array.astype(F32).astype(BF)


def hot_slots(slots, rank):
    topk, tok = rank.shape
    at_slot = small_iota((slots.shape[0], tok), 0)
    rank = small(rank)
    one, zero = jnp.ones((), BF), jnp.zeros((), BF)
    for at in range(topk):
        slots[:, at * tok : (at + 1) * tok] = jnp.where(at_slot == rank[at : at + 1, :], one, zero)


def place_kernel(row_dev, n_z, n_row, picks_ref, rank_ref):
    topk, tok = picks_ref.shape
    owner = owner_order(picks_ref[...], row_dev, n_z, n_row // n_z)
    at_owner = iota((n_row, tok), 0)
    onehots = [(at_owner == owner[k : k + 1, :]) for k in range(topk)]
    stacked = jnp.concatenate([jnp.where(hot, 1.0, 0.0) for hot in onehots], axis=0).astype(BF)
    upto = jnp.where(iota((tok, tok), 0) <= iota((tok, tok), 1), 1.0, 0.0).astype(BF)
    running = dot(stacked, upto)
    totals = dot(stacked, jnp.ones((tok, tok), BF))
    base = jnp.full((n_row, tok), -1.0, F32)
    for k in range(topk):
        part = slice(k * n_row, (k + 1) * n_row)
        rank = jnp.sum(jnp.where(onehots[k], running[part] + base, 0.0), axis=0, keepdims=True)
        base = base + totals[part]
        rank_ref[k : k + 1, :] = rank.astype(I32)


def place_picks(picks_t, row_dev, n_row, n_z):
    return pl.pallas_call(
        functools.partial(place_kernel, row_dev, n_z, n_row),
        out_shape=jax.ShapeDtypeStruct(picks_t.shape, I32),
        compiler_params=pltpu.CompilerParams(vmem_limit_bytes=12 * MIB),
        cost_estimate=pl.CostEstimate(flops=1_000_000_000, bytes_accessed=200_000, transcendentals=0),
        name="place_picks",
    )(picks_t)


def take_rows(table, index):
    topk, tok = index.shape
    within, group = index % 8, index // 8
    parts = [slice(q, q + 8) for q in range(0, topk, 8)]
    found = [jnp.zeros((8, tok), F32) for _ in parts]
    for g in range(table.shape[0] // 8):
        rows = table[8 * g : 8 * g + 8, :]
        for q, part in enumerate(parts):
            got = jnp.take_along_axis(rows, within[part], axis=0, mode="promise_in_bounds")
            found[q] = jnp.where(group[part] == g, got, found[q])
    return jnp.concatenate(found, axis=0)


def weigh_kernel(
    row_dev, n_x, query_ref, first_ref, second_ref, picks_ref, rank_ref, grad_ref,
    sent_ref, weight_ref, score_a, score_b, lhs, slots,
):
    topk, tok = picks_ref.shape
    half = first_ref.shape[1]
    nb = second_ref.shape[0]
    n_z = sent_ref.shape[0]
    query = query_ref[...]
    score_a[...] = dot(first_ref[...], query[:, :half], NT)
    score_b[...] = dot(second_ref[...], query[:, half:], NT)
    picks = picks_ref[...]
    score = take_rows(score_a, picks // nb) + take_rows(score_b, picks % nb)
    expo = jnp.exp(score)
    weight = expo / jnp.sum(expo, axis=0, keepdims=True)
    weight_ref[...] = weight
    weight = weight.astype(BF)
    local = picks % row_dev
    high, low = small(local // 256), small(local % 256)
    owner = small(owner_order(picks, row_dev, n_z, n_x))
    rows = (4 * n_z * n_x, tok)
    at_owner = small(iota(rows, 0) // 4)
    kind = small(iota(rows, 0) % 4)
    token = small_iota((1, tok), 1)
    zero = jnp.zeros((), BF)
    for k in range(topk):
        at = slice(k, k + 1)
        value = jnp.where(kind == 0.0, weight[at, :], jnp.where(
            kind == 1.0, high[at, :], jnp.where(kind == 2.0, low[at, :], token)))
        lhs[:, k * tok : (k + 1) * tok] = jnp.where(at_owner == owner[at, :], value, zero)
    hot_slots(slots, rank_ref[...])
    lists = dot(lhs[...], slots[...], NT).astype(BF)
    for z in range(n_z):
        sent_ref[z, :tok, :] = grad_ref[...]
        sent_ref[z, tok:, :] = lists[4 * n_x * z : 4 * n_x * (z + 1)]


def weigh(query, keys_first, keys_second, picks_t, rank, out_grad, row_dev, n_x, n_z, cap):
    topk, tok = picks_t.shape
    cols = out_grad.shape[1]
    return pl.pallas_call(
        functools.partial(weigh_kernel, row_dev, n_x),
        out_shape=(
            jax.ShapeDtypeStruct((n_z, tok + 4 * n_x, cols), BF),
            jax.ShapeDtypeStruct((topk, tok), F32),
        ),
        scratch_shapes=[
            pltpu.VMEM((keys_first.shape[0], tok), F32),
            pltpu.VMEM((keys_second.shape[0], tok), F32),
            pltpu.VMEM((4 * n_x * n_z, topk * tok), BF),
            pltpu.VMEM((cap, topk * tok), BF),
        ],
        compiler_params=pltpu.CompilerParams(vmem_limit_bytes=12 * MIB),
        cost_estimate=pl.CostEstimate(flops=4_000_000_000, bytes_accessed=1_000_000, transcendentals=4096),
        name="weigh",
    )(query, keys_first, keys_second, picks_t, rank, out_grad)


def listed(lists, x_own, kind):
    return lists[pl.ds(4 * x_own + kind, 1), :]


def owner_kernel(place_ref, got_ref, *rest):
    n_x = (len(rest) - 5) // 2
    value_refs = rest[: 2 * n_x]
    mixed_ref, pick_ref, values, hot, lists = rest[2 * n_x :]
    cap = pick_ref.shape[2]
    half = value_refs[0].shape[0]
    rows = value_refs[0].shape[1]
    tok = mixed_ref.shape[0]
    x_at, dp_at = place_ref[0], place_ref[1]

    @pl.when(pl.program_id(0) == 0)
    def _():
        for s in range(n_x):
            for at, ref in ((dp_at, value_refs[2 * s]), (1 - dp_at, value_refs[2 * s + 1])):
                values[s, pl.ds(pl.multiple_of(at * half, half), half), :] = ref[...]

    lists[...] = got_ref[0, tok:, :].astype(F32)
    count = small_iota((256, cap), 0)
    one, zero = jnp.ones((), BF), jnp.zeros((), BF)
    picked = []
    weights = []
    tokens = []
    for s in range(n_x):
        x_own = lax.rem(x_at - s + n_x, n_x)
        weights.append(listed(lists, x_own, 0))
        tokens.append(listed(lists, x_own, 3))
        high, low = listed(lists, x_own, 1), listed(lists, x_own, 2)
        for at in range(rows // 256):
            here = jnp.where(high == at, low, -1.0).astype(BF)
            hot[s, at * 256 : (at + 1) * 256, :] = jnp.where(count == here, one, zero)
        picked.append(dot(values[s], hot[s]))
    picked = jnp.concatenate(picked, axis=1)
    token = jnp.concatenate(tokens, axis=1).astype(BF)
    weight = jnp.concatenate(weights, axis=1).astype(BF)
    at_token = small_iota((tok, n_x * cap), 0) == token
    spread = dot(got_ref[0, :tok, :], jnp.where(at_token, one, zero), TN)
    pick = jnp.sum(picked * spread, axis=0, keepdims=True)
    for s in range(n_x):
        x_own = lax.rem(x_at - s + n_x, n_x)
        pick_ref[0, pl.ds(x_own, 1), :] = pick[:, s * cap : (s + 1) * cap]
    mixed_ref[...] = dot(jnp.where(at_token, weight, zero), picked.astype(BF), NT)


def owner_side(place, got, value_halves, cap):
    blocks, tall, cols = got.shape
    n_x = len(value_halves) // 2
    tok = tall - 4 * n_x
    half, rows = value_halves[0].shape
    return pl.pallas_call(
        owner_kernel,
        grid_spec=pltpu.PrefetchScalarGridSpec(
            num_scalar_prefetch=1,
            grid=(blocks,),
            in_specs=[pl.BlockSpec((1, tall, cols), lambda b, place: (b, 0, 0))]
            + [pl.BlockSpec((half, rows), lambda *_: (0, 0), pipeline_mode=pl.Buffered(1))] * (2 * n_x),
            out_specs=[
                pl.BlockSpec((tok, cols), lambda b, place: (b, 0)),
                pl.BlockSpec((1, n_x, cap), lambda b, place: (b, 0, 0)),
            ],
            scratch_shapes=[
                pltpu.VMEM((n_x, cols, rows), BF),
                pltpu.VMEM((n_x, rows, cap), BF),
                pltpu.VMEM((4 * n_x, cap), F32),
            ],
        ),
        out_shape=(
            jax.ShapeDtypeStruct((blocks * tok, cols), F32),
            jax.ShapeDtypeStruct((blocks, n_x, cap), F32),
        ),
        compiler_params=pltpu.CompilerParams(vmem_limit_bytes=20 * MIB),
        cost_estimate=pl.CostEstimate(flops=12_000_000_000, bytes_accessed=10_000_000, transcendentals=0),
        name="owner_side",
    )(place, got, *value_halves)


def scatter_kernel(n_x, place_ref, *rest):
    got_refs = rest[:n_x]
    out_ref, hot, spread, lists = rest[-4:]
    blocks, tall, cols = got_refs[0].shape
    kinds = lists.shape[1]
    cap = spread.shape[1] // (n_x * blocks)
    tok = tall - kinds
    x_own = place_ref[0]
    one, zero = jnp.ones((), BF), jnp.zeros((), BF)

    @pl.when(pl.program_id(0) == 0)
    def _():
        at_token = small_iota((tok, cap), 0)
        for s in range(n_x):
            for b in range(blocks):
                at = s * blocks + b
                lists[at] = got_refs[s][b, tok:, :].astype(F32)
                token = listed(lists.at[at], x_own, 3).astype(BF)
                spread[:, at * cap : (at + 1) * cap] = dot(
                    got_refs[s][b, :tok, :], jnp.where(at_token == token, one, zero), TN
                ).astype(BF)

    chunk = (place_ref[2] * pl.num_programs(0) + pl.program_id(0)).astype(F32)
    count = small_iota((256, cap), 0)
    for at in range(n_x * blocks):
        weight = listed(lists.at[at], x_own, 0).astype(BF)
        high, low = listed(lists.at[at], x_own, 1), listed(lists.at[at], x_own, 2)
        here = jnp.where(high == chunk, low, -1.0).astype(BF)
        hot[:, at * cap : (at + 1) * cap] = jnp.where(count == here, weight, zero)
    total = dot(hot[...], spread[...], NT)
    if len(rest) > n_x + 4:
        total = total + rest[n_x][...].astype(F32)
    out_ref[...] = total.astype(out_ref.dtype)


def scatter(place, gots, rows, kind, come=()):
    n_x = len(gots)
    blocks, tall, cols = gots[0].shape
    cap = cols
    tok = tall - 4 * n_x
    half = rows // 2
    each = pl.BlockSpec((256, cols), lambda r, place: (r, 0))
    fixed = pl.BlockSpec(gots[0].shape, lambda r, place: (0, 0, 0), pipeline_mode=pl.Buffered(1))
    return pl.pallas_call(
        functools.partial(scatter_kernel, n_x),
        grid_spec=pltpu.PrefetchScalarGridSpec(
            num_scalar_prefetch=1,
            grid=(half // 256,),
            in_specs=[fixed] * n_x + [each] * len(come),
            out_specs=each,
            scratch_shapes=[
                pltpu.VMEM((256, n_x * blocks * cap), BF),
                pltpu.VMEM((cols, n_x * blocks * cap), BF),
                pltpu.VMEM((n_x * blocks, 4 * n_x, cap), F32),
            ],
        ),
        out_shape=jax.ShapeDtypeStruct((half, cols), kind),
        compiler_params=pltpu.CompilerParams(vmem_limit_bytes=16 * MIB),
        cost_estimate=pl.CostEstimate(flops=5_000_000_000, bytes_accessed=6_000_000, transcendentals=0),
        name="scatter_mine" if come else "scatter_theirs",
    )(place, *gots, *come)


def grads_kernel(
    row_dev, n_z, parts_ref, rank_ref, picks_ref, weight_ref, query_ref, first_ref, second_ref,
    qw_ref, tokens_ref, token_grad_ref, part_ref, slots, sums, grad_b,
):
    topk, tok = picks_ref.shape
    half = first_ref.shape[1]
    na, nb = first_ref.shape[0], second_ref.shape[0]
    n_row, cap = parts_ref.shape[0] * parts_ref.shape[2], parts_ref.shape[3]
    by_slot = jnp.sum(parts_ref[...], axis=1).reshape(n_row, cap)
    one = by_slot.astype(BF)
    rest = by_slot - one.astype(F32)
    two = rest.astype(BF)
    three = (rest - two.astype(F32)).astype(BF)
    hot_slots(slots, rank_ref[...])
    sums[...] = dot(jnp.concatenate([one, two, three], axis=0), slots[...])
    picks = picks_ref[...]
    owner = owner_order(picks, row_dev, n_z, n_row // n_z)
    at_owner = iota((n_row, tok), 0)
    rows = []
    for k in range(topk):
        got = sums[:, k * tok : (k + 1) * tok]
        got = got[:n_row] + got[n_row : 2 * n_row] + got[2 * n_row :]
        rows.append(jnp.sum(jnp.where(at_owner == owner[k : k + 1, :], got, 0.0), axis=0, keepdims=True))
    pick_grad = jnp.concatenate(rows, axis=0)
    weight = weight_ref[...]
    score_grad = weight * (pick_grad - jnp.sum(weight * pick_grad, axis=0, keepdims=True))
    first_index = picks // nb
    second_index = picks % nb
    grad_a = jnp.zeros((na, tok), F32)
    for k in range(topk):
        grad_a = grad_a + jnp.where(
            iota((na, tok), 0) == first_index[k : k + 1, :], score_grad[k : k + 1, :], 0.0
        )
    grad_a = grad_a.astype(BF)
    tile = 128

    def one_tile(i, carry):
        at_b = iota((tile, tok), 0) + i * tile
        total = jnp.zeros((tile, tok), F32)
        for k in range(topk):
            total = total + jnp.where(
                at_b == second_index[k : k + 1, :], score_grad[k : k + 1, :], 0.0
            )
        grad_b[pl.ds(pl.multiple_of(i * tile, tile), tile), :] = total.astype(BF)
        return carry

    lax.fori_loop(0, nb // tile, one_tile, 0)
    query = query_ref[...]
    query_grad = jnp.concatenate(
        [dot(grad_a, first_ref[...], TN), dot(grad_b[...], second_ref[...], TN)], axis=1
    ).astype(BF)
    token_grad_ref[...] = dot(query_grad, qw_ref[...], NT).astype(BF)
    qw_part = dot(query_grad, tokens_ref[...], TN).astype(BF)
    first_part = dot(query[:, :half], grad_a, (((0,), (1,)), ((), ()))).astype(BF)
    second_part = dot(query[:, half:], grad_b[...], (((0,), (1,)), ((), ()))).astype(BF)
    n_qw = tokens_ref.shape[1]
    for h in range(2):
        part_ref[h, :, :n_qw] = qw_part[h * half : (h + 1) * half]
        part_ref[h, :, n_qw : n_qw + nb // 2] = second_part[:, h * (nb // 2) : (h + 1) * (nb // 2)]
        end = n_qw + (nb + na) // 2
        part_ref[h, :, n_qw + nb // 2 : end] = first_part[:, h * (na // 2) : (h + 1) * (na // 2)]
        part_ref[h, :, end:] = jnp.zeros((half, part_ref.shape[2] - end), BF)


def unfold_kernel(place_ref, mine_ref, other_ref, qw_ref, first_ref, second_ref):
    n_qw, n_second, n_first = qw_ref.shape[0], second_ref.shape[0] // 2, first_ref.shape[0] // 2
    half = mine_ref.shape[0]
    for side, ref in ((place_ref[1], mine_ref), (place_ref[2], other_ref)):
        qw_ref[:, pl.ds(pl.multiple_of(side * half, half), half)] = ref[:, :n_qw].astype(F32).T
        second_ref[pl.ds(pl.multiple_of(side * n_second, n_second), n_second), :] = (
            ref[:, n_qw : n_qw + n_second].astype(F32).T
        )
        first_ref[pl.ds(pl.multiple_of(side * n_first, n_first), n_first), :] = (
            ref[:, n_qw + n_second : n_qw + n_second + n_first].astype(F32).T
        )


def unfold(place, mine, other, shapes):
    return pl.pallas_call(
        unfold_kernel,
        in_specs=[pl.BlockSpec(memory_space=pltpu.SMEM)] + [pl.BlockSpec(memory_space=pltpu.VMEM)] * 2,
        out_shape=tuple(jax.ShapeDtypeStruct(shape, F32) for shape in shapes),
        compiler_params=pltpu.CompilerParams(vmem_limit_bytes=12 * MIB),
        name="unfold",
    )(place, mine, other)


def grads(parts, rank, picks_t, weight, query, keys_first, keys_second, qw, tokens, row_dev, n_z):
    topk, tok = picks_t.shape
    cap = parts.shape[3]
    n_row = parts.shape[0] * parts.shape[2]
    na, half = keys_first.shape
    nb = keys_second.shape[0]
    return pl.pallas_call(
        functools.partial(grads_kernel, row_dev, n_z),
        out_shape=(
            jax.ShapeDtypeStruct(tokens.shape, BF),
            jax.ShapeDtypeStruct((2, half, -(-(qw.shape[0] + (na + nb) // 2) // 128) * 128), BF),
        ),
        scratch_shapes=[
            pltpu.VMEM((cap, topk * tok), BF),
            pltpu.VMEM((3 * n_row, topk * tok), F32),
            pltpu.VMEM((nb, tok), BF),
        ],
        compiler_params=pltpu.CompilerParams(vmem_limit_bytes=16 * MIB),
        cost_estimate=pl.CostEstimate(flops=4_000_000_000, bytes_accessed=4_000_000, transcendentals=0),
        name="grads",
    )(parts, rank, picks_t, weight, query, keys_first, keys_second, qw, tokens)


def body(tokens, query_weight, keys_first, keys_second, values, picks, out_grad):
    tok, topk = picks.shape
    row_dev, cols = values.shape
    na, half = keys_first.shape
    nb = keys_second.shape[0]
    n_row, n_dim = lax.axis_size("row"), lax.axis_size("dim")
    cap = 2 * tok * topk // n_row
    n_x = 4
    n_z = n_row // n_x
    row_at, dp_at = lax.axis_index("row"), lax.axis_index("dp")
    place = jnp.stack([row_at // n_z, dp_at, 1 - dp_at, row_at % n_z]).astype(I32)
    rings = [[x * n_z + z for z in range(n_z)] for x in range(n_x)]
    planes = [[r * n_dim + m for r in ring for m in range(n_dim)] for ring in rings]

    def other_core(array):
        return lax.ppermute(array, "dp", [(0, 1), (1, 0)])

    def along_x(array, shift):
        pairs = [(x * n_z + z, (x + shift) % n_x * n_z + z) for x in range(n_x) for z in range(n_z)]
        return lax.ppermute(array, "row", pairs)

    def along_dim(array, shift):
        return lax.ppermute(array, "dim", [(m, (m + shift) % n_dim) for m in range(n_dim)])

    partial = dot(tokens, query_weight)
    partial, values = lax.optimization_barrier((partial, values))
    near = [along_dim(partial, s) for s in (1, 2, 3)]
    picks_t = picks.T
    rank = place_picks(picks_t, row_dev, n_row, n_z)

    values_t = values.T
    own_half = lax.dynamic_slice_in_dim(values_t, dp_at * (cols // 2), cols // 2, 0)
    other_half = lax.dynamic_slice_in_dim(values_t, (1 - dp_at) * (cols // 2), cols // 2, 0)
    value_halves = [own_half, other_half]
    for s in range(1, n_x):
        got = along_x(own_half, s)
        value_halves += [got, other_core(got)]

    query = ((partial + near[1]) + (near[0] + near[2])).astype(BF)
    query, rank = lax.optimization_barrier((query, rank))
    sent, weight = weigh(
        query, keys_first, keys_second, picks_t, rank, out_grad, row_dev, n_x, n_z, cap
    )
    got = lax.all_to_all(sent, "row", 0, 0, tiled=True, axis_index_groups=rings)

    mixed_part, pick_part = owner_side(place, got, value_halves, cap)
    gots = [got] + [along_x(got, s) for s in range(1, n_x)]
    pick_sent = jnp.broadcast_to(pick_part[:, None], (n_z, n_dim, n_x, cap))
    pick_parts = lax.all_to_all(
        pick_sent.reshape(n_z * n_dim, n_x, cap), ("row", "dim"), 0, 0, tiled=True,
        axis_index_groups=planes,
    ).reshape(n_z, n_dim, n_x, cap)

    mixed = lax.psum_scatter(
        mixed_part, "row", tiled=True, axis_index_groups=rings
    ).astype(BF)
    pick_parts, gots = lax.optimization_barrier((pick_parts, gots))
    token_grad, sums = grads(
        pick_parts, rank, picks_t, weight, query, keys_first, keys_second, query_weight, tokens,
        row_dev, n_z,
    )
    theirs = lax.dynamic_index_in_dim(sums, 1 - dp_at, 0, keepdims=False)
    mine = lax.dynamic_index_in_dim(sums, dp_at, 0, keepdims=False)
    mine = (mine.astype(F32) + other_core(theirs).astype(F32)).astype(BF)
    shape = (n_row, half // n_row, mine.shape[1])
    received = lax.all_to_all(mine.reshape(shape), "row", 0, 0, tiled=True)
    summed = jnp.sum(received.astype(F32), axis=0).astype(BF)
    come = other_core(scatter(place, gots, row_dev, BF))
    summed, come = lax.optimization_barrier((summed, come))
    summed = jnp.broadcast_to(summed[None], shape)
    mine = lax.all_to_all(summed, "row", 0, 0, tiled=True).reshape(mine.shape)
    own_place = jnp.stack([row_at // n_z, dp_at, dp_at]).astype(I32)
    value_grad = scatter(own_place, gots, row_dev, F32, (come,))
    mine, mixed, value_grad = lax.optimization_barrier((mine, mixed, value_grad))
    other = other_core(mine)
    qw_grad, first_grad, second_grad = unfold(
        place, mine, other, (query_weight.shape, keys_first.shape, keys_second.shape)
    )
    return (mixed, token_grad, qw_grad, first_grad, second_grad, value_grad)


def solution(mesh):
    return jax.shard_map(
        body,
        mesh=mesh,
        in_specs=(
            P(("dp", "row"), "dim"),
            P("dim", None),
            P(),
            P(),
            P("row", "dim"),
            P(("dp", "row"), None),
            P(("dp", "row"), "dim"),
        ),
        out_specs=(
            P(("dp", "row"), "dim"),
            P(("dp", "row"), "dim"),
            P("dim", None),
            P(),
            P(),
            P(("row", "dp"), "dim"),
        ),
        check_vma=False,
    )
```

time: 249 us -> 167 us (0.67)
  blocking collectives: 61.4 us -> 0 us
  local copies, waits for them, and re-layouts: 24.1 us -> 6.06 us
  between operations: 0.95 us -> 14.2 us
  Pallas kernels: 47.5 us -> 41.8 us
  other arithmetic: 9.63 us -> 4.92 us
  starting transfers between devices: 41 us -> 38.4 us
    all_to_all x2 -> x0, blocking collectives: 49.4 us -> none  [the longest x1 26.7 us: body(): lax.all_to_all(sums.reshape(n_row, share, -1), 'row', 0, 0, tiled=True)]
    unnamed x44 -> x18, local copies, waits for them, and re-layouts: 15.9 us -> 2.9 us
    all_gather x1 -> x0, blocking collectives: 12 us -> none  [body(): query = lax.all_gather(quarter, 'dim', tiled=True)]
    ppermute x12 -> x15, waiting for transfers between devices: 19.2 us -> 11.3 us  [the longest x6 4.11 us: other_core(): return lax.ppermute(array, 'dp', [(0, 1), (1, 0)])]
    pallas_call x1, Pallas kernels: 23.5 us -> 15.6 us  [owner_side(): pl.pallas_call(owner_kernel, grid_spec=pltpu.PrefetchScalarGridSpec(num_s...]
    all_to_all x4, waiting for transfers between devices: 39.3 us -> 46.1 us  [the longest x1 16.7 us: body(): received = lax.all_to_all(mine.reshape(shape), 'row', 0, 0, tiled=True)]
    reduce_sum x3 -> x1, other arithmetic: 3.67 us -> 0.1 us  [body(): summed = jnp.sum(received.astype(F32), axis=0).astype(BF)]
    add x2 -> x0, other arithmetic: 2.85 us -> none  [the longest x1 2.33 us: body(): value_grad = mine + lax.ppermute(theirs, 'dp', [(0, 1), (1, 0)])]
  transfers between devices with their start and end apart: 16 -> 20, of which waited for: 10 -> 8; matrix products, arithmetic and copies ran while one was open for 7% -> 5% of each run, Pallas kernels for 8% -> 22%
where the time goes in v2:
time: 167 us; the launch traced here: 164 us
  waiting for transfers between devices  57.4 us (34%)
  Pallas kernels  41.8 us (25%)
  starting transfers between devices  38.4 us (23%)
  between operations  14.2 us (9%)
  local copies, waits for them, and re-layouts  6.06 us (4%)
  other arithmetic  4.92 us (3%)
    pallas_call x2, Pallas kernels, scatter(): pl.pallas_call(functools.partial(scatter_kernel, n_x), grid_spec=pltpu.Pr...  17.3 us
    all_to_all x1, waiting for transfers between devices, body(): received = lax.all_to_all(mine.reshape(shape), 'row', 0, 0, tiled=True)  16.7 us
    pallas_call x1, Pallas kernels, owner_side(): pl.pallas_call(owner_kernel, grid_spec=pltpu.PrefetchScalarGridSpec(num_s...  15.6 us
    all_to_all x1, waiting for transfers between devices, body(): got = lax.all_to_all(sent, 'row', 0, 0, tiled=True, axis_index_groups=rings)  12.6 us
    ppermute x6, starting transfers between devices, along_x(): return lax.ppermute(array, 'row', pairs)  11.5 us
    all_to_all x1, waiting for transfers between devices, body(): lax.all_to_all(pick_sent.reshape(n_z * n_dim, n_x, cap), ('row', 'dim'),...  8.92 us
    all_to_all x1, starting transfers between devices, body(): got = lax.all_to_all(sent, 'row', 0, 0, tiled=True, axis_index_groups=rings)  8.47 us
    all_to_all x1, waiting for transfers between devices, body(): mine = lax.all_to_all(summed, 'row', 0, 0, tiled=True).reshape(mine.shape)  7.79 us
  transfers between devices with their start and end apart: 20, of which 8 were waited for; matrix products, arithmetic and copies ran while one was open for 5% of the time, Pallas kernels for 22%

profile of v2, /device:TPU:8, one launch (start us, length us, event | category | flops | bytes accessed | tf_op | source)
XLA Modules:
  0.0 164.3 jit_solution(205668200553679157)
XLA Ops:
  7.2 1.3 fusion.2
  8.5 1.7 %collective-permute-start.1 = (f32[128,512]{1,0:T(8,128)S(1)}, f32[128,512]{1,0:T(8,128)S(1)}, u32[]{:S(2)}, u32[]{:S(2)}) collective-permute-start(f32[128,512]{1,0:T(8,128)S(1)} %fusion.2), channel_id=1, source_target_pairs={{0,1},{1,2},{2,3},{3,0},{4,5},{5,6},{6,7},{7,4},{8,9},{9,10},{10,1... | collective-permute-start | bytes 786440 | tf_op jit(solution)/shard_map/ppermute | solution.py:424
  10.2 0.7 collective-permute-start.2
  10.9 2.0 %collective-permute-start = (f32[128,512]{1,0:T(8,128)S(1)}, f32[128,512]{1,0:T(8,128)}, u32[]{:S(2)}, u32[]{:S(2)}) collective-permute-start(f32[128,512]{1,0:T(8,128)S(1)} %fusion.2), channel_id=1, source_target_pairs={{0,2},{1,3},{2,0},{3,1},{4,6},{5,7},{6,4},{7,5},{8,10},{9,11},{10,... | collective-permute-start | bytes 786440 | tf_op jit(solution)/shard_map/ppermute | solution.py:424
  12.9 1.5 copy.13
  14.4 0.1 dynamic-slice_bitcast_fusion.1
  14.5 1.6 collective-permute-start.3
  16.1 2.7 %collective-permute-start.5 = (bf16[128,2048]{1,0:T(8,128)(2,1)S(1)}, bf16[128,2048]{1,0:T(8,128)(2,1)}, u32[]{:S(2)}, u32[]{:S(2)}) collective-permute-start(bf16[128,2048]{1,0:T(8,128)(2,1)S(1)} %get-tuple-element.53.rest_0_), channel_id=1, source_target_pairs={{0,64},{4,68},{8,72},{12,76},{16,80},{20,84},{24,88},{28,92},{32,9... | collective-permute-start | bytes 1572872 | tf_op jit(solution)/shard_map/ppermute | solution.py:421
  18.8 0.3 place_picks.1.rank_ref
  19.2 1.5 collective-permute-start.7
  20.7 3.7 %collective-permute-done = f32[128,512]{1,0:T(8,128)} collective-permute-done((f32[128,512]{1,0:T(8,128)S(1)}, f32[128,512]{1,0:T(8,128)}, u32[]{:S(2)}, u32[]{:S(2)}) %collective-permute-start) | collective-permute-done | bytes 262176 | tf_op jit(solution)/shard_map/ppermute | solution.py:424
  24.4 1.1 add_convert_fusion.query_ref
  25.5 2.5 %weigh.1 = (bf16[8,144,256]{2,1,0:T(8,128)(2,1)}, f32[32,128]{1,0:T(8,128)S(1)}) custom-call(bf16[128,512]{1,0:T(8,128)(2,1)S(1)} %add_convert_fusion.query_ref, bf16[64,256]{1,0:T(8,128)(2,1)S(1)} %copy-done.7, bf16[1024,256]{1,0:T(8,128)(2,1)S(1)} %copy-done.2, s32[32,128]{1,0:T(8,128)S(1)} %bitcast.25, s32[32,128]{1,0:T(8,128)S(1)} %place_picks.1.rank_ref, ...), custom_call_target="tpu_custom_call" | custom-call | flops 4000000000 | bytes 1000000 | tf_op jit(solution)/shard_map/weigh/pallas_call | solution.py:132
  28.0 8.5 %all-to-all-start = ((bf16[8,144,256]{2,1,0:T(8,128)(2,1)}), bf16[8,144,256]{2,1,0:T(8,128)(2,1)S(1)}, u32[]{:S(2)}, u32[]{:S(2)}) async-start(bf16[8,144,256]{2,1,0:T(8,128)(2,1)} %get-tuple-element.32), calls=%async_computation | async-start | bytes 1179648 | tf_op jit(solution)/shard_map/all_to_all | solution.py:445
  36.5 0.1 collective-permute-start.4
  36.6 0.8 copy-done.4
  37.4 3.6 %collective-permute-done.5.rest_4_ = bf16[128,2048]{1,0:T(8,128)(2,1)} collective-permute-done((bf16[128,2048]{1,0:T(8,128)(2,1)S(1)}, bf16[128,2048]{1,0:T(8,128)(2,1)}, u32[]{:S(2)}, u32[]{:S(2)}) %collective-permute-start.5) | collective-permute-done | bytes 524320 | tf_op jit(solution)/shard_map/ppermute | solution.py:421
  41.0 0.5 collective-permute-start.8
  41.5 0.1 pad_add_fusion.place_ref
  41.6 12.6 %all-to-all-done.got_ref.rest_0_ = bf16[8,144,256]{2,1,0:T(8,128)(2,1)S(1)} async-done(((bf16[8,144,256]{2,1,0:T(8,128)(2,1)}), bf16[8,144,256]{2,1,0:T(8,128)(2,1)S(1)}, u32[]{:S(2)}, u32[]{:S(2)}) %all-to-all-start) | async-done | bytes 589856 | tf_op jit(solution)/shard_map/all_to_all | solution.py:445
  54.2 1.5 collective-permute-start.9
  55.7 2.7 %collective-permute-start.10 = (bf16[8,144,256]{2,1,0:T(8,128)(2,1)S(1)}, bf16[8,144,256]{2,1,0:T(8,128)(2,1)}, u32[]{:S(2)}, u32[]{:S(2)}) collective-permute-start(bf16[8,144,256]{2,1,0:T(8,128)(2,1)S(1)} %all-to-all-done.got_ref.rest_0_), channel_id=1, source_target_pairs={{0,64},{4,68},{8,72},{12,76},{16,80},{20,84},{24,88},{28,92},{32,9... | collective-permute-start | bytes 1769480 | tf_op jit(solution)/shard_map/ppermute | solution.py:421
  58.4 1.4 collective-permute-start.11
  59.9 1.0 copy-done.5
  60.9 15.6 %owner_side.1 = (f32[1024,256]{1,0:T(8,128)}, f32[8,4,256]{2,1,0:T(4,128)S(1)}) custom-call(s32[4]{0:T(128)S(1)} %pad_add_fusion.place_ref, bf16[8,144,256]{2,1,0:T(8,128)(2,1)S(1)} %all-to-all-done.got_ref.rest_0_, bf16[128,2048]{1,0:T(8,128)(2,1)S(1)} %get-tuple-element.53.rest_0_, bf16[128,2048]{1,0:T(8,128)(2,1)S(1)} %get-tuple-element.52.rest_1_, ...), custom_call_target="tpu_custom_call" | custom-call | flops 12000000000 | bytes 10000000 | tf_op jit(solution)/shard_map/owner_side/pallas_call | solution.py:202
  76.5 0.7 broadcast_in_dim.4
  77.2 4.9 %all-to-all-start.1 = ((f32[32,4,256]{2,1,0:T(4,128)}), f32[32,4,256]{2,1,0:T(4,128)S(1)}, u32[]{:S(2)}, u32[]{:S(2)}) async-start(f32[32,4,256]{2,1,0:T(4,128)} %bitcast.7), calls=%async_computation.1 | async-start | bytes 262144 | tf_op jit(solution)/shard_map/all_to_all | solution.py:450
  82.1 0.0 reduce-scatter.2.cloned.1.call-start
  82.1 8.9 %all-to-all-done.1 = f32[32,4,256]{2,1,0:T(4,128)S(1)} async-done(((f32[32,4,256]{2,1,0:T(4,128)}), f32[32,4,256]{2,1,0:T(4,128)S(1)}, u32[]{:S(2)}, u32[]{:S(2)}) %all-to-all-start.1) | async-done | bytes 131104 | tf_op jit(solution)/shard_map/all_to_all | solution.py:450
  91.1 1.0 copy-done.3
  92.1 3.9 %grads.1 = (bf16[128,512]{1,0:T(8,128)(2,1)}, bf16[2,256,1152]{2,1,0:T(8,128)(2,1)S(1)}) custom-call(f32[8,4,4,256]{3,2,1,0:T(4,128)S(1)} %bitcast.23, s32[32,128]{1,0:T(8,128)S(1)} %place_picks.1.rank_ref, s32[32,128]{1,0:T(8,128)S(1)} %bitcast.26, f32[32,128]{1,0:T(8,128)S(1)} %get-tuple-element.36.weight_ref, ...), custom_call_target="tpu_custom_call" | custom-call | flops 4000000000 | bytes 4000000 | tf_op jit(solution)/shard_map/grads/pallas_call | solution.py:385
  96.1 0.1 collective-permute-start.12
  96.2 0.0 reduce-scatter.2.cloned.1.call-update
  96.2 2.1 %collective-permute-done.12 = bf16[256,1152]{1,0:T(8,128)(2,1)} collective-permute-done((bf16[256,1152]{1,0:T(8,128)(2,1)S(1)}, bf16[256,1152]{1,0:T(8,128)(2,1)}, u32[]{:S(2)}, u32[]{:S(2)}) %collective-permute-start.12) | collective-permute-done | bytes 589856 | tf_op jit(solution)/shard_map/ppermute | solution.py:417
  98.3 2.0 %fusion.1 = bf16[32,8,1152]{2,1,0:T(8,128)(2,1)} fusion(bf16[256,1152]{1,0:T(8,128)(2,1)} %collective-permute-done.12, bf16[2,256,1152]{2,1,0:T(8,128)(2,1)S(1)} %get-tuple-element.37, s32[]{:T(128)S(6)} %select_n.29), kind=kLoop, calls=%fused_computation.2 | loop fusion | flops 1179648 | bytes 1769476 | tf_op jit(solution)/shard_map/reshape | solution.py:467
  100.4 3.9 %all-to-all-start.2 = ((bf16[32,8,1152]{2,1,0:T(8,128)(2,1)}), bf16[32,8,1152]{2,1,0:T(8,128)(2,1)S(1)}, u32[]{:S(2)}, u32[]{:S(2)}) async-start(bf16[32,8,1152]{2,1,0:T(8,128)(2,1)} %fusion.1), calls=%async_computation.2 | async-start | bytes 1179648 | tf_op jit(solution)/shard_map/all_to_all | solution.py:467
  104.3 8.3 %scatter_theirs.1 = bf16[1024,256]{1,0:T(8,128)(2,1)S(1)} custom-call(s32[4]{0:T(128)S(1)} %pad_add_fusion.place_ref, bf16[8,144,256]{2,1,0:T(8,128)(2,1)S(1)} %all-to-all-done.got_ref.rest_0_, bf16[8,144,256]{2,1,0:T(8,128)(2,1)S(1)} %collective-permute-done.9.rest_1_, bf16[8,144,256]{2,1,0:T(8,128)(2,1)} %collective-permute-done.10.rest_2_, ...), custom_call_target="tpu_custom_call" | custom-call | flops 5000000000 | bytes 6000000 | tf_op jit(solution)/shard_map/scatter_theirs/pallas_call | solution.py:272
  112.5 0.2 collective-permute-start.13
  112.8 16.7 %all-to-all-done.2 = bf16[32,8,1152]{2,1,0:T(8,128)(2,1)S(1)} async-done(((bf16[32,8,1152]{2,1,0:T(8,128)(2,1)}), bf16[32,8,1152]{2,1,0:T(8,128)(2,1)S(1)}, u32[]{:S(2)}, u32[]{:S(2)}) %all-to-all-start.2) | async-done | bytes 589856 | tf_op jit(solution)/shard_map/all_to_all | solution.py:467
  129.5 0.1 reduce_sum.12
  129.6 0.9 broadcast_in_dim.5
  130.5 4.3 %all-to-all-start.3 = ((bf16[32,8,1152]{2,1,0:T(8,128)(2,1)}), bf16[32,8,1152]{2,1,0:T(8,128)(2,1)S(1)}, u32[]{:S(2)}, u32[]{:S(2)}) async-start(bf16[32,8,1152]{2,1,0:T(8,128)(2,1)} %broadcast_in_dim.5), calls=%async_computation.3 | async-start | bytes 1179648 | tf_op jit(solution)/shard_map/all_to_all | solution.py:472
  134.8 0.1 pad_add_fusion.1.place_ref
  134.9 1.5 convert_element_type.25
  136.4 9.0 %scatter_mine.1 = f32[1024,256]{1,0:T(8,128)} custom-call(s32[3]{0:T(128)S(1)} %pad_add_fusion.1.place_ref, bf16[8,144,256]{2,1,0:T(8,128)(2,1)S(1)} %all-to-all-done.got_ref.rest_0_, bf16[8,144,256]{2,1,0:T(8,128)(2,1)S(1)} %collective-permute-done.9.rest_1_, bf16[8,144,256]{2,1,0:T(8,128)(2,1)} %collective-permute-done.10.rest_2_, ...), custom_call_target="tpu_custom_call" | custom-call | flops 5000000000 | bytes 6000000 | tf_op jit(solution)/shard_map/scatter_mine/pallas_call | solution.py:272
  145.4 7.8 %all-to-all-done.3 = bf16[32,8,1152]{2,1,0:T(8,128)(2,1)S(1)} async-done(((bf16[32,8,1152]{2,1,0:T(8,128)(2,1)}), bf16[32,8,1152]{2,1,0:T(8,128)(2,1)S(1)}, u32[]{:S(2)}, u32[]{:S(2)}) %all-to-all-start.3) | async-done | bytes 589856 | tf_op jit(solution)/shard_map/all_to_all | solution.py:472
  153.2 2.0 %collective-permute-done.14.other_ref = bf16[256,1152]{1,0:T(8,128)(2,1)S(1)} collective-permute-done((bf16[256,1152]{1,0:T(8,128)(2,1)S(1)}, bf16[256,1152]{1,0:T(8,128)(2,1)S(1)}, u32[]{:S(2)}, u32[]{:S(2)}) %collective-permute-start.14) | collective-permute-done | bytes 589856 | tf_op jit(solution)/shard_map/ppermute | solution.py:417
  155.2 2.2 %unfold.1 = (f32[512,512]{1,0:T(8,128)}, f32[64,256]{1,0:T(8,128)}, f32[1024,256]{1,0:T(8,128)}) custom-call(s32[4]{0:T(128)S(1)} %pad_add_fusion.place_ref, bf16[256,1152]{1,0:T(8,128)(2,1)S(1)} %bitcast.22, bf16[256,1152]{1,0:T(8,128)(2,1)S(1)} %collective-permute-done.14.other_ref), custom_call_target="tpu_custom_call" | custom-call | tf_op jit(solution)/shard_map/unfold/pallas_call | solution.py:370
  (30 shorter events, 0.1 us)
Async XLA Ops:
  8.5 10.7 %collective-permute-start.1 = (f32[128,512]{1,0:T(8,128)S(1)}, f32[128,512]{1,0:T(8,128)S(1)}, u32[]{:S(2)}, u32[]{:S(2)}) collective-permute-start(f32[128,512]{1,0:T(8,128)S(1)} %fusion.2), channel_id=1, source_target_pairs={{0,1},{1,2},{2,3},{3,0},{4,5},{5,6},{6,7},{7,4},{8,9},{9,10},{10,1... | collective-permute-start | bytes 786440 | tf_op jit(solution)/shard_map/ppermute | solution.py:424
  10.2 10.5 %collective-permute-start.2 = (f32[128,512]{1,0:T(8,128)S(1)}, f32[128,512]{1,0:T(8,128)}, u32[]{:S(2)}, u32[]{:S(2)}) collective-permute-start(f32[128,512]{1,0:T(8,128)S(1)} %fusion.2), channel_id=1, source_target_pairs={{0,3},{1,0},{2,1},{3,2},{4,7},{5,4},{6,5},{7,6},{8,11},{9,8},{10,9... | collective-permute-start | bytes 786440 | tf_op jit(solution)/shard_map/ppermute | solution.py:424
  10.9 13.5 %collective-permute-start = (f32[128,512]{1,0:T(8,128)S(1)}, f32[128,512]{1,0:T(8,128)}, u32[]{:S(2)}, u32[]{:S(2)}) collective-permute-start(f32[128,512]{1,0:T(8,128)S(1)} %fusion.2), channel_id=1, source_target_pairs={{0,2},{1,3},{2,0},{3,1},{4,6},{5,7},{6,4},{7,5},{8,10},{9,11},{10,... | collective-permute-start | bytes 786440 | tf_op jit(solution)/shard_map/ppermute | solution.py:424
  14.4 4.4 %copy-start.8 = (s32[128,32]{0,1:T(8,128)S(1)}, s32[128,32]{0,1:T(8,128)}, u32[]{:S(2)}) copy-start(s32[128,32]{0,1:T(8,128)} %param.12) | copy-start | bytes 49156
  14.5 22.0 %collective-permute-start.3 = (bf16[128,2048]{1,0:T(8,128)(2,1)S(1)}, bf16[128,2048]{1,0:T(8,128)(2,1)S(1)}, u32[]{:S(2)}, u32[]{:S(2)}) collective-permute-start(bf16[128,2048]{1,0:T(8,128)(2,1)S(1)} %get-tuple-element.53.rest_0_), channel_id=1, source_target_pairs={{0,32},{4,36},{8,40},{12,44},{16,48},{20,52},{24,56},{28,60},{32,6... | collective-permute-start | bytes 1572872 | tf_op jit(solution)/shard_map/ppermute | solution.py:421
  16.1 24.9 %collective-permute-start.5 = (bf16[128,2048]{1,0:T(8,128)(2,1)S(1)}, bf16[128,2048]{1,0:T(8,128)(2,1)}, u32[]{:S(2)}, u32[]{:S(2)}) collective-permute-start(bf16[128,2048]{1,0:T(8,128)(2,1)S(1)} %get-tuple-element.53.rest_0_), channel_id=1, source_target_pairs={{0,64},{4,68},{8,72},{12,76},{16,80},{20,84},{24,88},{28,92},{32,9... | collective-permute-start | bytes 1572872 | tf_op jit(solution)/shard_map/ppermute | solution.py:421
  19.2 6.3 %copy-start.2 = (bf16[1024,256]{1,0:T(8,128)(2,1)S(1)}, bf16[1024,256]{1,0:T(8,128)(2,1)}, u32[]{:S(2)}) copy-start(bf16[1024,256]{1,0:T(8,128)(2,1)} %second_ref.3) | copy-start | bytes 1572868
  19.2 6.3 %copy-start.6 = (bf16[128,256]{1,0:T(8,128)(2,1)S(1)}, bf16[128,256]{1,0:T(8,128)(2,1)}, u32[]{:S(2)}) copy-start(bf16[128,256]{1,0:T(8,128)(2,1)} %grad_ref.1) | copy-start | bytes 196612
  19.2 6.3 %copy-start.7 = (bf16[64,256]{1,0:T(8,128)(2,1)S(1)}, bf16[64,256]{1,0:T(8,128)(2,1)}, u32[]{:S(2)}) copy-start(bf16[64,256]{1,0:T(8,128)(2,1)} %first_ref.3) | copy-start | bytes 98308
  19.2 21.8 %collective-permute-start.7 = (bf16[128,2048]{1,0:T(8,128)(2,1)S(1)}, bf16[128,2048]{1,0:T(8,128)(2,1)}, u32[]{:S(2)}, u32[]{:S(2)}) collective-permute-start(bf16[128,2048]{1,0:T(8,128)(2,1)S(1)} %get-tuple-element.53.rest_0_), channel_id=1, source_target_pairs={{0,96},{4,100},{8,104},{12,108},{16,112},{20,116},{24,120},{28,124... | collective-permute-start | bytes 1572872 | tf_op jit(solution)/shard_map/ppermute | solution.py:421
  28.0 26.2 %all-to-all-start = ((bf16[8,144,256]{2,1,0:T(8,128)(2,1)}), bf16[8,144,256]{2,1,0:T(8,128)(2,1)S(1)}, u32[]{:S(2)}, u32[]{:S(2)}) async-start(bf16[8,144,256]{2,1,0:T(8,128)(2,1)} %get-tuple-element.32), calls=%async_computation | async-start | bytes 1179648 | tf_op jit(solution)/shard_map/all_to_all | solution.py:445
  36.5 21.9 %collective-permute-start.4 = (bf16[128,2048]{1,0:T(8,128)(2,1)S(1)}, bf16[128,2048]{1,0:T(8,128)(2,1)}, u32[]{:S(2)}, u32[]{:S(2)}) collective-permute-start(bf16[128,2048]{1,0:T(8,128)(2,1)S(1)} %collective-permute-done.3.rest_2_), channel_id=1, source_target_pairs={{0,128},{128,0},{1,129},{129,1},{2,130},{130,2},{3,131},{131,3},{4... | collective-permute-start | bytes 1572872 | tf_op jit(solution)/shard_map/ppermute | solution.py:417
  36.6 0.8 copy-start.4
  41.0 18.9 %collective-permute-start.6 = (bf16[128,2048]{1,0:T(8,128)(2,1)}, bf16[128,2048]{1,0:T(8,128)(2,1)}, u32[]{:S(2)}, u32[]{:S(2)}) collective-permute-start(bf16[128,2048]{1,0:T(8,128)(2,1)} %collective-permute-done.5.rest_4_), channel_id=1, source_target_pairs={{0,128},{128,0},{1,129},{129,1},{2,130},{130,2},{3,131},{131,3},{4... | collective-permute-start | bytes 1572872 | tf_op jit(solution)/shard_map/ppermute | solution.py:417
  41.0 18.9 %collective-permute-start.8 = (bf16[128,2048]{1,0:T(8,128)(2,1)}, bf16[128,2048]{1,0:T(8,128)(2,1)}, u32[]{:S(2)}, u32[]{:S(2)}) collective-permute-start(bf16[128,2048]{1,0:T(8,128)(2,1)} %collective-permute-done.7.rest_6_), channel_id=1, source_target_pairs={{0,128},{128,0},{1,129},{129,1},{2,130},{130,2},{3,131},{131,3},{4... | collective-permute-start | bytes 1572872 | tf_op jit(solution)/shard_map/ppermute | solution.py:417
  54.2 36.9 %collective-permute-start.9 = (bf16[8,144,256]{2,1,0:T(8,128)(2,1)S(1)}, bf16[8,144,256]{2,1,0:T(8,128)(2,1)S(1)}, u32[]{:S(2)}, u32[]{:S(2)}) collective-permute-start(bf16[8,144,256]{2,1,0:T(8,128)(2,1)S(1)} %all-to-all-done.got_ref.rest_0_), channel_id=1, source_target_pairs={{0,32},{4,36},{8,40},{12,44},{16,48},{20,52},{24,56},{28,60},{32,6... | collective-permute-start | bytes 1769480 | tf_op jit(solution)/shard_map/ppermute | solution.py:421
  55.7 35.4 %collective-permute-start.10 = (bf16[8,144,256]{2,1,0:T(8,128)(2,1)S(1)}, bf16[8,144,256]{2,1,0:T(8,128)(2,1)}, u32[]{:S(2)}, u32[]{:S(2)}) collective-permute-start(bf16[8,144,256]{2,1,0:T(8,128)(2,1)S(1)} %all-to-all-done.got_ref.rest_0_), channel_id=1, source_target_pairs={{0,64},{4,68},{8,72},{12,76},{16,80},{20,84},{24,88},{28,92},{32,9... | collective-permute-start | bytes 1769480 | tf_op jit(solution)/shard_map/ppermute | solution.py:421
  58.4 32.6 %collective-permute-start.11 = (bf16[8,144,256]{2,1,0:T(8,128)(2,1)S(1)}, bf16[8,144,256]{2,1,0:T(8,128)(2,1)}, u32[]{:S(2)}, u32[]{:S(2)}) collective-permute-start(bf16[8,144,256]{2,1,0:T(8,128)(2,1)S(1)} %all-to-all-done.got_ref.rest_0_), channel_id=1, source_target_pairs={{0,96},{4,100},{8,104},{12,108},{16,112},{20,116},{24,120},{28,124... | collective-permute-start | bytes 1769480 | tf_op jit(solution)/shard_map/ppermute | solution.py:421
  59.9 1.0 copy-start.5
  60.9 30.2 %copy-start = (bf16[512,512]{1,0:T(8,128)(2,1)S(1)}, bf16[512,512]{1,0:T(8,128)(2,1)}, u32[]{:S(2)}) copy-start(bf16[512,512]{1,0:T(8,128)(2,1)} %qw_ref.1) | copy-start | bytes 1572868
  60.9 30.2 %copy-start.1 = (bf16[128,512]{1,0:T(8,128)(2,1)S(1)}, bf16[128,512]{1,0:T(8,128)(2,1)}, u32[]{:S(2)}) copy-start(bf16[128,512]{1,0:T(8,128)(2,1)} %tokens_ref.1) | copy-start | bytes 393220
  77.2 13.9 %all-to-all-start.1 = ((f32[32,4,256]{2,1,0:T(4,128)}), f32[32,4,256]{2,1,0:T(4,128)S(1)}, u32[]{:S(2)}, u32[]{:S(2)}) async-start(f32[32,4,256]{2,1,0:T(4,128)} %bitcast.7), calls=%async_computation.1 | async-start | bytes 262144 | tf_op jit(solution)/shard_map/all_to_all | solution.py:450
  82.1 52.8 %reduce-scatter.2.cloned.1.call-start = ((), (), s32[]{:S(2)}) async-start(), calls=%async_computation.5 | async-start | bytes 1179648 | tf_op jit(solution)/shard_map/reduce_scatter | solution.py:455
  91.1 1.0 copy-start.3
  96.1 2.2 %collective-permute-start.12 = (bf16[256,1152]{1,0:T(8,128)(2,1)S(1)}, bf16[256,1152]{1,0:T(8,128)(2,1)}, u32[]{:S(2)}, u32[]{:S(2)}) collective-permute-start(bf16[256,1152]{1,0:T(8,128)(2,1)S(1)} %dynamic-slice_bitcast_fusion), channel_id=1, source_target_pairs={{0,128},{128,0},{1,129},{129,1},{2,130},{130,2},{3,131},{131,3},{4... | collective-permute-start | bytes 1769480 | tf_op jit(solution)/shard_map/ppermute | solution.py:417
  100.4 29.1 %all-to-all-start.2 = ((bf16[32,8,1152]{2,1,0:T(8,128)(2,1)}), bf16[32,8,1152]{2,1,0:T(8,128)(2,1)S(1)}, u32[]{:S(2)}, u32[]{:S(2)}) async-start(bf16[32,8,1152]{2,1,0:T(8,128)(2,1)} %fusion.1), calls=%async_computation.2 | async-start | bytes 1179648 | tf_op jit(solution)/shard_map/all_to_all | solution.py:467
  112.5 17.1 %collective-permute-start.13 = (bf16[1024,256]{1,0:T(8,128)(2,1)S(1)}, bf16[1024,256]{1,0:T(8,128)(2,1)S(1)}, u32[]{:S(2)}, u32[]{:S(2)}) collective-permute-start(bf16[1024,256]{1,0:T(8,128)(2,1)S(1)} %scatter_theirs.1), channel_id=1, source_target_pairs={{0,128},{128,0},{1,129},{129,1},{2,130},{130,2},{3,131},{131,3},{4... | collective-permute-start | bytes 1572872 | tf_op jit(solution)/shard_map/ppermute | solution.py:417
  130.5 22.8 %all-to-all-start.3 = ((bf16[32,8,1152]{2,1,0:T(8,128)(2,1)}), bf16[32,8,1152]{2,1,0:T(8,128)(2,1)S(1)}, u32[]{:S(2)}, u32[]{:S(2)}) async-start(bf16[32,8,1152]{2,1,0:T(8,128)(2,1)} %broadcast_in_dim.5), calls=%async_computation.3 | async-start | bytes 1179648 | tf_op jit(solution)/shard_map/all_to_all | solution.py:472
  153.2 2.0 %collective-permute-start.14 = (bf16[256,1152]{1,0:T(8,128)(2,1)S(1)}, bf16[256,1152]{1,0:T(8,128)(2,1)S(1)}, u32[]{:S(2)}, u32[]{:S(2)}) collective-permute-start(bf16[256,1152]{1,0:T(8,128)(2,1)S(1)} %bitcast.21), channel_id=1, source_target_pairs={{0,128},{128,0},{1,129},{129,1},{2,130},{130,2},{3,131},{131,3},{4... | collective-permute-start | bytes 1769480 | tf_op jit(solution)/shard_map/ppermute | solution.py:417
Sparse Core Ops, SparseCore 0:
  96.4 38.4 reduce-scatter.1

commit v3 on v2

--- a/solution.py
+++ b/solution.py
@@ -152,10 +152,10 @@
 
 
 def owner_kernel(place_ref, got_ref, *rest):
-    n_x = (len(rest) - 5) // 2
+    n_x = (len(rest) - 6) // 2
     value_refs = rest[: 2 * n_x]
-    mixed_ref, pick_ref, values, hot, lists = rest[2 * n_x :]
-    cap = pick_ref.shape[2]
+    mixed_ref, pick_ref, values, hot, lists, done = rest[2 * n_x :]
+    cap = 2 * pick_ref.shape[2]
     half = value_refs[0].shape[0]
     rows = value_refs[0].shape[1]
     tok = mixed_ref.shape[0]
@@ -163,9 +163,15 @@
 
     @pl.when(pl.program_id(0) == 0)
     def _():
-        for s in range(n_x):
-            for at, ref in ((dp_at, value_refs[2 * s]), (1 - dp_at, value_refs[2 * s + 1])):
-                values[s, pl.ds(pl.multiple_of(at * half, half), half), :] = ref[...]
+        copies = []
+        for i, ref in enumerate(value_refs):
+            at = pl.multiple_of((dp_at if i % 2 == 0 else 1 - dp_at) * half, half)
+            place = values.at[i // 2, pl.ds(at, half), :]
+            copies.append(pltpu.make_async_copy(ref, place, done.at[i]))
+        for copy in copies:
+            copy.start()
+        for copy in copies:
+            copy.wait()
 
     lists[...] = got_ref[0, tok:, :].astype(F32)
     count = small_iota((256, cap), 0)
@@ -190,7 +196,9 @@
     pick = jnp.sum(picked * spread, axis=0, keepdims=True)
     for s in range(n_x):
         x_own = lax.rem(x_at - s + n_x, n_x)
-        pick_ref[0, pl.ds(x_own, 1), :] = pick[:, s * cap : (s + 1) * cap]
+        for half_at in range(2):
+            at = s * cap + half_at * 128
+            pick_ref[0, pl.ds(2 * x_own + half_at, 1), :] = pick[:, at : at + 128]
     mixed_ref[...] = dot(jnp.where(at_token, weight, zero), picked.astype(BF), NT)
 
 
@@ -205,20 +213,21 @@
             num_scalar_prefetch=1,
             grid=(blocks,),
             in_specs=[pl.BlockSpec((1, tall, cols), lambda b, place: (b, 0, 0))]
-            + [pl.BlockSpec((half, rows), lambda *_: (0, 0), pipeline_mode=pl.Buffered(1))] * (2 * n_x),
+            + [pl.BlockSpec(memory_space=pltpu.HBM)] * (2 * n_x),
             out_specs=[
                 pl.BlockSpec((tok, cols), lambda b, place: (b, 0)),
-                pl.BlockSpec((1, n_x, cap), lambda b, place: (b, 0, 0)),
+                pl.BlockSpec((1, 2 * n_x, cap // 2), lambda b, place: (b, 0, 0)),
             ],
             scratch_shapes=[
                 pltpu.VMEM((n_x, cols, rows), BF),
                 pltpu.VMEM((n_x, rows, cap), BF),
                 pltpu.VMEM((4 * n_x, cap), F32),
+                pltpu.SemaphoreType.DMA((2 * n_x,)),
             ],
         ),
         out_shape=(
             jax.ShapeDtypeStruct((blocks * tok, cols), F32),
-            jax.ShapeDtypeStruct((blocks, n_x, cap), F32),
+            jax.ShapeDtypeStruct((blocks, 2 * n_x, cap // 2), F32),
         ),
         compiler_params=pltpu.CompilerParams(vmem_limit_bytes=20 * MIB),
         cost_estimate=pl.CostEstimate(flops=12_000_000_000, bytes_accessed=10_000_000, transcendentals=0),
@@ -226,78 +235,74 @@
     )(place, got, *value_halves)
 
 
-def scatter_kernel(n_x, place_ref, *rest):
-    got_refs = rest[:n_x]
-    out_ref, hot, spread, lists = rest[-4:]
-    blocks, tall, cols = got_refs[0].shape
-    kinds = lists.shape[1]
-    cap = spread.shape[1] // (n_x * blocks)
-    tok = tall - kinds
+def scatter_kernel(n_after, place_ref, got_ref, *rest):
+    come_refs, (out_ref, hot, spread, lists) = rest[n_after:-4], rest[-4:]
+    blocks, kinds, cap = lists.shape
+    tok = got_ref.shape[1] - kinds
     x_own = place_ref[0]
     one, zero = jnp.ones((), BF), jnp.zeros((), BF)
 
     @pl.when(pl.program_id(0) == 0)
     def _():
         at_token = small_iota((tok, cap), 0)
-        for s in range(n_x):
-            for b in range(blocks):
-                at = s * blocks + b
-                lists[at] = got_refs[s][b, tok:, :].astype(F32)
-                token = listed(lists.at[at], x_own, 3).astype(BF)
-                spread[:, at * cap : (at + 1) * cap] = dot(
-                    got_refs[s][b, :tok, :], jnp.where(at_token == token, one, zero), TN
-                ).astype(BF)
+        for at in range(blocks):
+            lists[at] = got_ref[at, tok:, :].astype(F32)
+            token = listed(lists.at[at], x_own, 3).astype(BF)
+            spread[:, at * cap : (at + 1) * cap] = dot(
+                got_ref[at, :tok, :], jnp.where(at_token == token, one, zero), TN
+            ).astype(BF)
 
     chunk = (place_ref[2] * pl.num_programs(0) + pl.program_id(0)).astype(F32)
     count = small_iota((256, cap), 0)
-    for at in range(n_x * blocks):
+    for at in range(blocks):
         weight = listed(lists.at[at], x_own, 0).astype(BF)
         high, low = listed(lists.at[at], x_own, 1), listed(lists.at[at], x_own, 2)
         here = jnp.where(high == chunk, low, -1.0).astype(BF)
         hot[:, at * cap : (at + 1) * cap] = jnp.where(count == here, weight, zero)
     total = dot(hot[...], spread[...], NT)
-    if len(rest) > n_x + 4:
-        total = total + rest[n_x][...].astype(F32)
+    for come_ref in come_refs:
+        total = total + come_ref[...]
     out_ref[...] = total.astype(out_ref.dtype)
 
 
-def scatter(place, gots, rows, kind, come=()):
-    n_x = len(gots)
-    blocks, tall, cols = gots[0].shape
+def scatter(place, got, after, rows, n_x, come=()):
+    blocks, tall, cols = got.shape
     cap = cols
-    tok = tall - 4 * n_x
     half = rows // 2
     each = pl.BlockSpec((256, cols), lambda r, place: (r, 0))
-    fixed = pl.BlockSpec(gots[0].shape, lambda r, place: (0, 0, 0), pipeline_mode=pl.Buffered(1))
+    fixed = pl.BlockSpec(got.shape, lambda r, place: (0, 0, 0), pipeline_mode=pl.Buffered(1))
     return pl.pallas_call(
-        functools.partial(scatter_kernel, n_x),
+        functools.partial(scatter_kernel, len(after)),
         grid_spec=pltpu.PrefetchScalarGridSpec(
             num_scalar_prefetch=1,
             grid=(half // 256,),
-            in_specs=[fixed] * n_x + [each] * len(come),
+            in_specs=[fixed] + [pl.BlockSpec(memory_space=pl.ANY)] * len(after) + [each] * len(come),
             out_specs=each,
             scratch_shapes=[
-                pltpu.VMEM((256, n_x * blocks * cap), BF),
-                pltpu.VMEM((cols, n_x * blocks * cap), BF),
-                pltpu.VMEM((n_x * blocks, 4 * n_x, cap), F32),
+                pltpu.VMEM((256, blocks * cap), BF),
+                pltpu.VMEM((cols, blocks * cap), BF),
+                pltpu.VMEM((blocks, 4 * n_x, cap), F32),
             ],
         ),
-        out_shape=jax.ShapeDtypeStruct((half, cols), kind),
+        out_shape=jax.ShapeDtypeStruct((half, cols), F32),
         compiler_params=pltpu.CompilerParams(vmem_limit_bytes=16 * MIB),
         cost_estimate=pl.CostEstimate(flops=5_000_000_000, bytes_accessed=6_000_000, transcendentals=0),
         name="scatter_mine" if come else "scatter_theirs",
-    )(place, *gots, *come)
+    )(place, got, *after, *come)
 
 
 def grads_kernel(
-    row_dev, n_z, parts_ref, rank_ref, picks_ref, weight_ref, query_ref, first_ref, second_ref,
-    qw_ref, tokens_ref, token_grad_ref, part_ref, slots, sums, grad_b,
+    row_dev, n_z, place_ref, parts_ref, rank_ref, picks_ref, weight_ref, query_ref, first_ref, second_ref,
+    qw_ref, tokens_ref, token_grad_ref, mine_ref, theirs_ref, slots, sums, grad_b, halves,
 ):
     topk, tok = picks_ref.shape
     half = first_ref.shape[1]
     na, nb = first_ref.shape[0], second_ref.shape[0]
-    n_row, cap = parts_ref.shape[0] * parts_ref.shape[2], parts_ref.shape[3]
-    by_slot = jnp.sum(parts_ref[...], axis=1).reshape(n_row, cap)
+    n_row, cap = parts_ref.shape[0] * parts_ref.shape[2] // 2, 2 * parts_ref.shape[3]
+    halves[...] = jnp.sum(parts_ref[...], axis=1).reshape(2 * n_row, cap // 2)
+    by_slot = jnp.concatenate(
+        [halves[pl.ds(0, n_row, stride=2), :], halves[pl.ds(1, n_row, stride=2), :]], axis=1
+    )
     one = by_slot.astype(BF)
     rest = by_slot - one.astype(F32)
     two = rest.astype(BF)
@@ -341,16 +346,47 @@
         [dot(grad_a, first_ref[...], TN), dot(grad_b[...], second_ref[...], TN)], axis=1
     ).astype(BF)
     token_grad_ref[...] = dot(query_grad, qw_ref[...], NT).astype(BF)
-    qw_part = dot(query_grad, tokens_ref[...], TN).astype(BF)
-    first_part = dot(query[:, :half], grad_a, (((0,), (1,)), ((), ()))).astype(BF)
-    second_part = dot(query[:, half:], grad_b[...], (((0,), (1,)), ((), ()))).astype(BF)
     n_qw = tokens_ref.shape[1]
+    at_second, end = n_qw + nb // 2, n_qw + (nb + na) // 2
+    query_a, query_b = query[:, :half], query[:, half:]
+    parts = []
     for h in range(2):
-        part_ref[h, :, :n_qw] = qw_part[h * half : (h + 1) * half]
-        part_ref[h, :, n_qw : n_qw + nb // 2] = second_part[:, h * (nb // 2) : (h + 1) * (nb // 2)]
-        end = n_qw + (nb + na) // 2
-        part_ref[h, :, n_qw + nb // 2 : end] = first_part[:, h * (na // 2) : (h + 1) * (na // 2)]
-        part_ref[h, :, end:] = jnp.zeros((half, part_ref.shape[2] - end), BF)
+        qw_part = dot(query_grad[:, h * half : (h + 1) * half], tokens_ref[...], TN)
+        own_b = slice(h * (nb // 2), (h + 1) * (nb // 2))
+        second_part = dot(query_b, grad_b[own_b, :], (((0,), (1,)), ((), ())))
+        first_part = dot(query_a, grad_a[h * (na // 2) : (h + 1) * (na // 2)], (((0,), (1,)), ((), ())))
+        rest = jnp.zeros((half, mine_ref.shape[1] - end), F32)
+        parts.append(jnp.concatenate([qw_part, second_part, first_part, rest], axis=1))
+    swap = place_ref[1] == 1
+    mine_ref[...] = jnp.where(swap, parts[1], parts[0])
+    theirs_ref[...] = jnp.where(swap, parts[0], parts[1]).astype(theirs_ref.dtype)
+
+
+def grads(place, parts, rank, picks_t, weight, query, keys_first, keys_second, qw, tokens, row_dev, n_z):
+    topk, tok = picks_t.shape
+    cap = 2 * parts.shape[3]
+    n_row = parts.shape[0] * parts.shape[2] // 2
+    na, half = keys_first.shape
+    nb = keys_second.shape[0]
+    folded = (half, -(-(qw.shape[0] + (na + nb) // 2) // 128) * 128)
+    return pl.pallas_call(
+        functools.partial(grads_kernel, row_dev, n_z),
+        in_specs=[pl.BlockSpec(memory_space=pltpu.SMEM)] + [pl.BlockSpec(memory_space=pltpu.VMEM)] * 9,
+        out_shape=(
+            jax.ShapeDtypeStruct(tokens.shape, BF),
+            jax.ShapeDtypeStruct(folded, F32),
+            jax.ShapeDtypeStruct(folded, BF),
+        ),
+        scratch_shapes=[
+            pltpu.VMEM((cap, topk * tok), BF),
+            pltpu.VMEM((3 * n_row, topk * tok), F32),
+            pltpu.VMEM((nb, tok), BF),
+            pltpu.VMEM((2 * n_row, cap // 2), F32),
+        ],
+        compiler_params=pltpu.CompilerParams(vmem_limit_bytes=16 * MIB),
+        cost_estimate=pl.CostEstimate(flops=4_000_000_000, bytes_accessed=4_000_000, transcendentals=0),
+        name="grads",
+    )(place, parts, rank, picks_t, weight, query, keys_first, keys_second, qw, tokens)
 
 
 def unfold_kernel(place_ref, mine_ref, other_ref, qw_ref, first_ref, second_ref):
@@ -374,29 +410,6 @@
         compiler_params=pltpu.CompilerParams(vmem_limit_bytes=12 * MIB),
         name="unfold",
     )(place, mine, other)
-
-
-def grads(parts, rank, picks_t, weight, query, keys_first, keys_second, qw, tokens, row_dev, n_z):
-    topk, tok = picks_t.shape
-    cap = parts.shape[3]
-    n_row = parts.shape[0] * parts.shape[2]
-    na, half = keys_first.shape
-    nb = keys_second.shape[0]
-    return pl.pallas_call(
-        functools.partial(grads_kernel, row_dev, n_z),
-        out_shape=(
-            jax.ShapeDtypeStruct(tokens.shape, BF),
-            jax.ShapeDtypeStruct((2, half, -(-(qw.shape[0] + (na + nb) // 2) // 128) * 128), BF),
-        ),
-        scratch_shapes=[
-            pltpu.VMEM((cap, topk * tok), BF),
-            pltpu.VMEM((3 * n_row, topk * tok), F32),
-            pltpu.VMEM((nb, tok), BF),
-        ],
-        compiler_params=pltpu.CompilerParams(vmem_limit_bytes=16 * MIB),
-        cost_estimate=pl.CostEstimate(flops=4_000_000_000, bytes_accessed=4_000_000, transcendentals=0),
-        name="grads",
-    )(parts, rank, picks_t, weight, query, keys_first, keys_second, qw, tokens)
 
 
 def body(tokens, query_weight, keys_first, keys_second, values, picks, out_grad):
@@ -411,6 +424,7 @@
     row_at, dp_at = lax.axis_index("row"), lax.axis_index("dp")
     place = jnp.stack([row_at // n_z, dp_at, 1 - dp_at, row_at % n_z]).astype(I32)
     rings = [[x * n_z + z for z in range(n_z)] for x in range(n_x)]
+    columns = [[x * n_z + z for x in range(n_x)] for z in range(n_z)]
     planes = [[r * n_dim + m for r in ring for m in range(n_dim)] for ring in rings]
 
     def other_core(array):
@@ -444,34 +458,33 @@
     )
     got = lax.all_to_all(sent, "row", 0, 0, tiled=True, axis_index_groups=rings)
 
+    corners = [part[:8, :128] for part in value_halves[3::2]]
+    late, corners = lax.optimization_barrier((got, corners))
+    got_x = lax.all_gather(late, "row", tiled=True, axis_index_groups=columns)
     mixed_part, pick_part = owner_side(place, got, value_halves, cap)
-    gots = [got] + [along_x(got, s) for s in range(1, n_x)]
-    pick_sent = jnp.broadcast_to(pick_part[:, None], (n_z, n_dim, n_x, cap))
+    pick_sent = jnp.broadcast_to(pick_part[:, None], (n_z, n_dim) + pick_part.shape[1:])
     pick_parts = lax.all_to_all(
-        pick_sent.reshape(n_z * n_dim, n_x, cap), ("row", "dim"), 0, 0, tiled=True,
+        pick_sent.reshape((n_z * n_dim,) + pick_part.shape[1:]), ("row", "dim"), 0, 0, tiled=True,
         axis_index_groups=planes,
-    ).reshape(n_z, n_dim, n_x, cap)
+    ).reshape(pick_sent.shape)
 
     mixed = lax.psum_scatter(
         mixed_part, "row", tiled=True, axis_index_groups=rings
     ).astype(BF)
-    pick_parts, gots = lax.optimization_barrier((pick_parts, gots))
-    token_grad, sums = grads(
-        pick_parts, rank, picks_t, weight, query, keys_first, keys_second, query_weight, tokens,
+    token_grad, mine, theirs = grads(
+        place, pick_parts, rank, picks_t, weight, query, keys_first, keys_second, query_weight, tokens,
         row_dev, n_z,
     )
-    theirs = lax.dynamic_index_in_dim(sums, 1 - dp_at, 0, keepdims=False)
-    mine = lax.dynamic_index_in_dim(sums, dp_at, 0, keepdims=False)
-    mine = (mine.astype(F32) + other_core(theirs).astype(F32)).astype(BF)
+    mine = (mine + other_core(theirs).astype(F32)).astype(BF)
     shape = (n_row, half // n_row, mine.shape[1])
     received = lax.all_to_all(mine.reshape(shape), "row", 0, 0, tiled=True)
     summed = jnp.sum(received.astype(F32), axis=0).astype(BF)
-    come = other_core(scatter(place, gots, row_dev, BF))
+    come = other_core(scatter(place, got_x, corners, row_dev, n_x))
     summed, come = lax.optimization_barrier((summed, come))
     summed = jnp.broadcast_to(summed[None], shape)
     mine = lax.all_to_all(summed, "row", 0, 0, tiled=True).reshape(mine.shape)
     own_place = jnp.stack([row_at // n_z, dp_at, dp_at]).astype(I32)
-    value_grad = scatter(own_place, gots, row_dev, F32, (come,))
+    value_grad = scatter(own_place, got_x, corners, row_dev, n_x, (come,))
     mine, mixed, value_grad = lax.optimization_barrier((mine, mixed, value_grad))
     other = other_core(mine)
     qw_grad, first_grad, second_grad = unfold(

time: 167 us -> 160 us (0.958)
  blocking collectives: 0 us -> 12.7 us
  waiting for transfers between devices: 57.4 us -> 46.6 us
  starting transfers between devices: 38.4 us -> 31.2 us
  Pallas kernels: 41.8 us -> 39.3 us
  other arithmetic: 4.92 us -> 2.81 us
    all_to_all x0 -> x1, blocking collectives: none -> 12.7 us  [body(): lax.all_to_all(pick_sent.reshape((n_z * n_dim,) + pick_part.shape[1:]), (...]
    all_to_all x1 -> x0, waiting for transfers between devices: 8.92 us -> none  [body(): lax.all_to_all(pick_sent.reshape(n_z * n_dim, n_x, cap), ('row', 'dim'),...]
    ppermute x6 -> x3, starting transfers between devices: 11.5 us -> 5.81 us  [along_x(): return lax.ppermute(array, 'row', pairs)]
    all_to_all x1 -> x0, starting transfers between devices: 4.9 us -> none  [body(): lax.all_to_all(pick_sent.reshape(n_z * n_dim, n_x, cap), ('row', 'dim'),...]
    all_to_all x1, waiting for transfers between devices: 12.6 us -> 9.35 us  [body(): got = lax.all_to_all(sent, 'row', 0, 0, tiled=True, axis_index_groups=rings)]
    unnamed x18 -> x22, local copies, waits for them, and re-layouts: 2.9 us -> 5.24 us
    all_to_all x1, waiting for transfers between devices: 16.7 us -> 14.5 us  [body(): received = lax.all_to_all(mine.reshape(shape), 'row', 0, 0, tiled=True)]
    ppermute x6, waiting for transfers between devices: 4.11 us -> 6.33 us  [other_core(): return lax.ppermute(array, 'dp', [(0, 1), (1, 0)])]
  transfers between devices with their start and end apart: 20 -> 17, of which waited for: 8 -> 10; matrix products, arithmetic and copies ran while one was open for 5% -> 3% of each run, Pallas kernels for 22% -> 24%
where the time goes in v3:
time: 160 us; the launch traced here: 157 us
  waiting for transfers between devices  46.6 us (29%)
  Pallas kernels  39.3 us (25%)
  starting transfers between devices  31.2 us (20%)
  between operations  15.7 us (10%)
  blocking collectives  12.7 us (8%)
  local copies, waits for them, and re-layouts  7.7 us (5%)
  other arithmetic  2.81 us (2%)
    pallas_call x1, Pallas kernels, owner_side(): pl.pallas_call(owner_kernel, grid_spec=pltpu.PrefetchScalarGridSpec(num_s...  15.1 us
    pallas_call x2, Pallas kernels, scatter(): pl.pallas_call(functools.partial(scatter_kernel, len(after)), grid_spec=p...  14.8 us
    all_to_all x1, waiting for transfers between devices, body(): received = lax.all_to_all(mine.reshape(shape), 'row', 0, 0, tiled=True)  14.5 us
    all_to_all x1, blocking collectives, body(): lax.all_to_all(pick_sent.reshape((n_z * n_dim,) + pick_part.shape[1:]), (...  12.7 us
    all_to_all x1, waiting for transfers between devices, body(): got = lax.all_to_all(sent, 'row', 0, 0, tiled=True, axis_index_groups=rings)  9.35 us
    all_to_all x1, starting transfers between devices, body(): got = lax.all_to_all(sent, 'row', 0, 0, tiled=True, axis_index_groups=rings)  8.46 us
    ppermute x6, waiting for transfers between devices, other_core(): return lax.ppermute(array, 'dp', [(0, 1), (1, 0)])  6.33 us
    all_to_all x1, starting transfers between devices, body(): mine = lax.all_to_all(summed, 'row', 0, 0, tiled=True).reshape(mine.shape)  6.03 us
  transfers between devices with their start and end apart: 17, of which 10 were waited for; matrix products, arithmetic and copies ran while one was open for 3% of the time, Pallas kernels for 24%

profile of v3, /device:TPU:8, one launch (start us, length us, event | category | flops | bytes accessed | tf_op | source)
XLA Modules:
  0.0 157.4 jit_solution(17016730940894152182)
XLA Ops:
  8.0 1.3 fusion.1
  9.3 1.7 %collective-permute-start.1 = (f32[128,512]{1,0:T(8,128)S(1)}, f32[128,512]{1,0:T(8,128)S(1)}, u32[]{:S(2)}, u32[]{:S(2)}) collective-permute-start(f32[128,512]{1,0:T(8,128)S(1)} %fusion.1), channel_id=1, source_target_pairs={{0,1},{1,2},{2,3},{3,0},{4,5},{5,6},{6,7},{7,4},{8,9},{9,10},{10,1... | collective-permute-start | bytes 786440 | tf_op jit(solution)/shard_map/ppermute | solution.py:438
  11.0 0.7 collective-permute-start.2
  11.7 2.0 %collective-permute-start = (f32[128,512]{1,0:T(8,128)S(1)}, f32[128,512]{1,0:T(8,128)S(1)}, u32[]{:S(2)}, u32[]{:S(2)}) collective-permute-start(f32[128,512]{1,0:T(8,128)S(1)} %fusion.1), channel_id=1, source_target_pairs={{0,2},{1,3},{2,0},{3,1},{4,6},{5,7},{6,4},{7,5},{8,10},{9,11},{10,... | collective-permute-start | bytes 786440 | tf_op jit(solution)/shard_map/ppermute | solution.py:438
  13.7 1.5 copy.15
  15.2 0.1 dynamic-slice_bitcast_fusion
  15.4 1.6 collective-permute-start.3
  16.9 2.7 %collective-permute-start.5 = (bf16[128,2048]{1,0:T(8,128)(2,1)S(1)}, bf16[128,2048]{1,0:T(8,128)(2,1)}, u32[]{:S(2)}, u32[]{:S(2)}) collective-permute-start(bf16[128,2048]{1,0:T(8,128)(2,1)S(1)} %get-tuple-element.53.rest_0_), channel_id=1, source_target_pairs={{0,64},{4,68},{8,72},{12,76},{16,80},{20,84},{24,88},{28,92},{32,9... | collective-permute-start | bytes 1572872 | tf_op jit(solution)/shard_map/ppermute | solution.py:435
  19.7 0.3 place_picks.1.rank_ref
  20.0 1.5 collective-permute-start.7
  21.6 3.6 %collective-permute-done = f32[128,512]{1,0:T(8,128)S(1)} collective-permute-done((f32[128,512]{1,0:T(8,128)S(1)}, f32[128,512]{1,0:T(8,128)S(1)}, u32[]{:S(2)}, u32[]{:S(2)}) %collective-permute-start) | collective-permute-done | bytes 262176 | tf_op jit(solution)/shard_map/ppermute | solution.py:438
  25.1 0.1 add_convert_fusion.1.query_ref
  25.2 2.5 %weigh.1 = (bf16[8,144,256]{2,1,0:T(8,128)(2,1)}, f32[32,128]{1,0:T(8,128)S(1)}) custom-call(bf16[128,512]{1,0:T(8,128)(2,1)S(1)} %add_convert_fusion.1.query_ref, bf16[64,256]{1,0:T(8,128)(2,1)S(1)} %copy-done.9, bf16[1024,256]{1,0:T(8,128)(2,1)S(1)} %copy-done.6, s32[32,128]{1,0:T(8,128)S(1)} %bitcast.20, s32[32,128]{1,0:T(8,128)S(1)} %place_picks.1.rank_ref, ...), custom_call_target="tpu_custom_call" | custom-call | flops 4000000000 | bytes 1000000 | tf_op jit(solution)/shard_map/weigh/pallas_call | solution.py:132
  27.8 8.5 %all-to-all-start = ((bf16[8,144,256]{2,1,0:T(8,128)(2,1)}), bf16[8,144,256]{2,1,0:T(8,128)(2,1)S(1)}, u32[]{:S(2)}, u32[]{:S(2)}) async-start(bf16[8,144,256]{2,1,0:T(8,128)(2,1)} %get-tuple-element.32), calls=%async_computation | async-start | bytes 1179648 | tf_op jit(solution)/shard_map/all_to_all | solution.py:459
  36.2 0.0 all-gather.2.cloned.1.call-start
  36.3 0.1 collective-permute-start.4
  36.4 5.4 %collective-permute-done.5.rest_4_ = bf16[128,2048]{1,0:T(8,128)(2,1)} collective-permute-done((bf16[128,2048]{1,0:T(8,128)(2,1)S(1)}, bf16[128,2048]{1,0:T(8,128)(2,1)}, u32[]{:S(2)}, u32[]{:S(2)}) %collective-permute-start.5) | collective-permute-done | bytes 524320 | tf_op jit(solution)/shard_map/ppermute | solution.py:435
  41.8 0.5 collective-permute-start.8
  42.3 1.6 %collective-permute-done.6.rest_5_ = bf16[128,2048]{1,0:T(8,128)(2,1)S(1)} collective-permute-done((bf16[128,2048]{1,0:T(8,128)(2,1)}, bf16[128,2048]{1,0:T(8,128)(2,1)S(1)}, u32[]{:S(2)}, u32[]{:S(2)}) %collective-permute-start.6) | collective-permute-done | bytes 524320 | tf_op jit(solution)/shard_map/ppermute | solution.py:431
  43.9 0.7 collective-permute-done.8.rest_7_
  44.7 9.4 %all-to-all-done.got_ref = bf16[8,144,256]{2,1,0:T(8,128)(2,1)S(1)} async-done(((bf16[8,144,256]{2,1,0:T(8,128)(2,1)}), bf16[8,144,256]{2,1,0:T(8,128)(2,1)S(1)}, u32[]{:S(2)}, u32[]{:S(2)}) %all-to-all-start) | async-done | bytes 589856 | tf_op jit(solution)/shard_map/all_to_all | solution.py:459
  54.0 0.8 copy-done
  54.9 0.0 reduce-scatter.2.cloned.1.call-start
  54.9 0.1 pad_add_fusion.place_ref
  55.0 1.1 copy-done.1
  56.1 15.1 %owner_side.1 = (f32[1024,256]{1,0:T(8,128)}, f32[8,8,128]{2,1,0:T(8,128)S(1)}) custom-call(s32[4]{0:T(128)S(1)} %pad_add_fusion.place_ref, bf16[8,144,256]{2,1,0:T(8,128)(2,1)S(1)} %copy-done.1, bf16[128,2048]{1,0:T(8,128)(2,1)S(1)} %get-tuple-element.53.rest_0_, bf16[128,2048]{1,0:T(8,128)(2,1)S(1)} %get-tuple-element.52.rest_1_, ...), custom_call_target="tpu_custom_call" | custom-call | flops 12000000000 | bytes 10000000 | tf_op jit(solution)/shard_map/owner_side/pallas_call | solution.py:210
  71.2 12.7 %all_to_all.20 = f32[32,8,128]{2,1,0:T(8,128)S(1)} all-to-all(f32[32,8,128]{2,1,0:T(8,128)S(1)} %bitcast.22), channel_id=1, replica_groups={{0,1,2,3,4,5,6,7,8,9,10,11,12,13,14,15,16,17,18,19,20,21,22,23,24,25,26..., dimensions={0} | all-to-all | bytes 262144 | tf_op jit(solution)/shard_map/all_to_all | solution.py:466
  83.9 4.4 %grads.1 = (bf16[128,512]{1,0:T(8,128)(2,1)}, f32[256,1152]{1,0:T(8,128)S(1)}, bf16[256,1152]{1,0:T(8,128)(2,1)S(1)}) custom-call(s32[4]{0:T(128)S(1)} %pad_add_fusion.place_ref, f32[8,4,8,128]{3,2,1,0:T(8,128)S(1)} %bitcast.18, s32[32,128]{1,0:T(8,128)S(1)} %place_picks.1.rank_ref, s32[32,128]{1,0:T(8,128)S(1)} %bitcast.21, ...), custom_call_target="tpu_custom_call" | custom-call | flops 4000000000 | bytes 4000000 | tf_op jit(solution)/shard_map/grads/pallas_call | solution.py:372
  88.3 0.0 reduce-scatter.2.cloned.1.call-update
  88.3 2.0 %collective-permute-done.9 = bf16[256,1152]{1,0:T(8,128)(2,1)S(1)} collective-permute-done((bf16[256,1152]{1,0:T(8,128)(2,1)S(1)}, bf16[256,1152]{1,0:T(8,128)(2,1)S(1)}, u32[]{:S(2)}, u32[]{:S(2)}) %collective-permute-start.9) | collective-permute-done | bytes 589856 | tf_op jit(solution)/shard_map/ppermute | solution.py:431
  90.3 0.9 fusion
  91.2 5.7 %all-to-all-start.2 = ((bf16[32,8,1152]{2,1,0:T(8,128)(2,1)}), bf16[32,8,1152]{2,1,0:T(8,128)(2,1)S(1)}, u32[]{:S(2)}, u32[]{:S(2)}) async-start(bf16[32,8,1152]{2,1,0:T(8,128)(2,1)} %fusion), calls=%async_computation.2 | async-start | bytes 1179648 | tf_op jit(solution)/shard_map/all_to_all | solution.py:480
  97.0 0.0 all-gather.2.cloned.1.call-done.got_ref
  97.0 1.7 %copy-done.4 = bf16[32,144,256]{2,1,0:T(8,128)(2,1)S(1)} copy-done((bf16[32,144,256]{2,1,0:T(8,128)(2,1)S(1)}, bf16[32,144,256]{2,1,0:T(8,128)(2,1)}, u32[]{:S(2)}) %copy-start.4) | copy-done | bytes 2359320
  98.7 7.0 %scatter_theirs.1 = f32[1024,256]{1,0:T(8,128)S(1)} custom-call(s32[4]{0:T(128)S(1)} %pad_add_fusion.place_ref, bf16[32,144,256]{2,1,0:T(8,128)(2,1)S(1)} %copy-done.4, bf16[8,128]{1,0:T(8,128)(2,1)S(1)} %slice.12.rest_0_, bf16[8,128]{1,0:T(8,128)(2,1)S(1)} %slice.13.rest_1_, bf16[8,128]{1,0:T(8,128)(2,1)S(1)} %slice.14.rest_2_), custom_call_target="tpu_custom_call" | custom-call | flops 5000000000 | bytes 6000000 | tf_op jit(solution)/shard_map/scatter_theirs/pallas_call | solution.py:274
  105.7 0.1 collective-permute-start.10
  105.8 14.5 %all-to-all-done.2 = bf16[32,8,1152]{2,1,0:T(8,128)(2,1)S(1)} async-done(((bf16[32,8,1152]{2,1,0:T(8,128)(2,1)}), bf16[32,8,1152]{2,1,0:T(8,128)(2,1)S(1)}, u32[]{:S(2)}, u32[]{:S(2)}) %all-to-all-start.2) | async-done | bytes 589856 | tf_op jit(solution)/shard_map/all_to_all | solution.py:480
  120.3 0.1 reduce_sum.12
  120.4 0.9 broadcast_in_dim.5
  121.3 6.0 %all-to-all-start.3 = ((bf16[32,8,1152]{2,1,0:T(8,128)(2,1)}), bf16[32,8,1152]{2,1,0:T(8,128)(2,1)S(1)}, u32[]{:S(2)}, u32[]{:S(2)}) async-start(bf16[32,8,1152]{2,1,0:T(8,128)(2,1)} %broadcast_in_dim.5), calls=%async_computation.3 | async-start | bytes 1179648 | tf_op jit(solution)/shard_map/all_to_all | solution.py:485
  127.3 0.1 pad_add_fusion.1.place_ref
  127.4 1.6 %reduce-scatter.2.cloned.1.call-done = f32[128,256]{1,0:T(8,128)} async-done(((f32[1024,256]{1,0:T(8,128)}), f32[128,256]{1,0:T(8,128)}) %reduce-scatter.2.cloned.1.call-update) | async-done | bytes 131088 | tf_op jit(solution)/shard_map/reduce_scatter | solution.py:471
  129.0 1.5 convert_element_type.17
  130.6 1.7 %copy-done.5 = bf16[32,144,256]{2,1,0:T(8,128)(2,1)S(1)} copy-done((bf16[32,144,256]{2,1,0:T(8,128)(2,1)S(1)}, bf16[32,144,256]{2,1,0:T(8,128)(2,1)}, u32[]{:S(2)}) %copy-start.5) | copy-done | bytes 2359320
  132.2 7.8 %scatter_mine.1 = f32[1024,256]{1,0:T(8,128)} custom-call(s32[3]{0:T(128)S(1)} %pad_add_fusion.1.place_ref, bf16[32,144,256]{2,1,0:T(8,128)(2,1)S(1)} %copy-done.5, bf16[8,128]{1,0:T(8,128)(2,1)S(1)} %slice.12.rest_0_, bf16[8,128]{1,0:T(8,128)(2,1)S(1)} %slice.13.rest_1_, bf16[8,128]{1,0:T(8,128)(2,1)S(1)} %slice.14.rest_2_, ...), custom_call_target="tpu_custom_call" | custom-call | flops 5000000000 | bytes 6000000 | tf_op jit(solution)/shard_map/scatter_mine/pallas_call | solution.py:274
  140.0 5.8 %all-to-all-done.3 = bf16[32,8,1152]{2,1,0:T(8,128)(2,1)S(1)} async-done(((bf16[32,8,1152]{2,1,0:T(8,128)(2,1)}), bf16[32,8,1152]{2,1,0:T(8,128)(2,1)S(1)}, u32[]{:S(2)}, u32[]{:S(2)}) %all-to-all-start.3) | async-done | bytes 589856 | tf_op jit(solution)/shard_map/all_to_all | solution.py:485
  145.8 2.0 %collective-permute-done.11.other_ref = bf16[256,1152]{1,0:T(8,128)(2,1)S(1)} collective-permute-done((bf16[256,1152]{1,0:T(8,128)(2,1)S(1)}, bf16[256,1152]{1,0:T(8,128)(2,1)S(1)}, u32[]{:S(2)}, u32[]{:S(2)}) %collective-permute-start.11) | collective-permute-done | bytes 589856 | tf_op jit(solution)/shard_map/ppermute | solution.py:431
  147.8 2.2 %unfold.1 = (f32[512,512]{1,0:T(8,128)}, f32[64,256]{1,0:T(8,128)}, f32[1024,256]{1,0:T(8,128)}) custom-call(s32[4]{0:T(128)S(1)} %pad_add_fusion.place_ref, bf16[256,1152]{1,0:T(8,128)(2,1)S(1)} %bitcast.17, bf16[256,1152]{1,0:T(8,128)(2,1)S(1)} %collective-permute-done.11.other_ref), custom_call_target="tpu_custom_call" | custom-call | tf_op jit(solution)/shard_map/unfold/pallas_call | solution.py:406
  (32 shorter events, 0.1 us)
Async XLA Ops:
  9.3 10.7 %collective-permute-start.1 = (f32[128,512]{1,0:T(8,128)S(1)}, f32[128,512]{1,0:T(8,128)S(1)}, u32[]{:S(2)}, u32[]{:S(2)}) collective-permute-start(f32[128,512]{1,0:T(8,128)S(1)} %fusion.1), channel_id=1, source_target_pairs={{0,1},{1,2},{2,3},{3,0},{4,5},{5,6},{6,7},{7,4},{8,9},{9,10},{10,1... | collective-permute-start | bytes 786440 | tf_op jit(solution)/shard_map/ppermute | solution.py:438
  11.0 10.6 %collective-permute-start.2 = (f32[128,512]{1,0:T(8,128)S(1)}, f32[128,512]{1,0:T(8,128)S(1)}, u32[]{:S(2)}, u32[]{:S(2)}) collective-permute-start(f32[128,512]{1,0:T(8,128)S(1)} %fusion.1), channel_id=1, source_target_pairs={{0,3},{1,0},{2,1},{3,2},{4,7},{5,4},{6,5},{7,6},{8,11},{9,8},{10,9... | collective-permute-start | bytes 786440 | tf_op jit(solution)/shard_map/ppermute | solution.py:438
  11.7 13.4 %collective-permute-start = (f32[128,512]{1,0:T(8,128)S(1)}, f32[128,512]{1,0:T(8,128)S(1)}, u32[]{:S(2)}, u32[]{:S(2)}) collective-permute-start(f32[128,512]{1,0:T(8,128)S(1)} %fusion.1), channel_id=1, source_target_pairs={{0,2},{1,3},{2,0},{3,1},{4,6},{5,7},{6,4},{7,5},{8,10},{9,11},{10,... | collective-permute-start | bytes 786440 | tf_op jit(solution)/shard_map/ppermute | solution.py:438
  15.2 4.4 %copy-start.10 = (s32[128,32]{0,1:T(8,128)S(1)}, s32[128,32]{0,1:T(8,128)}, u32[]{:S(2)}) copy-start(s32[128,32]{0,1:T(8,128)} %param.12) | copy-start | bytes 49156
  15.4 20.9 %collective-permute-start.3 = (bf16[128,2048]{1,0:T(8,128)(2,1)S(1)}, bf16[128,2048]{1,0:T(8,128)(2,1)}, u32[]{:S(2)}, u32[]{:S(2)}) collective-permute-start(bf16[128,2048]{1,0:T(8,128)(2,1)S(1)} %get-tuple-element.53.rest_0_), channel_id=1, source_target_pairs={{0,32},{4,36},{8,40},{12,44},{16,48},{20,52},{24,56},{28,60},{32,6... | collective-permute-start | bytes 1572872 | tf_op jit(solution)/shard_map/ppermute | solution.py:435
  16.9 24.9 %collective-permute-start.5 = (bf16[128,2048]{1,0:T(8,128)(2,1)S(1)}, bf16[128,2048]{1,0:T(8,128)(2,1)}, u32[]{:S(2)}, u32[]{:S(2)}) collective-permute-start(bf16[128,2048]{1,0:T(8,128)(2,1)S(1)} %get-tuple-element.53.rest_0_), channel_id=1, source_target_pairs={{0,64},{4,68},{8,72},{12,76},{16,80},{20,84},{24,88},{28,92},{32,9... | collective-permute-start | bytes 1572872 | tf_op jit(solution)/shard_map/ppermute | solution.py:435
  20.0 5.2 %copy-start.6 = (bf16[1024,256]{1,0:T(8,128)(2,1)S(1)}, bf16[1024,256]{1,0:T(8,128)(2,1)}, u32[]{:S(2)}) copy-start(bf16[1024,256]{1,0:T(8,128)(2,1)} %second_ref.3) | copy-start | bytes 1572868
  20.0 5.2 %copy-start.8 = (bf16[128,256]{1,0:T(8,128)(2,1)S(1)}, bf16[128,256]{1,0:T(8,128)(2,1)}, u32[]{:S(2)}) copy-start(bf16[128,256]{1,0:T(8,128)(2,1)} %grad_ref.1) | copy-start | bytes 196612
  20.0 5.2 %copy-start.9 = (bf16[64,256]{1,0:T(8,128)(2,1)S(1)}, bf16[64,256]{1,0:T(8,128)(2,1)}, u32[]{:S(2)}) copy-start(bf16[64,256]{1,0:T(8,128)(2,1)} %first_ref.3) | copy-start | bytes 98308
  20.0 21.8 %collective-permute-start.7 = (bf16[128,2048]{1,0:T(8,128)(2,1)S(1)}, bf16[128,2048]{1,0:T(8,128)(2,1)}, u32[]{:S(2)}, u32[]{:S(2)}) collective-permute-start(bf16[128,2048]{1,0:T(8,128)(2,1)S(1)} %get-tuple-element.53.rest_0_), channel_id=1, source_target_pairs={{0,96},{4,100},{8,104},{12,108},{16,112},{20,116},{24,120},{28,124... | collective-permute-start | bytes 1572872 | tf_op jit(solution)/shard_map/ppermute | solution.py:435
  27.8 26.3 %all-to-all-start = ((bf16[8,144,256]{2,1,0:T(8,128)(2,1)}), bf16[8,144,256]{2,1,0:T(8,128)(2,1)S(1)}, u32[]{:S(2)}, u32[]{:S(2)}) async-start(bf16[8,144,256]{2,1,0:T(8,128)(2,1)} %get-tuple-element.32), calls=%async_computation | async-start | bytes 1179648 | tf_op jit(solution)/shard_map/all_to_all | solution.py:459
  36.2 60.8 %all-gather.2.cloned.1.call-start = ((), (), s32[]{:S(2)}) async-start(), calls=%async_computation.5 | async-start | bytes 2949120 | tf_op jit(solution)/shard_map/all_gather | solution.py:463
  36.3 6.0 %collective-permute-start.4 = (bf16[128,2048]{1,0:T(8,128)(2,1)}, bf16[128,2048]{1,0:T(8,128)(2,1)S(1)}, u32[]{:S(2)}, u32[]{:S(2)}) collective-permute-start(bf16[128,2048]{1,0:T(8,128)(2,1)} %collective-permute-done.3.rest_2_), channel_id=1, source_target_pairs={{0,128},{128,0},{1,129},{129,1},{2,130},{130,2},{3,131},{131,3},{4... | collective-permute-start | bytes 1572872 | tf_op jit(solution)/shard_map/ppermute | solution.py:431
  41.8 2.1 %collective-permute-start.6 = (bf16[128,2048]{1,0:T(8,128)(2,1)}, bf16[128,2048]{1,0:T(8,128)(2,1)S(1)}, u32[]{:S(2)}, u32[]{:S(2)}) collective-permute-start(bf16[128,2048]{1,0:T(8,128)(2,1)} %collective-permute-done.5.rest_4_), channel_id=1, source_target_pairs={{0,128},{128,0},{1,129},{129,1},{2,130},{130,2},{3,131},{131,3},{4... | collective-permute-start | bytes 1572872 | tf_op jit(solution)/shard_map/ppermute | solution.py:431
  41.8 2.9 %collective-permute-start.8 = (bf16[128,2048]{1,0:T(8,128)(2,1)}, bf16[128,2048]{1,0:T(8,128)(2,1)S(1)}, u32[]{:S(2)}, u32[]{:S(2)}) collective-permute-start(bf16[128,2048]{1,0:T(8,128)(2,1)} %collective-permute-done.7.rest_6_), channel_id=1, source_target_pairs={{0,128},{128,0},{1,129},{129,1},{2,130},{130,2},{3,131},{131,3},{4... | collective-permute-start | bytes 1572872 | tf_op jit(solution)/shard_map/ppermute | solution.py:431
  54.0 0.8 copy-start
  54.9 74.1 %reduce-scatter.2.cloned.1.call-start = ((), (), s32[]{:S(2)}) async-start(), calls=%async_computation.6 | async-start | bytes 1179648 | tf_op jit(solution)/shard_map/reduce_scatter | solution.py:471
  55.0 1.1 copy-start.1
  56.1 27.8 %copy-start.2 = (bf16[512,512]{1,0:T(8,128)(2,1)S(1)}, bf16[512,512]{1,0:T(8,128)(2,1)}, u32[]{:S(2)}) copy-start(bf16[512,512]{1,0:T(8,128)(2,1)} %qw_ref.1) | copy-start | bytes 1572868
  56.1 27.8 %copy-start.3 = (bf16[128,512]{1,0:T(8,128)(2,1)S(1)}, bf16[128,512]{1,0:T(8,128)(2,1)}, u32[]{:S(2)}) copy-start(bf16[128,512]{1,0:T(8,128)(2,1)} %tokens_ref.1) | copy-start | bytes 393220
  56.1 27.8 %copy-start.7 = (bf16[1024,256]{1,0:T(8,128)(2,1)S(1)}, bf16[1024,256]{1,0:T(8,128)(2,1)}, u32[]{:S(2)}) copy-start(bf16[1024,256]{1,0:T(8,128)(2,1)} %second_ref.3) | copy-start | bytes 1572868
  88.3 2.0 %collective-permute-start.9 = (bf16[256,1152]{1,0:T(8,128)(2,1)S(1)}, bf16[256,1152]{1,0:T(8,128)(2,1)S(1)}, u32[]{:S(2)}, u32[]{:S(2)}) collective-permute-start(bf16[256,1152]{1,0:T(8,128)(2,1)S(1)} %get-tuple-element.37), channel_id=1, source_target_pairs={{0,128},{128,0},{1,129},{129,1},{2,130},{130,2},{3,131},{131,3},{4... | collective-permute-start | bytes 1769480 | tf_op jit(solution)/shard_map/ppermute | solution.py:431
  91.2 29.1 %all-to-all-start.2 = ((bf16[32,8,1152]{2,1,0:T(8,128)(2,1)}), bf16[32,8,1152]{2,1,0:T(8,128)(2,1)S(1)}, u32[]{:S(2)}, u32[]{:S(2)}) async-start(bf16[32,8,1152]{2,1,0:T(8,128)(2,1)} %fusion), calls=%async_computation.2 | async-start | bytes 1179648 | tf_op jit(solution)/shard_map/all_to_all | solution.py:480
  97.0 1.7 %copy-start.4 = (bf16[32,144,256]{2,1,0:T(8,128)(2,1)S(1)}, bf16[32,144,256]{2,1,0:T(8,128)(2,1)}, u32[]{:S(2)}) copy-start(bf16[32,144,256]{2,1,0:T(8,128)(2,1)} %all-gather.2.cloned.1.call-done.got_ref) | copy-start | bytes 7077892
  105.7 14.7 %collective-permute-start.10 = (f32[1024,256]{1,0:T(8,128)S(1)}, f32[1024,256]{1,0:T(8,128)S(1)}, u32[]{:S(2)}, u32[]{:S(2)}) collective-permute-start(f32[1024,256]{1,0:T(8,128)S(1)} %scatter_theirs.1), channel_id=1, source_target_pairs={{0,128},{128,0},{1,129},{129,1},{2,130},{130,2},{3,131},{131,3},{4... | collective-permute-start | bytes 3145736 | tf_op jit(solution)/shard_map/ppermute | solution.py:431
  121.3 24.5 %all-to-all-start.3 = ((bf16[32,8,1152]{2,1,0:T(8,128)(2,1)}), bf16[32,8,1152]{2,1,0:T(8,128)(2,1)S(1)}, u32[]{:S(2)}, u32[]{:S(2)}) async-start(bf16[32,8,1152]{2,1,0:T(8,128)(2,1)} %broadcast_in_dim.5), calls=%async_computation.3 | async-start | bytes 1179648 | tf_op jit(solution)/shard_map/all_to_all | solution.py:485
  130.6 1.7 %copy-start.5 = (bf16[32,144,256]{2,1,0:T(8,128)(2,1)S(1)}, bf16[32,144,256]{2,1,0:T(8,128)(2,1)}, u32[]{:S(2)}) copy-start(bf16[32,144,256]{2,1,0:T(8,128)(2,1)} %all-gather.2.cloned.1.call-done.got_ref) | copy-start | bytes 7077892
  145.8 2.0 %collective-permute-start.11 = (bf16[256,1152]{1,0:T(8,128)(2,1)S(1)}, bf16[256,1152]{1,0:T(8,128)(2,1)S(1)}, u32[]{:S(2)}, u32[]{:S(2)}) collective-permute-start(bf16[256,1152]{1,0:T(8,128)(2,1)S(1)} %bitcast.16), channel_id=1, source_target_pairs={{0,128},{128,0},{1,129},{129,1},{2,130},{130,2},{3,131},{131,3},{4... | collective-permute-start | bytes 1769480 | tf_op jit(solution)/shard_map/ppermute | solution.py:431
Sparse Core Ops, SparseCore 0:
  55.0 30.4 all-gather.1
Sparse Core Ops, SparseCore 1:
  88.4 40.5 reduce-scatter.1

commit v4 on v3

--- a/solution.py
+++ b/solution.py
@@ -121,9 +121,12 @@
         lhs[:, k * tok : (k + 1) * tok] = jnp.where(at_owner == owner[at, :], value, zero)
     hot_slots(slots, rank_ref[...])
     lists = dot(lhs[...], slots[...], NT).astype(BF)
+    fold, cap = tok // 2, slots.shape[0]
     for z in range(n_z):
-        sent_ref[z, :tok, :] = grad_ref[...]
-        sent_ref[z, tok:, :] = lists[4 * n_x * z : 4 * n_x * (z + 1)]
+        sent_ref[z, :fold, :cap] = grad_ref[:fold]
+        sent_ref[z, :fold, cap:] = grad_ref[fold:]
+        sent_ref[z, fold:, :cap] = lists[4 * n_x * z : 4 * n_x * (z + 1)]
+        sent_ref[z, fold:, cap:] = jnp.zeros((4 * n_x, cap), BF)
 
 
 def weigh(query, keys_first, keys_second, picks_t, rank, out_grad, row_dev, n_x, n_z, cap):
@@ -132,7 +135,7 @@
     return pl.pallas_call(
         functools.partial(weigh_kernel, row_dev, n_x),
         out_shape=(
-            jax.ShapeDtypeStruct((n_z, tok + 4 * n_x, cols), BF),
+            jax.ShapeDtypeStruct((n_z, tok // 2 + 4 * n_x, 2 * cols), BF),
             jax.ShapeDtypeStruct((topk, tok), F32),
         ),
         scratch_shapes=[
@@ -145,6 +148,11 @@
         cost_estimate=pl.CostEstimate(flops=4_000_000_000, bytes_accessed=1_000_000, transcendentals=4096),
         name="weigh",
     )(query, keys_first, keys_second, picks_t, rank, out_grad)
+
+
+def unfolded(got):
+    rows, cols = got.shape[0] - 16, got.shape[1] // 2
+    return jnp.concatenate([got[:rows, :cols], got[:rows, cols:]], axis=0)
 
 
 def listed(lists, x_own, kind):
@@ -173,7 +181,7 @@
         for copy in copies:
             copy.wait()
 
-    lists[...] = got_ref[0, tok:, :].astype(F32)
+    lists[...] = got_ref[0, tok // 2 :, : lists.shape[1]].astype(F32)
     count = small_iota((256, cap), 0)
     one, zero = jnp.ones((), BF), jnp.zeros((), BF)
     picked = []
@@ -192,7 +200,7 @@
     token = jnp.concatenate(tokens, axis=1).astype(BF)
     weight = jnp.concatenate(weights, axis=1).astype(BF)
     at_token = small_iota((tok, n_x * cap), 0) == token
-    spread = dot(got_ref[0, :tok, :], jnp.where(at_token, one, zero), TN)
+    spread = dot(unfolded(got_ref[0]), jnp.where(at_token, one, zero), TN)
     pick = jnp.sum(picked * spread, axis=0, keepdims=True)
     for s in range(n_x):
         x_own = lax.rem(x_at - s + n_x, n_x)
@@ -205,14 +213,14 @@
 def owner_side(place, got, value_halves, cap):
     blocks, tall, cols = got.shape
     n_x = len(value_halves) // 2
-    tok = tall - 4 * n_x
+    tok, width, cols = 2 * (tall - 4 * n_x), cols, cols // 2
     half, rows = value_halves[0].shape
     return pl.pallas_call(
         owner_kernel,
         grid_spec=pltpu.PrefetchScalarGridSpec(
             num_scalar_prefetch=1,
             grid=(blocks,),
-            in_specs=[pl.BlockSpec((1, tall, cols), lambda b, place: (b, 0, 0))]
+            in_specs=[pl.BlockSpec((1, tall, width), lambda b, place: (b, 0, 0))]
             + [pl.BlockSpec(memory_space=pltpu.HBM)] * (2 * n_x),
             out_specs=[
                 pl.BlockSpec((tok, cols), lambda b, place: (b, 0)),
@@ -238,7 +246,7 @@
 def scatter_kernel(n_after, place_ref, got_ref, *rest):
     come_refs, (out_ref, hot, spread, lists) = rest[n_after:-4], rest[-4:]
     blocks, kinds, cap = lists.shape
-    tok = got_ref.shape[1] - kinds
+    tok = 2 * (got_ref.shape[1] - kinds)
     x_own = place_ref[0]
     one, zero = jnp.ones((), BF), jnp.zeros((), BF)
 
@@ -246,10 +254,10 @@
     def _():
         at_token = small_iota((tok, cap), 0)
         for at in range(blocks):
-            lists[at] = got_ref[at, tok:, :].astype(F32)
+            lists[at] = got_ref[at, tok // 2 :, :cap].astype(F32)
             token = listed(lists.at[at], x_own, 3).astype(BF)
             spread[:, at * cap : (at + 1) * cap] = dot(
-                got_ref[at, :tok, :], jnp.where(at_token == token, one, zero), TN
+                unfolded(got_ref[at]), jnp.where(at_token == token, one, zero), TN
             ).astype(BF)
 
     chunk = (place_ref[2] * pl.num_programs(0) + pl.program_id(0)).astype(F32)
@@ -266,8 +274,8 @@
 
 
 def scatter(place, got, after, rows, n_x, come=()):
-    blocks, tall, cols = got.shape
-    cap = cols
+    blocks, tall, width = got.shape
+    cols = cap = width // 2
     half = rows // 2
     each = pl.BlockSpec((256, cols), lambda r, place: (r, 0))
     fixed = pl.BlockSpec(got.shape, lambda r, place: (0, 0, 0), pipeline_mode=pl.Buffered(1))

time: 160 us -> 177 us (1.11)
  waiting for transfers between devices: 46.6 us -> 55.1 us
  local copies, waits for them, and re-layouts: 7.7 us -> 13.4 us
  blocking collectives: 12.7 us -> 17.8 us
    ppermute x3, waiting for transfers between devices: 5.44 us -> 19.2 us  [along_x(): return lax.ppermute(array, 'row', pairs)]
    all_to_all x1, waiting for transfers between devices: 9.35 us -> 0.01 us  [body(): got = lax.all_to_all(sent, 'row', 0, 0, tiled=True, axis_index_groups=rings)]
    ppermute x3, waiting for transfers between devices: 3.56 us -> 9.5 us  [along_dim(): lax.ppermute(array, 'dim', [(m, (m + shift) % n_dim) for m in range(n_dim)])]
    unnamed x22 -> x34, local copies, waits for them, and re-layouts: 5.24 us -> 10.9 us
    all_to_all x1, blocking collectives: 12.7 us -> 17.8 us  [body(): lax.all_to_all(pick_sent.reshape((n_z * n_dim,) + pick_part.shape[1:]), (...]
  transfers between devices with their start and end apart: 17 -> 17, of which waited for: 10 -> 11; matrix products, arithmetic and copies ran while one was open for 3% -> 3% of each run, Pallas kernels for 24% -> 19%
where the time goes in v4:
time: 177 us; the launch traced here: 174 us
  waiting for transfers between devices  55.1 us (31%)
  Pallas kernels  38.2 us (22%)
  starting transfers between devices  30 us (17%)
  blocking collectives  17.8 us (10%)
  between operations  15.7 us (9%)
  local copies, waits for them, and re-layouts  13.4 us (8%)
  other arithmetic  2.81 us (2%)
    ppermute x3, waiting for transfers between devices, along_x(): return lax.ppermute(array, 'row', pairs)  19.2 us
    all_to_all x1, blocking collectives, body(): lax.all_to_all(pick_sent.reshape((n_z * n_dim,) + pick_part.shape[1:]), (...  17.8 us
    pallas_call x2, Pallas kernels, scatter(): pl.pallas_call(functools.partial(scatter_kernel, len(after)), grid_spec=p...  14.8 us
    all_to_all x1, waiting for transfers between devices, body(): received = lax.all_to_all(mine.reshape(shape), 'row', 0, 0, tiled=True)  14.3 us
    pallas_call x1, Pallas kernels, owner_side(): pl.pallas_call(owner_kernel, grid_spec=pltpu.PrefetchScalarGridSpec(num_s...  13.9 us
    unnamed x34, local copies, waits for them, and re-layouts  10.9 us
    ppermute x3, waiting for transfers between devices, along_dim(): lax.ppermute(array, 'dim', [(m, (m + shift) % n_dim) for m in range(n_dim)])  9.5 us
    all_to_all x1, starting transfers between devices, body(): got = lax.all_to_all(sent, 'row', 0, 0, tiled=True, axis_index_groups=rings)  8.47 us
  transfers between devices with their start and end apart: 17, of which 11 were waited for; matrix products, arithmetic and copies ran while one was open for 3% of the time, Pallas kernels for 19%

profile of v4, /device:TPU:8, one launch (start us, length us, event | category | flops | bytes accessed | tf_op | source)
XLA Modules:
  0.0 174.3 jit_solution(17462464836441668016)
XLA Ops:
  8.0 1.3 fusion.1
  9.4 1.7 collective-permute-start.1
  11.0 0.7 collective-permute-start.2
  11.7 2.0 %collective-permute-start = (f32[128,512]{1,0:T(8,128)S(1)}, f32[128,512]{1,0:T(8,128)S(1)}, u32[]{:S(2)}, u32[]{:S(2)}) collective-permute-start(f32[128,512]{1,0:T(8,128)S(1)} %fusion.1), channel_id=1, source_target_pairs={{0,2},{1,3},{2,0},{3,1},{4,6},{5,7},{6,4},{7,5},{8,10},{9,11},{10,... | collective-permute-start | bytes 786440 | tf_op jit(solution)/shard_map/ppermute | solution.py:446
  13.8 1.5 copy.15
  15.3 0.3 place_picks.1.rank_ref
  15.6 3.2 %collective-permute-done.1 = f32[128,512]{1,0:T(8,128)S(1)} collective-permute-done((f32[128,512]{1,0:T(8,128)S(1)}, f32[128,512]{1,0:T(8,128)S(1)}, u32[]{:S(2)}, u32[]{:S(2)}) %collective-permute-start.1) | collective-permute-done | bytes 262176 | tf_op jit(solution)/shard_map/ppermute | solution.py:446
  18.8 0.7 collective-permute-done.2
  19.5 5.6 %collective-permute-done = f32[128,512]{1,0:T(8,128)S(1)} collective-permute-done((f32[128,512]{1,0:T(8,128)S(1)}, f32[128,512]{1,0:T(8,128)S(1)}, u32[]{:S(2)}, u32[]{:S(2)}) %collective-permute-start) | collective-permute-done | bytes 262176 | tf_op jit(solution)/shard_map/ppermute | solution.py:446
  25.1 0.1 add_convert_fusion.1.query_ref
  25.2 2.6 %weigh.1 = (bf16[8,80,512]{2,1,0:T(8,128)(2,1)}, f32[32,128]{1,0:T(8,128)S(1)}) custom-call(bf16[128,512]{1,0:T(8,128)(2,1)S(1)} %add_convert_fusion.1.query_ref, bf16[64,256]{1,0:T(8,128)(2,1)S(1)} %copy-done.15, bf16[1024,256]{1,0:T(8,128)(2,1)S(1)} %copy-done.6, s32[32,128]{1,0:T(8,128)S(1)} %bitcast.20, s32[32,128]{1,0:T(8,128)S(1)} %place_picks.1.rank_ref, ...), custom_call_target="tpu_custom_call" | custom-call | flops 4000000000 | bytes 1000000 | tf_op jit(solution)/shard_map/weigh/pallas_call | solution.py:135
  27.8 8.5 %all-to-all-start = ((bf16[8,80,512]{2,1,0:T(8,128)(2,1)}), bf16[8,80,512]{2,1,0:T(8,128)(2,1)S(1)}, u32[]{:S(2)}, u32[]{:S(2)}) async-start(bf16[8,80,512]{2,1,0:T(8,128)(2,1)} %get-tuple-element.32), calls=%async_computation | async-start | bytes 1310720 | tf_op jit(solution)/shard_map/all_to_all | solution.py:467
  36.3 0.1 dynamic-slice_bitcast_fusion
  36.4 1.6 collective-permute-start.3
  38.0 2.7 %collective-permute-start.5 = (bf16[128,2048]{1,0:T(8,128)(2,1)S(1)}, bf16[128,2048]{1,0:T(8,128)(2,1)S(1)}, u32[]{:S(2)}, u32[]{:S(2)}) collective-permute-start(bf16[128,2048]{1,0:T(8,128)(2,1)S(1)} %get-tuple-element.53.rest_0_), channel_id=1, source_target_pairs={{0,64},{4,68},{8,72},{12,76},{16,80},{20,84},{24,88},{28,92},{32,9... | collective-permute-start | bytes 1572872 | tf_op jit(solution)/shard_map/ppermute | solution.py:443
  40.7 1.4 collective-permute-start.7
  42.2 9.4 %collective-permute-done.3.rest_2_ = bf16[128,2048]{1,0:T(8,128)(2,1)S(1)} collective-permute-done((bf16[128,2048]{1,0:T(8,128)(2,1)S(1)}, bf16[128,2048]{1,0:T(8,128)(2,1)S(1)}, u32[]{:S(2)}, u32[]{:S(2)}) %collective-permute-start.3) | collective-permute-done | bytes 524320 | tf_op jit(solution)/shard_map/ppermute | solution.py:443
  51.6 0.8 copy-done.8
  52.4 9.7 %collective-permute-done.5.rest_4_ = bf16[128,2048]{1,0:T(8,128)(2,1)S(1)} collective-permute-done((bf16[128,2048]{1,0:T(8,128)(2,1)S(1)}, bf16[128,2048]{1,0:T(8,128)(2,1)S(1)}, u32[]{:S(2)}, u32[]{:S(2)}) %collective-permute-start.5) | collective-permute-done | bytes 524320 | tf_op jit(solution)/shard_map/ppermute | solution.py:443
  62.1 0.8 copy-done.10
  62.9 0.5 collective-permute-start.8
  63.4 0.8 copy-done.12
  64.2 0.7 collective-permute-done.8.rest_7_
  65.0 0.8 copy-done
  66.0 1.1 copy-done.1
  67.1 1.0 copy-done.9
  68.1 1.0 copy-done.11
  69.2 1.0 copy-done.13
  70.2 13.9 %owner_side.1 = (f32[1024,256]{1,0:T(8,128)}, f32[8,8,128]{2,1,0:T(8,128)S(1)}) custom-call(s32[4]{0:T(128)S(1)} %pad_add_fusion.place_ref, bf16[8,80,512]{2,1,0:T(8,128)(2,1)S(1)} %copy-done.1, bf16[128,2048]{1,0:T(8,128)(2,1)S(1)} %get-tuple-element.53.rest_0_, bf16[128,2048]{1,0:T(8,128)(2,1)S(1)} %get-tuple-element.52.rest_1_, ...), custom_call_target="tpu_custom_call" | custom-call | flops 12000000000 | bytes 10000000 | tf_op jit(solution)/shard_map/owner_side/pallas_call | solution.py:218
  84.2 17.8 %all_to_all.20 = f32[32,8,128]{2,1,0:T(8,128)S(1)} all-to-all(f32[32,8,128]{2,1,0:T(8,128)S(1)} %bitcast.22), channel_id=1, replica_groups={{0,1,2,3,4,5,6,7,8,9,10,11,12,13,14,15,16,17,18,19,20,21,22,23,24,25,26..., dimensions={0} | all-to-all | bytes 262144 | tf_op jit(solution)/shard_map/all_to_all | solution.py:474
  102.0 4.4 %grads.1 = (bf16[128,512]{1,0:T(8,128)(2,1)}, f32[256,1152]{1,0:T(8,128)S(1)}, bf16[256,1152]{1,0:T(8,128)(2,1)S(1)}) custom-call(s32[4]{0:T(128)S(1)} %pad_add_fusion.place_ref, f32[8,4,8,128]{3,2,1,0:T(8,128)S(1)} %bitcast.18, s32[32,128]{1,0:T(8,128)S(1)} %place_picks.1.rank_ref, s32[32,128]{1,0:T(8,128)S(1)} %bitcast.21, ...), custom_call_target="tpu_custom_call" | custom-call | flops 4000000000 | bytes 4000000 | tf_op jit(solution)/shard_map/grads/pallas_call | solution.py:380
  106.5 2.0 %collective-permute-done.9 = bf16[256,1152]{1,0:T(8,128)(2,1)S(1)} collective-permute-done((bf16[256,1152]{1,0:T(8,128)(2,1)S(1)}, bf16[256,1152]{1,0:T(8,128)(2,1)S(1)}, u32[]{:S(2)}, u32[]{:S(2)}) %collective-permute-start.9) | collective-permute-done | bytes 589856 | tf_op jit(solution)/shard_map/ppermute | solution.py:439
  108.5 0.9 fusion
  109.4 4.4 %all-to-all-start.2 = ((bf16[32,8,1152]{2,1,0:T(8,128)(2,1)}), bf16[32,8,1152]{2,1,0:T(8,128)(2,1)S(1)}, u32[]{:S(2)}, u32[]{:S(2)}) async-start(bf16[32,8,1152]{2,1,0:T(8,128)(2,1)} %fusion), calls=%async_computation.2 | async-start | bytes 1179648 | tf_op jit(solution)/shard_map/all_to_all | solution.py:488
  113.8 1.7 copy-done.4
  115.5 7.0 %scatter_theirs.1 = f32[1024,256]{1,0:T(8,128)S(1)} custom-call(s32[4]{0:T(128)S(1)} %pad_add_fusion.place_ref, bf16[32,80,512]{2,1,0:T(8,128)(2,1)S(1)} %copy-done.4, bf16[8,128]{1,0:T(8,128)(2,1)S(1)} %slice.12.rest_0_, bf16[8,128]{1,0:T(8,128)(2,1)S(1)} %slice.13.rest_1_, bf16[8,128]{1,0:T(8,128)(2,1)S(1)} %slice.14.rest_2_), custom_call_target="tpu_custom_call" | custom-call | flops 5000000000 | bytes 6000000 | tf_op jit(solution)/shard_map/scatter_theirs/pallas_call | solution.py:282
  122.6 0.1 collective-permute-start.10
  122.7 14.3 %all-to-all-done.2 = bf16[32,8,1152]{2,1,0:T(8,128)(2,1)S(1)} async-done(((bf16[32,8,1152]{2,1,0:T(8,128)(2,1)}), bf16[32,8,1152]{2,1,0:T(8,128)(2,1)S(1)}, u32[]{:S(2)}, u32[]{:S(2)}) %all-to-all-start.2) | async-done | bytes 589856 | tf_op jit(solution)/shard_map/all_to_all | solution.py:488
  137.0 0.1 reduce_sum.12
  137.1 0.9 broadcast_in_dim.5
  137.9 6.3 %all-to-all-start.3 = ((bf16[32,8,1152]{2,1,0:T(8,128)(2,1)}), bf16[32,8,1152]{2,1,0:T(8,128)(2,1)S(1)}, u32[]{:S(2)}, u32[]{:S(2)}) async-start(bf16[32,8,1152]{2,1,0:T(8,128)(2,1)} %broadcast_in_dim.5), calls=%async_computation.3 | async-start | bytes 1179648 | tf_op jit(solution)/shard_map/all_to_all | solution.py:493
  144.3 1.4 reduce-scatter.2.cloned.1.call-done
  145.8 1.5 convert_element_type.17
  147.3 1.7 copy-done.5
  149.0 7.8 %scatter_mine.1 = f32[1024,256]{1,0:T(8,128)} custom-call(s32[3]{0:T(128)S(1)} %pad_add_fusion.1.place_ref, bf16[32,80,512]{2,1,0:T(8,128)(2,1)S(1)} %copy-done.5, bf16[8,128]{1,0:T(8,128)(2,1)S(1)} %slice.12.rest_0_, bf16[8,128]{1,0:T(8,128)(2,1)S(1)} %slice.13.rest_1_, bf16[8,128]{1,0:T(8,128)(2,1)S(1)} %slice.14.rest_2_, ...), custom_call_target="tpu_custom_call" | custom-call | flops 5000000000 | bytes 6000000 | tf_op jit(solution)/shard_map/scatter_mine/pallas_call | solution.py:282
  156.8 5.9 %all-to-all-done.3 = bf16[32,8,1152]{2,1,0:T(8,128)(2,1)S(1)} async-done(((bf16[32,8,1152]{2,1,0:T(8,128)(2,1)}), bf16[32,8,1152]{2,1,0:T(8,128)(2,1)S(1)}, u32[]{:S(2)}, u32[]{:S(2)}) %all-to-all-start.3) | async-done | bytes 589856 | tf_op jit(solution)/shard_map/all_to_all | solution.py:493
  162.7 2.0 %collective-permute-done.11.other_ref = bf16[256,1152]{1,0:T(8,128)(2,1)S(1)} collective-permute-done((bf16[256,1152]{1,0:T(8,128)(2,1)S(1)}, bf16[256,1152]{1,0:T(8,128)(2,1)S(1)}, u32[]{:S(2)}, u32[]{:S(2)}) %collective-permute-start.11) | collective-permute-done | bytes 589856 | tf_op jit(solution)/shard_map/ppermute | solution.py:439
  164.7 2.2 %unfold.1 = (f32[512,512]{1,0:T(8,128)}, f32[64,256]{1,0:T(8,128)}, f32[1024,256]{1,0:T(8,128)}) custom-call(s32[4]{0:T(128)S(1)} %pad_add_fusion.place_ref, bf16[256,1152]{1,0:T(8,128)(2,1)S(1)} %bitcast.17, bf16[256,1152]{1,0:T(8,128)(2,1)S(1)} %collective-permute-done.11.other_ref), custom_call_target="tpu_custom_call" | custom-call | tf_op jit(solution)/shard_map/unfold/pallas_call | solution.py:414
  (44 shorter events, 0.4 us)
Async XLA Ops:
  9.3 5.9 %copy-start.16 = (s32[128,32]{0,1:T(8,128)S(1)}, s32[128,32]{0,1:T(8,128)}, u32[]{:S(2)}) copy-start(s32[128,32]{0,1:T(8,128)} %param.12) | copy-start | bytes 49156
  9.4 9.5 %collective-permute-start.1 = (f32[128,512]{1,0:T(8,128)S(1)}, f32[128,512]{1,0:T(8,128)S(1)}, u32[]{:S(2)}, u32[]{:S(2)}) collective-permute-start(f32[128,512]{1,0:T(8,128)S(1)} %fusion.1), channel_id=1, source_target_pairs={{0,1},{1,2},{2,3},{3,0},{4,5},{5,6},{6,7},{7,4},{8,9},{9,10},{10,1... | collective-permute-start | bytes 786440 | tf_op jit(solution)/shard_map/ppermute | solution.py:446
  11.0 8.5 %collective-permute-start.2 = (f32[128,512]{1,0:T(8,128)S(1)}, f32[128,512]{1,0:T(8,128)S(1)}, u32[]{:S(2)}, u32[]{:S(2)}) collective-permute-start(f32[128,512]{1,0:T(8,128)S(1)} %fusion.1), channel_id=1, source_target_pairs={{0,3},{1,0},{2,1},{3,2},{4,7},{5,4},{6,5},{7,6},{8,11},{9,8},{10,9... | collective-permute-start | bytes 786440 | tf_op jit(solution)/shard_map/ppermute | solution.py:446
  11.7 13.4 %collective-permute-start = (f32[128,512]{1,0:T(8,128)S(1)}, f32[128,512]{1,0:T(8,128)S(1)}, u32[]{:S(2)}, u32[]{:S(2)}) collective-permute-start(f32[128,512]{1,0:T(8,128)S(1)} %fusion.1), channel_id=1, source_target_pairs={{0,2},{1,3},{2,0},{3,1},{4,6},{5,7},{6,4},{7,5},{8,10},{9,11},{10,... | collective-permute-start | bytes 786440 | tf_op jit(solution)/shard_map/ppermute | solution.py:446
  15.6 9.6 %copy-start.6 = (bf16[1024,256]{1,0:T(8,128)(2,1)S(1)}, bf16[1024,256]{1,0:T(8,128)(2,1)}, u32[]{:S(2)}) copy-start(bf16[1024,256]{1,0:T(8,128)(2,1)} %second_ref.3) | copy-start | bytes 1572868
  15.6 9.6 %copy-start.14 = (bf16[128,256]{1,0:T(8,128)(2,1)S(1)}, bf16[128,256]{1,0:T(8,128)(2,1)}, u32[]{:S(2)}) copy-start(bf16[128,256]{1,0:T(8,128)(2,1)} %grad_ref.1) | copy-start | bytes 196612
  15.6 9.6 %copy-start.15 = (bf16[64,256]{1,0:T(8,128)(2,1)S(1)}, bf16[64,256]{1,0:T(8,128)(2,1)}, u32[]{:S(2)}) copy-start(bf16[64,256]{1,0:T(8,128)(2,1)} %first_ref.3) | copy-start | bytes 98308
  27.8 37.2 %all-to-all-start = ((bf16[8,80,512]{2,1,0:T(8,128)(2,1)}), bf16[8,80,512]{2,1,0:T(8,128)(2,1)S(1)}, u32[]{:S(2)}, u32[]{:S(2)}) async-start(bf16[8,80,512]{2,1,0:T(8,128)(2,1)} %get-tuple-element.32), calls=%async_computation | async-start | bytes 1310720 | tf_op jit(solution)/shard_map/all_to_all | solution.py:467
  36.3 77.5 %all-gather.2.cloned.1.call-start = ((), (), s32[]{:S(2)}) async-start(), calls=%async_computation.5 | async-start | bytes 3276800 | tf_op jit(solution)/shard_map/all_gather | solution.py:471
  36.4 15.2 %collective-permute-start.3 = (bf16[128,2048]{1,0:T(8,128)(2,1)S(1)}, bf16[128,2048]{1,0:T(8,128)(2,1)S(1)}, u32[]{:S(2)}, u32[]{:S(2)}) collective-permute-start(bf16[128,2048]{1,0:T(8,128)(2,1)S(1)} %get-tuple-element.53.rest_0_), channel_id=1, source_target_pairs={{0,32},{4,36},{8,40},{12,44},{16,48},{20,52},{24,56},{28,60},{32,6... | collective-permute-start | bytes 1572872 | tf_op jit(solution)/shard_map/ppermute | solution.py:443
  38.0 24.1 %collective-permute-start.5 = (bf16[128,2048]{1,0:T(8,128)(2,1)S(1)}, bf16[128,2048]{1,0:T(8,128)(2,1)S(1)}, u32[]{:S(2)}, u32[]{:S(2)}) collective-permute-start(bf16[128,2048]{1,0:T(8,128)(2,1)S(1)} %get-tuple-element.53.rest_0_), channel_id=1, source_target_pairs={{0,64},{4,68},{8,72},{12,76},{16,80},{20,84},{24,88},{28,92},{32,9... | collective-permute-start | bytes 1572872 | tf_op jit(solution)/shard_map/ppermute | solution.py:443
  40.7 22.2 %collective-permute-start.7 = (bf16[128,2048]{1,0:T(8,128)(2,1)S(1)}, bf16[128,2048]{1,0:T(8,128)(2,1)S(1)}, u32[]{:S(2)}, u32[]{:S(2)}) collective-permute-start(bf16[128,2048]{1,0:T(8,128)(2,1)S(1)} %get-tuple-element.53.rest_0_), channel_id=1, source_target_pairs={{0,96},{4,100},{8,104},{12,108},{16,112},{20,116},{24,120},{28,124... | collective-permute-start | bytes 1572872 | tf_op jit(solution)/shard_map/ppermute | solution.py:443
  51.6 12.6 %collective-permute-start.4 = (bf16[128,2048]{1,0:T(8,128)(2,1)S(1)}, bf16[128,2048]{1,0:T(8,128)(2,1)S(1)}, u32[]{:S(2)}, u32[]{:S(2)}) collective-permute-start(bf16[128,2048]{1,0:T(8,128)(2,1)S(1)} %collective-permute-done.3.rest_2_), channel_id=1, source_target_pairs={{0,128},{128,0},{1,129},{129,1},{2,130},{130,2},{3,131},{131,3},{4... | collective-permute-start | bytes 1572872 | tf_op jit(solution)/shard_map/ppermute | solution.py:439
  51.6 0.8 copy-start.8
  62.1 2.1 %collective-permute-start.6 = (bf16[128,2048]{1,0:T(8,128)(2,1)S(1)}, bf16[128,2048]{1,0:T(8,128)(2,1)S(1)}, u32[]{:S(2)}, u32[]{:S(2)}) collective-permute-start(bf16[128,2048]{1,0:T(8,128)(2,1)S(1)} %collective-permute-done.5.rest_4_), channel_id=1, source_target_pairs={{0,128},{128,0},{1,129},{129,1},{2,130},{130,2},{3,131},{131,3},{4... | collective-permute-start | bytes 1572872 | tf_op jit(solution)/shard_map/ppermute | solution.py:439
  62.1 0.8 copy-start.10
  62.9 2.0 %collective-permute-start.8 = (bf16[128,2048]{1,0:T(8,128)(2,1)S(1)}, bf16[128,2048]{1,0:T(8,128)(2,1)S(1)}, u32[]{:S(2)}, u32[]{:S(2)}) collective-permute-start(bf16[128,2048]{1,0:T(8,128)(2,1)S(1)} %collective-permute-done.7.rest_6_), channel_id=1, source_target_pairs={{0,128},{128,0},{1,129},{129,1},{2,130},{130,2},{3,131},{131,3},{4... | collective-permute-start | bytes 1572872 | tf_op jit(solution)/shard_map/ppermute | solution.py:439
  63.4 0.8 copy-start.12
  65.0 0.8 copy-start
  65.8 79.9 %reduce-scatter.2.cloned.1.call-start = ((), (), s32[]{:S(2)}) async-start(), calls=%async_computation.6 | async-start | bytes 1179648 | tf_op jit(solution)/shard_map/reduce_scatter | solution.py:479
  66.0 1.1 copy-start.1
  67.1 1.0 copy-start.9
  68.1 1.0 copy-start.11
  69.2 1.0 copy-start.13
  70.2 31.8 %copy-start.2 = (bf16[512,512]{1,0:T(8,128)(2,1)S(1)}, bf16[512,512]{1,0:T(8,128)(2,1)}, u32[]{:S(2)}) copy-start(bf16[512,512]{1,0:T(8,128)(2,1)} %qw_ref.1) | copy-start | bytes 1572868
  70.2 31.8 %copy-start.3 = (bf16[128,512]{1,0:T(8,128)(2,1)S(1)}, bf16[128,512]{1,0:T(8,128)(2,1)}, u32[]{:S(2)}) copy-start(bf16[128,512]{1,0:T(8,128)(2,1)} %tokens_ref.1) | copy-start | bytes 393220
  70.2 31.8 %copy-start.7 = (bf16[1024,256]{1,0:T(8,128)(2,1)S(1)}, bf16[1024,256]{1,0:T(8,128)(2,1)}, u32[]{:S(2)}) copy-start(bf16[1024,256]{1,0:T(8,128)(2,1)} %second_ref.3) | copy-start | bytes 1572868
  106.5 2.0 %collective-permute-start.9 = (bf16[256,1152]{1,0:T(8,128)(2,1)S(1)}, bf16[256,1152]{1,0:T(8,128)(2,1)S(1)}, u32[]{:S(2)}, u32[]{:S(2)}) collective-permute-start(bf16[256,1152]{1,0:T(8,128)(2,1)S(1)} %get-tuple-element.37), channel_id=1, source_target_pairs={{0,128},{128,0},{1,129},{129,1},{2,130},{130,2},{3,131},{131,3},{4... | collective-permute-start | bytes 1769480 | tf_op jit(solution)/shard_map/ppermute | solution.py:439
  109.4 27.6 %all-to-all-start.2 = ((bf16[32,8,1152]{2,1,0:T(8,128)(2,1)}), bf16[32,8,1152]{2,1,0:T(8,128)(2,1)S(1)}, u32[]{:S(2)}, u32[]{:S(2)}) async-start(bf16[32,8,1152]{2,1,0:T(8,128)(2,1)} %fusion), calls=%async_computation.2 | async-start | bytes 1179648 | tf_op jit(solution)/shard_map/all_to_all | solution.py:488
  113.8 1.7 copy-start.4
  122.6 14.5 %collective-permute-start.10 = (f32[1024,256]{1,0:T(8,128)S(1)}, f32[1024,256]{1,0:T(8,128)S(1)}, u32[]{:S(2)}, u32[]{:S(2)}) collective-permute-start(f32[1024,256]{1,0:T(8,128)S(1)} %scatter_theirs.1), channel_id=1, source_target_pairs={{0,128},{128,0},{1,129},{129,1},{2,130},{130,2},{3,131},{131,3},{4... | collective-permute-start | bytes 3145736 | tf_op jit(solution)/shard_map/ppermute | solution.py:439
  137.9 24.8 %all-to-all-start.3 = ((bf16[32,8,1152]{2,1,0:T(8,128)(2,1)}), bf16[32,8,1152]{2,1,0:T(8,128)(2,1)S(1)}, u32[]{:S(2)}, u32[]{:S(2)}) async-start(bf16[32,8,1152]{2,1,0:T(8,128)(2,1)} %broadcast_in_dim.5), calls=%async_computation.3 | async-start | bytes 1179648 | tf_op jit(solution)/shard_map/all_to_all | solution.py:493
  147.3 1.7 copy-start.5
  162.7 2.0 %collective-permute-start.11 = (bf16[256,1152]{1,0:T(8,128)(2,1)S(1)}, bf16[256,1152]{1,0:T(8,128)(2,1)S(1)}, u32[]{:S(2)}, u32[]{:S(2)}) collective-permute-start(bf16[256,1152]{1,0:T(8,128)(2,1)S(1)} %bitcast.16), channel_id=1, source_target_pairs={{0,128},{128,0},{1,129},{129,1},{2,130},{130,2},{3,131},{131,3},{4... | collective-permute-start | bytes 1769480 | tf_op jit(solution)/shard_map/ppermute | solution.py:439
Sparse Core Ops, SparseCore 0:
  66.0 36.5 all-gather.1
Sparse Core Ops, SparseCore 1:
  106.6 39.1 reduce-scatter.1

commit v5 on v3

--- a/solution.py
+++ b/solution.py
@@ -468,14 +468,15 @@
         axis_index_groups=planes,
     ).reshape(pick_sent.shape)
 
-    mixed = lax.psum_scatter(
-        mixed_part, "row", tiled=True, axis_index_groups=rings
-    ).astype(BF)
     token_grad, mine, theirs = grads(
         place, pick_parts, rank, picks_t, weight, query, keys_first, keys_second, query_weight, tokens,
         row_dev, n_z,
     )
     mine = (mine + other_core(theirs).astype(F32)).astype(BF)
+    mine, mixed_part = lax.optimization_barrier((mine, mixed_part))
+    mixed = lax.psum_scatter(
+        mixed_part, "row", tiled=True, axis_index_groups=rings
+    ).astype(BF)
     shape = (n_row, half // n_row, mine.shape[1])
     received = lax.all_to_all(mine.reshape(shape), "row", 0, 0, tiled=True)
     summed = jnp.sum(received.astype(F32), axis=0).astype(BF)
@@ -485,7 +486,7 @@
     mine = lax.all_to_all(summed, "row", 0, 0, tiled=True).reshape(mine.shape)
     own_place = jnp.stack([row_at // n_z, dp_at, dp_at]).astype(I32)
     value_grad = scatter(own_place, got_x, corners, row_dev, n_x, (come,))
-    mine, mixed, value_grad = lax.optimization_barrier((mine, mixed, value_grad))
+    mine, value_grad = lax.optimization_barrier((mine, value_grad))
     other = other_core(mine)
     qw_grad, first_grad, second_grad = unfold(
         place, mine, other, (query_weight.shape, keys_first.shape, keys_second.shape)

time: 160 us -> 164 us (1.025)
  waiting for transfers between devices: 46.6 us -> 51.9 us
    all_to_all x1, waiting for transfers between devices: 5.79 us -> 14.9 us  [body(): mine = lax.all_to_all(summed, 'row', 0, 0, tiled=True).reshape(mine.shape)]
    all_to_all x1, waiting for transfers between devices: 14.5 us -> 9.39 us  [body(): received = lax.all_to_all(mine.reshape(shape), 'row', 0, 0, tiled=True)]
    reduce_scatter x1, waiting for transfers between devices: 1.63 us -> 4.83 us  [body(): lax.psum_scatter(mixed_part, 'row', tiled=True, axis_index_groups=rings)]
    ppermute x6, waiting for transfers between devices: 6.33 us -> 4.36 us  [other_core(): return lax.ppermute(array, 'dp', [(0, 1), (1, 0)])]
  transfers between devices with their start and end apart: 17 -> 17, of which waited for: 10 -> 9; matrix products, arithmetic and copies ran while one was open for 3% -> 3% of each run, Pallas kernels for 24% -> 23%
where the time goes in v5:
time: 164 us; the launch traced here: 163 us
  waiting for transfers between devices  51.9 us (32%)
  Pallas kernels  39.3 us (24%)
  starting transfers between devices  31.1 us (19%)
  between operations  15.7 us (10%)
  blocking collectives  12.7 us (8%)
  local copies, waits for them, and re-layouts  7.72 us (5%)
  other arithmetic  2.81 us (2%)
    pallas_call x1, Pallas kernels, owner_side(): pl.pallas_call(owner_kernel, grid_spec=pltpu.PrefetchScalarGridSpec(num_s...  15.1 us
    all_to_all x1, waiting for transfers between devices, body(): mine = lax.all_to_all(summed, 'row', 0, 0, tiled=True).reshape(mine.shape)  14.9 us
    pallas_call x2, Pallas kernels, scatter(): pl.pallas_call(functools.partial(scatter_kernel, len(after)), grid_spec=p...  14.8 us
    all_to_all x1, blocking collectives, body(): lax.all_to_all(pick_sent.reshape((n_z * n_dim,) + pick_part.shape[1:]), (...  12.7 us
    all_to_all x1, waiting for transfers between devices, body(): received = lax.all_to_all(mine.reshape(shape), 'row', 0, 0, tiled=True)  9.39 us
    all_to_all x1, waiting for transfers between devices, body(): got = lax.all_to_all(sent, 'row', 0, 0, tiled=True, axis_index_groups=rings)  9.35 us
    all_to_all x1, starting transfers between devices, body(): got = lax.all_to_all(sent, 'row', 0, 0, tiled=True, axis_index_groups=rings)  8.46 us
    all_to_all x1, starting transfers between devices, body(): mine = lax.all_to_all(summed, 'row', 0, 0, tiled=True).reshape(mine.shape)  5.88 us
  transfers between devices with their start and end apart: 17, of which 9 were waited for; matrix products, arithmetic and copies ran while one was open for 3% of the time, Pallas kernels for 23%

profile of v5, /device:TPU:8, one launch (start us, length us, event | category | flops | bytes accessed | tf_op | source)
XLA Modules:
  0.0 162.5 jit_solution(5863703599579286464)
XLA Ops:
  8.0 1.3 fusion
  9.3 1.7 %collective-permute-start.1 = (f32[128,512]{1,0:T(8,128)S(1)}, f32[128,512]{1,0:T(8,128)S(1)}, u32[]{:S(2)}, u32[]{:S(2)}) collective-permute-start(f32[128,512]{1,0:T(8,128)S(1)} %fusion), channel_id=1, source_target_pairs={{0,1},{1,2},{2,3},{3,0},{4,5},{5,6},{6,7},{7,4},{8,9},{9,10},{10,1... | collective-permute-start | bytes 786440 | tf_op jit(solution)/shard_map/ppermute | solution.py:438
  11.0 0.7 collective-permute-start.2
  11.7 2.0 %collective-permute-start = (f32[128,512]{1,0:T(8,128)S(1)}, f32[128,512]{1,0:T(8,128)S(1)}, u32[]{:S(2)}, u32[]{:S(2)}) collective-permute-start(f32[128,512]{1,0:T(8,128)S(1)} %fusion), channel_id=1, source_target_pairs={{0,2},{1,3},{2,0},{3,1},{4,6},{5,7},{6,4},{7,5},{8,10},{9,11},{10,... | collective-permute-start | bytes 786440 | tf_op jit(solution)/shard_map/ppermute | solution.py:438
  13.7 1.5 copy.15
  15.2 0.1 dynamic-slice_bitcast_fusion
  15.4 1.6 collective-permute-start.3
  16.9 2.7 %collective-permute-start.5 = (bf16[128,2048]{1,0:T(8,128)(2,1)S(1)}, bf16[128,2048]{1,0:T(8,128)(2,1)}, u32[]{:S(2)}, u32[]{:S(2)}) collective-permute-start(bf16[128,2048]{1,0:T(8,128)(2,1)S(1)} %get-tuple-element.55.rest_0_), channel_id=1, source_target_pairs={{0,64},{4,68},{8,72},{12,76},{16,80},{20,84},{24,88},{28,92},{32,9... | collective-permute-start | bytes 1572872 | tf_op jit(solution)/shard_map/ppermute | solution.py:435
  19.7 0.3 place_picks.1.rank_ref
  20.0 1.5 collective-permute-start.7
  21.6 3.6 %collective-permute-done = f32[128,512]{1,0:T(8,128)S(1)} collective-permute-done((f32[128,512]{1,0:T(8,128)S(1)}, f32[128,512]{1,0:T(8,128)S(1)}, u32[]{:S(2)}, u32[]{:S(2)}) %collective-permute-start) | collective-permute-done | bytes 262176 | tf_op jit(solution)/shard_map/ppermute | solution.py:438
  25.1 0.1 add_convert_fusion.1.query_ref
  25.2 2.5 %weigh.1 = (bf16[8,144,256]{2,1,0:T(8,128)(2,1)}, f32[32,128]{1,0:T(8,128)S(1)}) custom-call(bf16[128,512]{1,0:T(8,128)(2,1)S(1)} %add_convert_fusion.1.query_ref, bf16[64,256]{1,0:T(8,128)(2,1)S(1)} %copy-done.9, bf16[1024,256]{1,0:T(8,128)(2,1)S(1)} %copy-done.6, s32[32,128]{1,0:T(8,128)S(1)} %bitcast.19, s32[32,128]{1,0:T(8,128)S(1)} %place_picks.1.rank_ref, ...), custom_call_target="tpu_custom_call" | custom-call | flops 4000000000 | bytes 1000000 | tf_op jit(solution)/shard_map/weigh/pallas_call | solution.py:132
  27.8 8.5 %all-to-all-start = ((bf16[8,144,256]{2,1,0:T(8,128)(2,1)}), bf16[8,144,256]{2,1,0:T(8,128)(2,1)S(1)}, u32[]{:S(2)}, u32[]{:S(2)}) async-start(bf16[8,144,256]{2,1,0:T(8,128)(2,1)} %get-tuple-element.33), calls=%async_computation | async-start | bytes 1179648 | tf_op jit(solution)/shard_map/all_to_all | solution.py:459
  36.2 0.0 all-gather.2.cloned.1.call-start
  36.3 0.1 collective-permute-start.4
  36.4 5.4 %collective-permute-done.5.rest_4_ = bf16[128,2048]{1,0:T(8,128)(2,1)} collective-permute-done((bf16[128,2048]{1,0:T(8,128)(2,1)S(1)}, bf16[128,2048]{1,0:T(8,128)(2,1)}, u32[]{:S(2)}, u32[]{:S(2)}) %collective-permute-start.5) | collective-permute-done | bytes 524320 | tf_op jit(solution)/shard_map/ppermute | solution.py:435
  41.8 0.5 collective-permute-start.8
  42.3 1.6 collective-permute-done.6.rest_5_
  43.9 0.7 collective-permute-done.8.rest_7_
  44.7 9.4 %all-to-all-done.got_ref = bf16[8,144,256]{2,1,0:T(8,128)(2,1)S(1)} async-done(((bf16[8,144,256]{2,1,0:T(8,128)(2,1)}), bf16[8,144,256]{2,1,0:T(8,128)(2,1)S(1)}, u32[]{:S(2)}, u32[]{:S(2)}) %all-to-all-start) | async-done | bytes 589856 | tf_op jit(solution)/shard_map/all_to_all | solution.py:459
  54.0 0.8 copy-done
  54.8 0.0 all-gather.2.cloned.1.call-update
  54.9 0.1 pad_add_fusion.place_ref
  55.0 1.1 copy-done.1
  56.0 15.1 %owner_side.1 = (f32[1024,256]{1,0:T(8,128)}, f32[8,8,128]{2,1,0:T(8,128)S(1)}) custom-call(s32[4]{0:T(128)S(1)} %pad_add_fusion.place_ref, bf16[8,144,256]{2,1,0:T(8,128)(2,1)S(1)} %copy-done.1, bf16[128,2048]{1,0:T(8,128)(2,1)S(1)} %get-tuple-element.55.rest_0_, bf16[128,2048]{1,0:T(8,128)(2,1)S(1)} %get-tuple-element.54.rest_1_, ...), custom_call_target="tpu_custom_call" | custom-call | flops 12000000000 | bytes 10000000 | tf_op jit(solution)/shard_map/owner_side/pallas_call | solution.py:210
  71.1 12.7 %all_to_all.20 = f32[32,8,128]{2,1,0:T(8,128)S(1)} all-to-all(f32[32,8,128]{2,1,0:T(8,128)S(1)} %bitcast.21), channel_id=1, replica_groups={{0,1,2,3,4,5,6,7,8,9,10,11,12,13,14,15,16,17,18,19,20,21,22,23,24,25,26..., dimensions={0} | all-to-all | bytes 262144 | tf_op jit(solution)/shard_map/all_to_all | solution.py:466
  83.8 4.4 %grads.1 = (bf16[128,512]{1,0:T(8,128)(2,1)}, f32[256,1152]{1,0:T(8,128)S(1)}, bf16[256,1152]{1,0:T(8,128)(2,1)S(1)}) custom-call(s32[4]{0:T(128)S(1)} %pad_add_fusion.place_ref, f32[8,4,8,128]{3,2,1,0:T(8,128)S(1)} %bitcast.17, s32[32,128]{1,0:T(8,128)S(1)} %place_picks.1.rank_ref, s32[32,128]{1,0:T(8,128)S(1)} %bitcast.20, ...), custom_call_target="tpu_custom_call" | custom-call | flops 4000000000 | bytes 4000000 | tf_op jit(solution)/shard_map/grads/pallas_call | solution.py:372
  88.3 2.0 %collective-permute-done.9 = bf16[256,1152]{1,0:T(8,128)(2,1)S(1)} collective-permute-done((bf16[256,1152]{1,0:T(8,128)(2,1)S(1)}, bf16[256,1152]{1,0:T(8,128)(2,1)S(1)}, u32[]{:S(2)}, u32[]{:S(2)}) %collective-permute-start.9) | collective-permute-done | bytes 589856 | tf_op jit(solution)/shard_map/ppermute | solution.py:431
  90.3 0.9 add_convert_fusion
  91.2 5.7 %all-to-all-start.2 = ((bf16[32,8,1152]{2,1,0:T(8,128)(2,1)}), bf16[32,8,1152]{2,1,0:T(8,128)(2,1)S(1)}, u32[]{:S(2)}, u32[]{:S(2)}) async-start(bf16[32,8,1152]{2,1,0:T(8,128)(2,1)} %bitcast.9), calls=%async_computation.3 | async-start | bytes 1179648 | tf_op jit(solution)/shard_map/all_to_all | solution.py:481
  96.9 0.0 reduce-scatter.2.cloned.1.call-start
  97.0 0.0 all-gather.2.cloned.1.call-done.got_ref
  97.0 1.7 %copy-done.4 = bf16[32,144,256]{2,1,0:T(8,128)(2,1)S(1)} copy-done((bf16[32,144,256]{2,1,0:T(8,128)(2,1)S(1)}, bf16[32,144,256]{2,1,0:T(8,128)(2,1)}, u32[]{:S(2)}) %copy-start.4) | copy-done | bytes 2359320
  98.7 7.0 %scatter_theirs.1 = f32[1024,256]{1,0:T(8,128)S(1)} custom-call(s32[4]{0:T(128)S(1)} %pad_add_fusion.place_ref, bf16[32,144,256]{2,1,0:T(8,128)(2,1)S(1)} %copy-done.4, bf16[8,128]{1,0:T(8,128)(2,1)S(1)} %slice.12.rest_0_, bf16[8,128]{1,0:T(8,128)(2,1)S(1)} %slice.13.rest_1_, bf16[8,128]{1,0:T(8,128)(2,1)S(1)} %slice.14.rest_2_), custom_call_target="tpu_custom_call" | custom-call | flops 5000000000 | bytes 6000000 | tf_op jit(solution)/shard_map/scatter_theirs/pallas_call | solution.py:274
  105.7 0.1 collective-permute-start.10
  105.8 0.0 reduce-scatter.2.cloned.1.call-update
  105.8 9.4 %all-to-all-done.2 = bf16[32,8,1152]{2,1,0:T(8,128)(2,1)S(1)} async-done(((bf16[32,8,1152]{2,1,0:T(8,128)(2,1)}), bf16[32,8,1152]{2,1,0:T(8,128)(2,1)S(1)}, u32[]{:S(2)}, u32[]{:S(2)}) %all-to-all-start.2) | async-done | bytes 589856 | tf_op jit(solution)/shard_map/all_to_all | solution.py:481
  115.2 0.1 reduce_sum.12
  115.3 0.9 broadcast_in_dim.5
  116.2 5.9 %all-to-all-start.3 = ((bf16[32,8,1152]{2,1,0:T(8,128)(2,1)}), bf16[32,8,1152]{2,1,0:T(8,128)(2,1)S(1)}, u32[]{:S(2)}, u32[]{:S(2)}) async-start(bf16[32,8,1152]{2,1,0:T(8,128)(2,1)} %broadcast_in_dim.5), calls=%async_computation.4 | async-start | bytes 1179648 | tf_op jit(solution)/shard_map/all_to_all | solution.py:486
  122.1 0.1 pad_add_fusion.1.place_ref
  122.2 1.7 %copy-done.5 = bf16[32,144,256]{2,1,0:T(8,128)(2,1)S(1)} copy-done((bf16[32,144,256]{2,1,0:T(8,128)(2,1)S(1)}, bf16[32,144,256]{2,1,0:T(8,128)(2,1)}, u32[]{:S(2)}) %copy-start.5) | copy-done | bytes 2359320
  123.8 7.7 %scatter_mine.1 = f32[1024,256]{1,0:T(8,128)} custom-call(s32[3]{0:T(128)S(1)} %pad_add_fusion.1.place_ref, bf16[32,144,256]{2,1,0:T(8,128)(2,1)S(1)} %copy-done.5, bf16[8,128]{1,0:T(8,128)(2,1)S(1)} %slice.12.rest_0_, bf16[8,128]{1,0:T(8,128)(2,1)S(1)} %slice.13.rest_1_, bf16[8,128]{1,0:T(8,128)(2,1)S(1)} %slice.14.rest_2_, ...), custom_call_target="tpu_custom_call" | custom-call | flops 5000000000 | bytes 6000000 | tf_op jit(solution)/shard_map/scatter_mine/pallas_call | solution.py:274
  131.6 14.9 %all-to-all-done.3 = bf16[32,8,1152]{2,1,0:T(8,128)(2,1)S(1)} async-done(((bf16[32,8,1152]{2,1,0:T(8,128)(2,1)}), bf16[32,8,1152]{2,1,0:T(8,128)(2,1)S(1)}, u32[]{:S(2)}, u32[]{:S(2)}) %all-to-all-start.3) | async-done | bytes 589856 | tf_op jit(solution)/shard_map/all_to_all | solution.py:486
  146.5 4.8 %reduce-scatter.2.cloned.1.call-done = f32[128,256]{1,0:T(8,128)} async-done(((f32[1024,256]{1,0:T(8,128)}), f32[128,256]{1,0:T(8,128)}) %reduce-scatter.2.cloned.1.call-update) | async-done | bytes 131088 | tf_op jit(solution)/shard_map/reduce_scatter | solution.py:477
  151.4 1.5 convert_element_type.17
  152.9 2.2 %unfold.1 = (f32[512,512]{1,0:T(8,128)}, f32[64,256]{1,0:T(8,128)}, f32[1024,256]{1,0:T(8,128)}) custom-call(s32[4]{0:T(128)S(1)} %pad_add_fusion.place_ref, bf16[256,1152]{1,0:T(8,128)(2,1)S(1)} %bitcast.16, bf16[256,1152]{1,0:T(8,128)(2,1)S(1)} %collective-permute-done.11.other_ref), custom_call_target="tpu_custom_call" | custom-call | tf_op jit(solution)/shard_map/unfold/pallas_call | solution.py:406
  (32 shorter events, 0.1 us)
Async XLA Ops:
  9.3 10.7 %collective-permute-start.1 = (f32[128,512]{1,0:T(8,128)S(1)}, f32[128,512]{1,0:T(8,128)S(1)}, u32[]{:S(2)}, u32[]{:S(2)}) collective-permute-start(f32[128,512]{1,0:T(8,128)S(1)} %fusion), channel_id=1, source_target_pairs={{0,1},{1,2},{2,3},{3,0},{4,5},{5,6},{6,7},{7,4},{8,9},{9,10},{10,1... | collective-permute-start | bytes 786440 | tf_op jit(solution)/shard_map/ppermute | solution.py:438
  11.0 10.6 %collective-permute-start.2 = (f32[128,512]{1,0:T(8,128)S(1)}, f32[128,512]{1,0:T(8,128)S(1)}, u32[]{:S(2)}, u32[]{:S(2)}) collective-permute-start(f32[128,512]{1,0:T(8,128)S(1)} %fusion), channel_id=1, source_target_pairs={{0,3},{1,0},{2,1},{3,2},{4,7},{5,4},{6,5},{7,6},{8,11},{9,8},{10,9... | collective-permute-start | bytes 786440 | tf_op jit(solution)/shard_map/ppermute | solution.py:438
  11.7 13.4 %collective-permute-start = (f32[128,512]{1,0:T(8,128)S(1)}, f32[128,512]{1,0:T(8,128)S(1)}, u32[]{:S(2)}, u32[]{:S(2)}) collective-permute-start(f32[128,512]{1,0:T(8,128)S(1)} %fusion), channel_id=1, source_target_pairs={{0,2},{1,3},{2,0},{3,1},{4,6},{5,7},{6,4},{7,5},{8,10},{9,11},{10,... | collective-permute-start | bytes 786440 | tf_op jit(solution)/shard_map/ppermute | solution.py:438
  15.2 4.4 %copy-start.10 = (s32[128,32]{0,1:T(8,128)S(1)}, s32[128,32]{0,1:T(8,128)}, u32[]{:S(2)}) copy-start(s32[128,32]{0,1:T(8,128)} %param.12) | copy-start | bytes 49156
  15.4 20.9 %collective-permute-start.3 = (bf16[128,2048]{1,0:T(8,128)(2,1)S(1)}, bf16[128,2048]{1,0:T(8,128)(2,1)}, u32[]{:S(2)}, u32[]{:S(2)}) collective-permute-start(bf16[128,2048]{1,0:T(8,128)(2,1)S(1)} %get-tuple-element.55.rest_0_), channel_id=1, source_target_pairs={{0,32},{4,36},{8,40},{12,44},{16,48},{20,52},{24,56},{28,60},{32,6... | collective-permute-start | bytes 1572872 | tf_op jit(solution)/shard_map/ppermute | solution.py:435
  16.9 24.9 %collective-permute-start.5 = (bf16[128,2048]{1,0:T(8,128)(2,1)S(1)}, bf16[128,2048]{1,0:T(8,128)(2,1)}, u32[]{:S(2)}, u32[]{:S(2)}) collective-permute-start(bf16[128,2048]{1,0:T(8,128)(2,1)S(1)} %get-tuple-element.55.rest_0_), channel_id=1, source_target_pairs={{0,64},{4,68},{8,72},{12,76},{16,80},{20,84},{24,88},{28,92},{32,9... | collective-permute-start | bytes 1572872 | tf_op jit(solution)/shard_map/ppermute | solution.py:435
  20.0 5.2 %copy-start.6 = (bf16[1024,256]{1,0:T(8,128)(2,1)S(1)}, bf16[1024,256]{1,0:T(8,128)(2,1)}, u32[]{:S(2)}) copy-start(bf16[1024,256]{1,0:T(8,128)(2,1)} %second_ref.3) | copy-start | bytes 1572868
  20.0 5.2 %copy-start.8 = (bf16[128,256]{1,0:T(8,128)(2,1)S(1)}, bf16[128,256]{1,0:T(8,128)(2,1)}, u32[]{:S(2)}) copy-start(bf16[128,256]{1,0:T(8,128)(2,1)} %grad_ref.1) | copy-start | bytes 196612
  20.0 5.2 %copy-start.9 = (bf16[64,256]{1,0:T(8,128)(2,1)S(1)}, bf16[64,256]{1,0:T(8,128)(2,1)}, u32[]{:S(2)}) copy-start(bf16[64,256]{1,0:T(8,128)(2,1)} %first_ref.3) | copy-start | bytes 98308
  20.0 21.8 %collective-permute-start.7 = (bf16[128,2048]{1,0:T(8,128)(2,1)S(1)}, bf16[128,2048]{1,0:T(8,128)(2,1)}, u32[]{:S(2)}, u32[]{:S(2)}) collective-permute-start(bf16[128,2048]{1,0:T(8,128)(2,1)S(1)} %get-tuple-element.55.rest_0_), channel_id=1, source_target_pairs={{0,96},{4,100},{8,104},{12,108},{16,112},{20,116},{24,120},{28,124... | collective-permute-start | bytes 1572872 | tf_op jit(solution)/shard_map/ppermute | solution.py:435
  27.8 26.3 %all-to-all-start = ((bf16[8,144,256]{2,1,0:T(8,128)(2,1)}), bf16[8,144,256]{2,1,0:T(8,128)(2,1)S(1)}, u32[]{:S(2)}, u32[]{:S(2)}) async-start(bf16[8,144,256]{2,1,0:T(8,128)(2,1)} %get-tuple-element.33), calls=%async_computation | async-start | bytes 1179648 | tf_op jit(solution)/shard_map/all_to_all | solution.py:459
  36.2 60.8 %all-gather.2.cloned.1.call-start = ((), (), s32[]{:S(2)}) async-start(), calls=%async_computation.6 | async-start | bytes 2949120 | tf_op jit(solution)/shard_map/all_gather | solution.py:463
  36.3 6.0 %collective-permute-start.4 = (bf16[128,2048]{1,0:T(8,128)(2,1)}, bf16[128,2048]{1,0:T(8,128)(2,1)S(1)}, u32[]{:S(2)}, u32[]{:S(2)}) collective-permute-start(bf16[128,2048]{1,0:T(8,128)(2,1)} %collective-permute-done.3.rest_2_), channel_id=1, source_target_pairs={{0,128},{128,0},{1,129},{129,1},{2,130},{130,2},{3,131},{131,3},{4... | collective-permute-start | bytes 1572872 | tf_op jit(solution)/shard_map/ppermute | solution.py:431
  41.8 2.1 %collective-permute-start.6 = (bf16[128,2048]{1,0:T(8,128)(2,1)}, bf16[128,2048]{1,0:T(8,128)(2,1)S(1)}, u32[]{:S(2)}, u32[]{:S(2)}) collective-permute-start(bf16[128,2048]{1,0:T(8,128)(2,1)} %collective-permute-done.5.rest_4_), channel_id=1, source_target_pairs={{0,128},{128,0},{1,129},{129,1},{2,130},{130,2},{3,131},{131,3},{4... | collective-permute-start | bytes 1572872 | tf_op jit(solution)/shard_map/ppermute | solution.py:431
  41.8 2.9 %collective-permute-start.8 = (bf16[128,2048]{1,0:T(8,128)(2,1)}, bf16[128,2048]{1,0:T(8,128)(2,1)S(1)}, u32[]{:S(2)}, u32[]{:S(2)}) collective-permute-start(bf16[128,2048]{1,0:T(8,128)(2,1)} %collective-permute-done.7.rest_6_), channel_id=1, source_target_pairs={{0,128},{128,0},{1,129},{129,1},{2,130},{130,2},{3,131},{131,3},{4... | collective-permute-start | bytes 1572872 | tf_op jit(solution)/shard_map/ppermute | solution.py:431
  54.0 0.8 copy-start
  55.0 1.1 copy-start.1
  56.0 27.8 %copy-start.2 = (bf16[512,512]{1,0:T(8,128)(2,1)S(1)}, bf16[512,512]{1,0:T(8,128)(2,1)}, u32[]{:S(2)}) copy-start(bf16[512,512]{1,0:T(8,128)(2,1)} %qw_ref.1) | copy-start | bytes 1572868
  56.0 27.8 %copy-start.3 = (bf16[128,512]{1,0:T(8,128)(2,1)S(1)}, bf16[128,512]{1,0:T(8,128)(2,1)}, u32[]{:S(2)}) copy-start(bf16[128,512]{1,0:T(8,128)(2,1)} %tokens_ref.1) | copy-start | bytes 393220
  56.0 27.8 %copy-start.7 = (bf16[1024,256]{1,0:T(8,128)(2,1)S(1)}, bf16[1024,256]{1,0:T(8,128)(2,1)}, u32[]{:S(2)}) copy-start(bf16[1024,256]{1,0:T(8,128)(2,1)} %second_ref.3) | copy-start | bytes 1572868
  88.3 2.0 %collective-permute-start.9 = (bf16[256,1152]{1,0:T(8,128)(2,1)S(1)}, bf16[256,1152]{1,0:T(8,128)(2,1)S(1)}, u32[]{:S(2)}, u32[]{:S(2)}) collective-permute-start(bf16[256,1152]{1,0:T(8,128)(2,1)S(1)} %get-tuple-element.38), channel_id=1, source_target_pairs={{0,128},{128,0},{1,129},{129,1},{2,130},{130,2},{3,131},{131,3},{4... | collective-permute-start | bytes 1769480 | tf_op jit(solution)/shard_map/ppermute | solution.py:431
  91.2 24.0 %all-to-all-start.2 = ((bf16[32,8,1152]{2,1,0:T(8,128)(2,1)}), bf16[32,8,1152]{2,1,0:T(8,128)(2,1)S(1)}, u32[]{:S(2)}, u32[]{:S(2)}) async-start(bf16[32,8,1152]{2,1,0:T(8,128)(2,1)} %bitcast.9), calls=%async_computation.3 | async-start | bytes 1179648 | tf_op jit(solution)/shard_map/all_to_all | solution.py:481
  96.9 54.4 %reduce-scatter.2.cloned.1.call-start = ((), (), s32[]{:S(2)}) async-start(), calls=%async_computation.5 | async-start | bytes 1179648 | tf_op jit(solution)/shard_map/reduce_scatter | solution.py:477
  97.0 1.7 %copy-start.4 = (bf16[32,144,256]{2,1,0:T(8,128)(2,1)S(1)}, bf16[32,144,256]{2,1,0:T(8,128)(2,1)}, u32[]{:S(2)}) copy-start(bf16[32,144,256]{2,1,0:T(8,128)(2,1)} %all-gather.2.cloned.1.call-done.got_ref) | copy-start | bytes 7077892
  105.7 9.6 %collective-permute-start.10 = (f32[1024,256]{1,0:T(8,128)S(1)}, f32[1024,256]{1,0:T(8,128)S(1)}, u32[]{:S(2)}, u32[]{:S(2)}) collective-permute-start(f32[1024,256]{1,0:T(8,128)S(1)} %scatter_theirs.1), channel_id=1, source_target_pairs={{0,128},{128,0},{1,129},{129,1},{2,130},{130,2},{3,131},{131,3},{4... | collective-permute-start | bytes 3145736 | tf_op jit(solution)/shard_map/ppermute | solution.py:431
  116.2 30.3 %all-to-all-start.3 = ((bf16[32,8,1152]{2,1,0:T(8,128)(2,1)}), bf16[32,8,1152]{2,1,0:T(8,128)(2,1)S(1)}, u32[]{:S(2)}, u32[]{:S(2)}) async-start(bf16[32,8,1152]{2,1,0:T(8,128)(2,1)} %broadcast_in_dim.5), calls=%async_computation.4 | async-start | bytes 1179648 | tf_op jit(solution)/shard_map/all_to_all | solution.py:486
  122.2 1.7 %copy-start.5 = (bf16[32,144,256]{2,1,0:T(8,128)(2,1)S(1)}, bf16[32,144,256]{2,1,0:T(8,128)(2,1)}, u32[]{:S(2)}) copy-start(bf16[32,144,256]{2,1,0:T(8,128)(2,1)} %all-gather.2.cloned.1.call-done.got_ref) | copy-start | bytes 7077892
  146.5 6.4 %collective-permute-start.11 = (bf16[256,1152]{1,0:T(8,128)(2,1)S(1)}, bf16[256,1152]{1,0:T(8,128)(2,1)S(1)}, u32[]{:S(2)}, u32[]{:S(2)}) collective-permute-start(bf16[256,1152]{1,0:T(8,128)(2,1)S(1)} %bitcast.15), channel_id=1, source_target_pairs={{0,128},{128,0},{1,129},{129,1},{2,130},{130,2},{3,131},{131,3},{4... | collective-permute-start | bytes 1769480 | tf_op jit(solution)/shard_map/ppermute | solution.py:431
Sparse Core Ops, SparseCore 0:
  55.0 30.4 all-gather.1
Sparse Core Ops, SparseCore 1:
  105.9 45.4 reduce-scatter.1
